TPU v7x, 256 devices: a whole 4x4x8 slice. The times are simulated.
256 devices in a mesh: band: 64 (over z, x, core), rep: 4 (over y).
Axes of the slice: x: 4, y: 4, z: 8, core: 2. Of those that a mesh axis runs over, the one named last changes fastest.
Arguments:
- points: bfloat16 [262144, 256], P('band'), may hold values from -6 to 6
- rank_source: int32 [262144], replicated, may hold values from 0 to 262143, as said below
- thresholds: int32 [262144], replicated, may hold values from 1000 to 1399
- kept_tiles: int32 [32, 10], replicated, may hold values from -1 to 15, as said below
Outputs:
- degrees: float32 [262144], P('band')
Inputs may be any that keep to these rules, and one draw needn't show every extreme that they name: `rank_source`: A permutation of the input indices; each block of 4096 consecutive input indices holds exactly 64 points of each band (band = rank // 4096). `kept_tiles`: row q lists distinct codes a * 4 + c with 0 <= a <= c < 4, then -1 entries; every row lists at least 5 codes, some row lists all 10.
All inputs are finite; a program needn't handle non-finite values.
Results may differ from a plain program's by a relative error of at most 0.0003.
Values may be sent and summed in bfloat16 or wider, within the bound.
No kernel may reach another device: no remote copies, remote signals or barrier semaphores. Data moves between devices by JAX's collectives and lax.ppermute only.
A program may use at most 64 MiB of HBM per device.

v0:
```python
import jax
import jax.numpy as jnp
from jax import lax
from jax.sharding import PartitionSpec as P

TILE = 2048


def inverse_norm(block):
    values = block.astype(jnp.float32)
    return lax.rsqrt(jnp.sum(values * values, axis=1) + 1e-06)


def cosine_tile(left_rows, right_rows, left_inv, right_inv, left_rad, right_rad, same_tile):
    products = lax.dot_general(
        left_rows, right_rows, (((1,), (1,)), ((), ())), preferred_element_type=jnp.float32
    )
    distance = 1.0 - products * left_inv[:, None] * right_inv[None, :]
    radius = jnp.minimum(left_rad[:, None], right_rad[None, :])
    weight = jnp.maximum(0.0, 1.0 - distance / radius)
    row_ids = lax.broadcasted_iota(jnp.int32, weight.shape, 0)
    col_ids = lax.broadcasted_iota(jnp.int32, weight.shape, 1)
    return jnp.where(same_tile & (row_ids == col_ids), 0.0, weight)


def on_device(points, rank_source, thresholds, kept_tiles):
    band_total = lax.axis_size("band")
    rep_total = lax.axis_size("rep")
    band_id = lax.axis_index("band")
    rep_id = lax.axis_index("rep")
    local_count, feature_width = points.shape
    per_group = local_count // band_total
    mirror_band = band_total - 1 - band_id
    source_shard = rank_source // local_count
    mine_ranked = jnp.nonzero(source_shard == band_id, size=local_count, fill_value=0)[0]
    local_order = rank_source[mine_ranked] - band_id * local_count
    sorted_rows = points[local_order]
    grouped = sorted_rows.reshape(band_total, per_group, feature_width)
    payload = jnp.concatenate([grouped, grouped[::-1]], axis=1)
    received = lax.all_to_all(payload, "band", split_axis=0, concat_axis=0, tiled=True)

    def arrange(rows_in, band_index):
        sources = (
            lax.dynamic_slice_in_dim(rank_source, band_index * local_count, local_count, 0)
            // local_count
        )
        placed = jnp.argsort(sources, stable=True)
        restore = jnp.argsort(placed)
        return rows_in[restore]

    own_rows = arrange(received[:, :per_group].reshape(local_count, feature_width), band_id)
    mirror_rows = arrange(received[:, per_group:].reshape(local_count, feature_width), mirror_band)
    upper_side = band_id >= band_total // 2
    low_rows = jnp.where(upper_side, mirror_rows, own_rows)
    high_rows = jnp.where(upper_side, own_rows, mirror_rows)
    combined = jnp.concatenate([low_rows, high_rows], axis=0)
    inverses = inverse_norm(combined)
    pair_index = jnp.minimum(band_id, mirror_band)
    low_rad = lax.dynamic_slice_in_dim(thresholds, pair_index * local_count, local_count, 0)
    high_rad = lax.dynamic_slice_in_dim(
        thresholds, (band_total - 1 - pair_index) * local_count, local_count, 0
    )
    radius_all = jnp.concatenate([low_rad, high_rad]).astype(jnp.float32) / 1024.0
    tile_span = 2 * (local_count // TILE)
    total_slots = kept_tiles.shape[1]
    turn_count = -(-total_slots // rep_total)
    pair_codes = lax.dynamic_index_in_dim(kept_tiles, pair_index, 0, keepdims=False)

    def tile_work(tile_code, degree):
        left_tile = tile_code // tile_span
        right_tile = tile_code % tile_span
        left_start = left_tile * TILE
        right_start = right_tile * TILE
        weight = cosine_tile(
            lax.dynamic_slice_in_dim(combined, left_start, TILE, 0),
            lax.dynamic_slice_in_dim(combined, right_start, TILE, 0),
            lax.dynamic_slice_in_dim(inverses, left_start, TILE, 0),
            lax.dynamic_slice_in_dim(inverses, right_start, TILE, 0),
            lax.dynamic_slice_in_dim(radius_all, left_start, TILE, 0),
            lax.dynamic_slice_in_dim(radius_all, right_start, TILE, 0),
            left_tile == right_tile,
        )
        row_sums = jnp.sum(weight, axis=1)
        col_sums = jnp.sum(weight, axis=0) * (left_tile != right_tile).astype(jnp.float32)
        current = lax.dynamic_slice_in_dim(degree, left_start, TILE, 0)
        degree = lax.dynamic_update_slice_in_dim(degree, current + row_sums, left_start, 0)
        current = lax.dynamic_slice_in_dim(degree, right_start, TILE, 0)
        return lax.dynamic_update_slice_in_dim(degree, current + col_sums, right_start, 0)

    def visit(turn_index, degree):
        slot_index = rep_id + turn_index * rep_total
        tile_code = jnp.where(
            slot_index < total_slots, pair_codes[jnp.minimum(slot_index, total_slots - 1)], -1
        )

        def work_branch(carried):
            return tile_work(tile_code, carried)

        def skip_branch(carried):
            return carried

        return lax.cond(tile_code >= 0, work_branch, skip_branch, degree)

    degree = lax.fori_loop(0, turn_count, visit, jnp.zeros((2 * local_count,), jnp.float32))
    summed = lax.psum(degree, "rep")
    own_degree = jnp.where(upper_side, summed[local_count:], summed[:local_count])
    return own_degree / TILE


def solution(mesh):
    in_specs = (P("band", None), P(), P(), P())
    out_specs = P("band")
    return jax.shard_map(
        on_device, mesh=mesh, in_specs=in_specs, out_specs=out_specs, check_vma=False
    )
```

profile of v0, /device:TPU:1, one launch (start us, length us, event | category | flops | bytes accessed | tf_op | source)
XLA Modules:
  0.0 2066.9 jit_solution(11376488744270997335)
XLA Ops:
  0.0 2.8 convert_reduce_fusion
  2.8 1.3 copy.5
  4.2 3.1 reduce-window.21
  7.3 0.9 slice.50
  8.9 2.4 broadcast_add_fusion
  11.3 2.5 copy.6
  13.8 2.9 compare_select_fusion
  16.8 1.1 ne.81
  17.8 1806.6 %scatter_custom_fusion = s32[4096]{0:T(1024)S(1)} fusion(s32[262144]{0:T(1024)} %bitcast.23, s32[262144]{0:T(1024)} %ne.81, s32[]{:T(128)} %constant.161.clone.1), kind=kCustom, calls=%fused_computation.68 | custom fusion | flops 262144 | bytes 16896 | tf_op jit(solution)/shard_map/scatter-add | solution.py:35
  1825.8 23.0 %gather_fusion = s32[4096]{0:T(1024)S(1)} fusion(s32[262144]{0:T(1024)S(1)} %copy-done.1, s32[4096]{0:T(1024)S(1)} %broadcast_clamp_fusion.1), kind=kCustom, calls=%fused_computation | custom fusion | bytes 49152 | tf_op jit(solution)/shard_map/gather | solution.py:36
  1848.9 16.9 gather_fusion.1
  1865.9 3.1 rev.3
  1869.0 4.7 pad_maximum_fusion
  1873.7 13.2 all-to-all-start
  1887.0 5.8 sort.64
  1892.8 5.8 sort.65
  1898.6 5.8 sort.62
  1904.3 5.8 sort.63
  1910.3 0.7 fusion.23
  1911.1 70.3 %all-to-all-done = bf16[64,128,256]{2,1,0:T(8,128)(2,1)} async-done(((bf16[64,128,256]{2,1,0:T(8,128)(2,1)}), bf16[64,128,256]{2,1,0:T(8,128)(2,1)}, u32[]{:S(2)}, u32[]{:S(2)}) %all-to-all-start) | async-done | bytes 4194336 | tf_op jit(solution)/shard_map/all_to_all | solution.py:40
  1981.3 4.8 fusion.22
  1986.1 17.7 gather_fusion.3
  2003.8 17.7 gather_fusion.2
  2021.5 2.5 broadcast_select_fusion.1
  2024.0 2.3 multiply_reduce_fusion
  2026.4 2.2 pad_maximum_fusion.1
  2028.6 26.7 %while.16 = (s32[]{:T(128)}, f32[8192]{0:T(1024)S(1)}, s32[]{:T(128)}, s32[10]{0:T(128)S(1)}, bf16[8192,256]{1,0:T(8,128)(2,1)}, /*index=5*/f32[8192]{0:T(1024)S...) while((s32[]{:T(128)}, f32[8192]{0:T(1024)S(1)}, ...), condition=%wide.region_17.18_spmd, body=%wide.region_12.17_spmd.sunk | while | flops 2197817344 | bytes 2261614 | solution.py:104
  2030.1 11.3 conditional.2
  2030.1 11.2 fusion.18
  2042.7 11.4 conditional.2
  2042.7 11.2 fusion.18
  2055.3 10.9 psum.7
  (44 shorter events, 4.8 us)
Async XLA Ops:
  0.0 1848.9 %copy-start = (bf16[4096,256]{1,0:T(8,128)(2,1)S(1)}, bf16[4096,256]{1,0:T(8,128)(2,1)}, u32[]{:S(2)}) copy-start(bf16[4096,256]{1,0:T(8,128)(2,1)} %param.8) | copy-start | bytes 6291460
  7.3 1818.5 %copy-start.1 = (s32[262144]{0:T(1024)S(1)}, s32[262144]{0:T(1024)}, u32[]{:S(2)}) copy-start(s32[262144]{0:T(1024)} %param.9) | copy-start | bytes 3145732
  1873.7 36.4 %copy-start.2 = (s32[32,10]{0,1:T(8,128)S(1)}, s32[32,10]{0,1:T(8,128)}, u32[]{:S(2)}) copy-start(s32[32,10]{0,1:T(8,128)} %param.11) | copy-start | bytes 3844
  1873.7 107.6 %all-to-all-start = ((bf16[64,128,256]{2,1,0:T(8,128)(2,1)}), bf16[64,128,256]{2,1,0:T(8,128)(2,1)}, u32[]{:S(2)}, u32[]{:S(2)}) async-start(bf16[64,128,256]{2,1,0:T(8,128)(2,1)} %pad_maximum_fusion), calls=%async_computation | async-start | bytes 8388608 | tf_op jit(solution)/shard_map/all_to_all | solution.py:40
where the time goes:
time: 2080 us; the launch traced here: 2070 us
  other arithmetic  1860 us (89%)
  local copies, waits for them, and re-layouts  92.3 us (4%)
  waiting for transfers between devices  70.3 us (3%)
  matrix products  22.4 us (1%)
    scatter-add x1, other arithmetic, on_device(): jnp.nonzero(source_shard == band_id, size=local_count, fill_value=0)[0]  1810 us
    all_to_all x1, waiting for transfers between devices, on_device(): lax.all_to_all(payload, 'band', split_axis=0, concat_axis=0, tiled=True)  70.3 us
  transfers between devices with their start and end apart: 1, of which 1 were waited for; matrix products, arithmetic and copies ran while one was open for 1% of the time, Pallas kernels for 0%

commit v1 on v0

v1 whole, which is shorter than its diff:
```python
import jax
import jax.numpy as jnp
from jax import lax
from jax.experimental import pallas as pl
from jax.experimental.pallas import tpu as pltpu
from jax.sharding import PartitionSpec as P

TILE = 2048
LANES = 128
VMEM_LIMIT = 48 * 1024 * 1024
NT = (((1,), (1,)), ((), ()))


def prefix_matrix():
    row = lax.broadcasted_iota(jnp.int32, (LANES, 2 * LANES), 0)
    col = lax.broadcasted_iota(jnp.int32, (LANES, 2 * LANES), 1)
    return jnp.where((row <= col) | (col >= LANES), 1.0, 0.0).astype(jnp.bfloat16)


def block_band(device):
    return device if device % 2 == 0 else 64 - device


def send_kernel(s_ref, rank_ref, points_ref, out_ref, pos_ref, loc_ref, acc_ref, row_ref, hot_ref):
    shard = s_ref[0]
    first = s_ref[1]
    prefix = prefix_matrix()
    carry = jnp.zeros((64, LANES), jnp.float32)
    base = (first + 1).astype(jnp.float32)
    for j in range(32):
        source = rank_ref[pl.ds(j, 64, stride=32), :]
        mine = (source >> 12) == shard
        counts = jnp.dot(
            jnp.where(mine, 1.0, 0.0).astype(jnp.bfloat16), prefix, preferred_element_type=jnp.float32
        )
        pos_ref[j] = jnp.where(mine, carry + counts[:, :LANES] - base, -1.0)
        loc_ref[j] = source & 4095
        carry = carry + counts[:, LANES:]

    @pl.loop(0, 8)
    def _(g):
        accs = [jnp.zeros((8, LANES), jnp.int32) for _ in range(16)]
        rows = pl.ds(pl.multiple_of(g * 8, 8), 8)
        for j in range(32):
            pos = pos_ref[j, rows, :]
            loc = loc_ref[j, rows, :]
            for s in range(16):
                accs[s] = jnp.where(pos == float(s), loc, accs[s])
        for s in range(16):
            acc_ref[pl.ds(pl.multiple_of(g * 128 + s * 8, 8), 8), :] = accs[s]

    ones = jnp.ones((LANES, LANES), jnp.bfloat16)
    acc = acc_ref[...]
    high = (acc >> 6).astype(jnp.float32).astype(jnp.bfloat16)
    low = (acc & 63).astype(jnp.float32).astype(jnp.bfloat16)
    row_ref[...] = 64.0 * jnp.dot(high, ones, preferred_element_type=jnp.float32) + jnp.dot(
        low, ones, preferred_element_type=jnp.float32
    )
    lane = lax.broadcasted_iota(jnp.int32, (256, LANES), 1).astype(jnp.float32)
    for blk in range(4):
        parts = []
        for i in range(16):
            band = block_band(blk * 16 + i)
            parts.append(row_ref[pl.ds((band // 8) * 128 + band % 8, 16, stride=8), :])
        local = jnp.concatenate(parts, axis=0)
        for ch in range(32):
            hot_ref[:, ch * 128 : (ch + 1) * 128] = jnp.where(
                local == lane + float(ch * 128), 1.0, 0.0
            ).astype(jnp.bfloat16)
        out_ref[blk * 256 : (blk + 1) * 256, :] = jnp.dot(
            hot_ref[...], points_ref[...], preferred_element_type=jnp.float32
        ).astype(jnp.bfloat16)


def send_rows(scalars, rank2d, points):
    return pl.pallas_call(
        send_kernel,
        out_shape=jax.ShapeDtypeStruct((1024, 256), jnp.bfloat16),
        in_specs=[
            pl.BlockSpec(memory_space=pltpu.SMEM),
            pl.BlockSpec(memory_space=pltpu.VMEM),
            pl.BlockSpec(memory_space=pltpu.VMEM),
        ],
        out_specs=pl.BlockSpec(memory_space=pltpu.VMEM),
        scratch_shapes=[
            pltpu.VMEM((32, 64, LANES), jnp.float32),
            pltpu.VMEM((32, 64, LANES), jnp.int32),
            pltpu.VMEM((1024, LANES), jnp.int32),
            pltpu.VMEM((1024, LANES), jnp.float32),
            pltpu.VMEM((256, 4096), jnp.bfloat16),
        ],
        compiler_params=pltpu.CompilerParams(vmem_limit_bytes=VMEM_LIMIT),
        name="send_rows",
    )(scalars, rank2d, points)


def place_kernel(s_ref, rank_ref, thr_ref, row_ref, col_ref, place_ref, u_ref, v_ref):
    rep = s_ref[2]
    prefix = prefix_matrix()
    shard_iota = lax.broadcasted_iota(jnp.int32, (64, LANES), 0)
    u_iota = lax.broadcasted_iota(jnp.int32, (32, LANES), 0)
    v_iota = lax.broadcasted_iota(jnp.int32, (LANES, LANES), 0)
    for x in range(3):
        start = pl.multiple_of(s_ref[3 + x] * 32, 32)
        carry = jnp.zeros((64, LANES), jnp.float32)
        source = rank_ref[pl.ds(start, 32), :] >> 12
        thr = thr_ref[pl.ds(start, 32), :]
        for j in range(32):
            shard = source[j : j + 1, :]
            hot = shard == shard_iota
            counts = jnp.dot(
                jnp.where(hot, 1.0, 0.0).astype(jnp.bfloat16), prefix, preferred_element_type=jnp.float32
            )
            slot = jnp.sum(jnp.where(hot, carry + counts[:, :LANES], 0.0), axis=0, keepdims=True)
            slot = slot.astype(jnp.int32) - 1
            carry = carry + counts[:, LANES:]
            quarter = slot >> 4
            v = (shard & 7) * 16 + (slot & 15)
            if x == 2:
                place_ref[j : j + 1, :] = (((rep - quarter) & 3) * 8 + (shard >> 3)) * 128 + v
            else:
                u = ((quarter - rep) & 3) * 8 + (shard >> 3)
                u_hot = u == u_iota
                t = thr[j : j + 1, :]
                lanes = slice(j * LANES, (j + 1) * LANES)
                u_ref[0:32, lanes] = jnp.where(u_hot, (t >> 4).astype(jnp.float32), 0.0).astype(jnp.bfloat16)
                u_ref[32:64, lanes] = jnp.where(u_hot, (t & 15).astype(jnp.float32), 0.0).astype(jnp.bfloat16)
                u_ref[64:96, lanes] = jnp.where(u_hot, float(j >= 16), 0.0).astype(jnp.bfloat16)
                v_ref[:, lanes] = jnp.where(v == v_iota, 1.0, 0.0).astype(jnp.bfloat16)
        if x < 2:
            us = u_ref[...]
            vs = v_ref[...]
            rows = lax.dot_general(us, vs, NT, preferred_element_type=jnp.float32)
            cols = lax.dot_general(vs, us, NT, preferred_element_type=jnp.float32)
            row_ref[x, 0:32, :] = 1024.0 / (rows[0:32] * 16.0 + rows[32:64])
            row_ref[x, 32:64, :] = rows[64:96]
            col_ref[x, :, 0:32] = 1024.0 / (cols[:, 0:32] * 16.0 + cols[:, 32:64])
            col_ref[x, :, 32:64] = cols[:, 64:96]


def place(scalars, rank2d, thr2d):
    return pl.pallas_call(
        place_kernel,
        out_shape=(
            jax.ShapeDtypeStruct((2, 64, LANES), jnp.float32),
            jax.ShapeDtypeStruct((2, LANES, 64), jnp.float32),
            jax.ShapeDtypeStruct((32, LANES), jnp.int32),
        ),
        in_specs=[
            pl.BlockSpec(memory_space=pltpu.SMEM),
            pl.BlockSpec(memory_space=pltpu.VMEM),
            pl.BlockSpec(memory_space=pltpu.VMEM),
        ],
        out_specs=(pl.BlockSpec(memory_space=pltpu.VMEM),) * 3,
        scratch_shapes=[
            pltpu.VMEM((96, 4096), jnp.bfloat16),
            pltpu.VMEM((LANES, 4096), jnp.bfloat16),
        ],
        compiler_params=pltpu.CompilerParams(vmem_limit_bytes=VMEM_LIMIT),
        cost_estimate=pl.CostEstimate(flops=2 * 10**9, bytes_accessed=10**7, transcendentals=0),
        name="place",
    )(scalars, rank2d, thr2d)


def square_parts(block):
    values = block.astype(jnp.float32)
    square = values * values
    high = square.astype(jnp.bfloat16)
    low = (square - high.astype(jnp.float32)).astype(jnp.bfloat16)
    return high, low


def inverse_column(high, low):
    ones = jnp.ones((256, LANES), jnp.bfloat16)
    total = jnp.dot(high, ones, preferred_element_type=jnp.float32)
    total = total + jnp.dot(low, ones, preferred_element_type=jnp.float32)
    return lax.rsqrt(total + 1e-06)


def inverse_row(high, low):
    ones = jnp.ones((8, 256), jnp.bfloat16)
    total = lax.dot_general(ones, high, NT, preferred_element_type=jnp.float32)
    total = total + lax.dot_general(ones, low, NT, preferred_element_type=jnp.float32)
    return lax.rsqrt(total + 1e-06)


def load_column_meta(slot, col_ref, band, quarter, dest_ref):
    for u in range(8):
        rows = slice(u * LANES, (u + 1) * LANES)
        at = quarter * 8 + u
        dest_ref[slot, 1, rows, :] = jnp.broadcast_to(col_ref[band, :, at : at + 1], (LANES, LANES))
        dest_ref[slot, 2, rows, :] = jnp.broadcast_to(col_ref[band, :, 32 + at : 33 + at], (LANES, LANES))


def load_row_meta(slot, row_ref, band, quarter, dest_ref):
    for u in range(8):
        lanes = slice(u * LANES, (u + 1) * LANES)
        at = quarter * 8 + u
        dest_ref[slot, 1, :, lanes] = jnp.broadcast_to(row_ref[band, at : at + 1, :], (8, LANES))
        dest_ref[slot, 2, :, lanes] = jnp.broadcast_to(row_ref[band, 32 + at : 33 + at, :], (8, LANES))


def keep_rows(keep_ref, row_offset, col_offset, row_meta_ref, slot, dest_ref):
    upper = row_meta_ref[slot, 2] > 0.5
    for t in range(2):
        at = (row_offset + t) * 4 + col_offset
        dest_ref[t] = jnp.where(upper, keep_ref[at + 1], keep_ref[at])


def weigh(left_ref, left_at, left_meta, left_slot, right_ref, right_at, right_meta, right_slot,
          keep, prod_ref, row_sum_ref, col_sum_ref, left_sum, right_sum, diagonal):
    prod_ref[...] = lax.dot_general(
        left_ref[pl.ds(left_at, 256), :], right_ref[pl.ds(right_at, 512), :], NT,
        preferred_element_type=jnp.float32,
    )

    def strip(i, sums):
        at = pl.multiple_of(i * 32, 32)
        rows = pl.ds(pl.multiple_of(left_at + at, 32), 32)
        inv_i = left_meta[left_slot, 0, rows, :]
        rho_i = left_meta[left_slot, 1, rows, :]
        upper = left_meta[left_slot, 2, rows, :] > 0.5
        total = row_sum_ref[left_sum, rows, :]
        out = []
        for ch in range(4):
            cols = pl.ds(pl.multiple_of(right_at + ch * LANES, LANES), LANES)
            inv_j = right_meta[right_slot, 0, 0:1, cols]
            rho_j = right_meta[right_slot, 1, 0:1, cols]
            kept = jnp.where(upper, keep[1, 0:1, cols], keep[0, 0:1, cols])
            p = prod_ref[pl.ds(at, 32), ch * LANES : (ch + 1) * LANES]
            near = (p * inv_i) * inv_j - 1.0
            w = jnp.maximum(near * jnp.maximum(rho_i, rho_j) + kept, 0.0)
            if diagonal:
                row_ids = left_at + at + lax.broadcasted_iota(jnp.int32, w.shape, 0)
                col_ids = right_at + ch * LANES + lax.broadcasted_iota(jnp.int32, w.shape, 1)
                w = jnp.where(row_ids == col_ids, 0.0, w)
            total = total + w
            if not diagonal:
                out.append(sums[ch] + ((w[0:8] + w[8:16]) + (w[16:24] + w[24:32])))
        row_sum_ref[left_sum, rows, :] = total
        return tuple(out)

    zeros = () if diagonal else tuple(jnp.zeros((8, LANES), jnp.float32) for _ in range(4))
    sums = lax.fori_loop(0, 8, strip, zeros)
    if not diagonal:
        for ch in range(4):
            cols = pl.ds(pl.multiple_of(right_at + ch * LANES, LANES), LANES)
            col_sum_ref[right_sum, :, cols] += sums[ch]


def rows_to_lanes(row_sum_ref, slot):
    row = lax.broadcasted_iota(jnp.int32, (LANES, LANES), 0)
    lane = lax.broadcasted_iota(jnp.int32, (LANES, LANES), 1)
    out = []
    for u in range(8):
        total = jnp.sum(row_sum_ref[slot, u * LANES : (u + 1) * LANES, :], axis=1, keepdims=True)
        out.append(jnp.sum(jnp.where(row == lane, total, 0.0), axis=0, keepdims=True))
    return out


def cols_to_lanes(col_sum_ref, slot):
    return [
        jnp.sum(col_sum_ref[slot, :, u * LANES : (u + 1) * LANES], axis=0, keepdims=True)
        for u in range(8)
    ]


def near_kernel(s_ref, keep_ref, own_ref, other_ref, row_ref, col_ref, out_ref,
                left_meta, right_meta, keep, prod_ref, row_sum, col_sum):
    core = s_ref[6]
    own_offset = s_ref[7]
    other_offset = s_ref[8]
    high, low = square_parts(own_ref[...])
    left_meta[0, 0] = inverse_column(high, low)
    right_meta[0, 0] = inverse_row(high, low)
    high, low = square_parts(other_ref[...])
    right_meta[1, 0] = inverse_row(high, low)
    load_column_meta(0, col_ref, 0, 0, left_meta)
    load_row_meta(0, row_ref, 0, 0, right_meta)
    load_row_meta(1, row_ref, 1, 0, right_meta)
    row_sum[...] = jnp.zeros_like(row_sum)
    col_sum[...] = jnp.zeros_like(col_sum)

    keep_rows(keep_ref, own_offset, own_offset, right_meta, 0, keep)

    @pl.loop(0, 8)
    def _(i):
        weigh(own_ref, pl.multiple_of((i >> 1) * 256, 256), left_meta, 0, own_ref,
              pl.multiple_of((i & 1) * 512, 512), right_meta, 0,
              keep, prod_ref, row_sum, col_sum, 0, 0, True)

    keep_rows(keep_ref, own_offset, other_offset, right_meta, 1, keep)

    @pl.loop(0, 4)
    def _(i):
        weigh(own_ref, pl.multiple_of(i * 256, 256), left_meta, 0, other_ref,
              pl.multiple_of(((i >> 1) ^ core) * 512, 512), right_meta, 1,
              keep, prod_ref, row_sum, col_sum, 0, 0, False)

    for u, value in enumerate(rows_to_lanes(row_sum, 0)):
        out_ref[0, u : u + 1, :] = value
    for u, value in enumerate(cols_to_lanes(col_sum, 0)):
        out_ref[1, u : u + 1, :] = value


def far_kernel(s_ref, keep_ref, own_ref, other_ref, right_ref, left_ref, row_ref, col_ref, near_ref,
               out_ref, left_meta, right_meta, keep, prod_ref, row_sum, col_sum):
    own_offset = s_ref[7]
    other_offset = s_ref[8]
    cross = s_ref[9]
    left_offset = s_ref[10]
    high, low = square_parts(own_ref[...])
    left_meta[0, 0] = inverse_column(high, low)
    high, low = square_parts(other_ref[...])
    left_meta[1, 0] = inverse_column(high, low)
    high, low = square_parts(left_ref[...])
    left_meta[2, 0] = inverse_column(high, low)
    high, low = square_parts(right_ref[...])
    right_meta[0, 0] = inverse_row(high, low)
    load_column_meta(0, col_ref, 0, 0, left_meta)
    load_column_meta(1, col_ref, 1, 0, left_meta)
    load_column_meta(2, col_ref, cross, 3, left_meta)
    load_row_meta(0, row_ref, 0, 1, right_meta)
    row_sum[...] = jnp.zeros_like(row_sum)
    col_sum[...] = jnp.zeros_like(col_sum)
    for slot, (block_ref, offset) in enumerate(
        ((own_ref, own_offset), (other_ref, other_offset), (left_ref, left_offset))
    ):
        keep_rows(keep_ref, offset, own_offset, right_meta, 0, keep)

        @pl.loop(0, 8)
        def _(i):
            weigh(block_ref, pl.multiple_of((i >> 1) * 256, 256), left_meta, slot, right_ref,
                  pl.multiple_of((i & 1) * 512, 512), right_meta, 0,
                  keep, prod_ref, row_sum, col_sum, slot, 0, False)

    for slot in range(3):
        for u, value in enumerate(rows_to_lanes(row_sum, slot)):
            if slot < 2:
                value = value + near_ref[slot, u : u + 1, :]
            out_ref[slot, u : u + 1, :] = value
    for u, value in enumerate(cols_to_lanes(col_sum, 0)):
        out_ref[3, u : u + 1, :] = value


def pair_scratch(lefts, rights):
    return [
        pltpu.VMEM((lefts, 3, 1024, LANES), jnp.float32),
        pltpu.VMEM((rights, 3, 8, 1024), jnp.float32),
        pltpu.VMEM((2, 8, 1024), jnp.float32),
        pltpu.VMEM((256, 512), jnp.float32),
        pltpu.VMEM((lefts, 1024, LANES), jnp.float32),
        pltpu.VMEM((1, 8, 1024), jnp.float32),
    ]


def smem():
    return pl.BlockSpec(memory_space=pltpu.SMEM)


def vmem():
    return pl.BlockSpec(memory_space=pltpu.VMEM)


def near_pairs(scalars, keep, own, other, rows, cols):
    return pl.pallas_call(
        near_kernel,
        out_shape=jax.ShapeDtypeStruct((2, 8, LANES), jnp.float32),
        in_specs=[smem(), smem(), vmem(), vmem(), vmem(), vmem()],
        out_specs=vmem(),
        scratch_shapes=pair_scratch(1, 2),
        compiler_params=pltpu.CompilerParams(vmem_limit_bytes=VMEM_LIMIT),
        cost_estimate=pl.CostEstimate(flops=2 * 10**9, bytes_accessed=10**7, transcendentals=0),
        name="near_pairs",
    )(scalars, keep, own, other, rows, cols)


def far_pairs(scalars, keep, own, other, right, left, rows, cols, near):
    return pl.pallas_call(
        far_kernel,
        out_shape=jax.ShapeDtypeStruct((4, 8, LANES), jnp.float32),
        in_specs=[smem(), smem()] + [vmem()] * 7,
        out_specs=vmem(),
        scratch_shapes=pair_scratch(3, 1),
        compiler_params=pltpu.CompilerParams(vmem_limit_bytes=VMEM_LIMIT),
        cost_estimate=pl.CostEstimate(flops=4 * 10**9, bytes_accessed=10**7, transcendentals=0),
        name="far_pairs",
    )(scalars, keep, own, other, right, left, rows, cols, near)


def rank_kernel(place_ref, a_ref, b_ref, c_ref, d_ref, out_ref):
    place_at = place_ref[...]
    lane = place_at & 127
    which = place_at >> 7
    total = jnp.zeros((32, LANES), jnp.float32)
    for s, piece in enumerate((a_ref, b_ref, c_ref, d_ref)):
        for u in range(8):
            row = jnp.broadcast_to(piece[u : u + 1, :], (32, LANES))
            value = jnp.take_along_axis(row, lane, axis=1)
            total = jnp.where(which == s * 8 + u, value, total)
    out_ref[...] = total * (1.0 / TILE)


def to_rank_order(place_at, pieces):
    return pl.pallas_call(
        rank_kernel,
        out_shape=jax.ShapeDtypeStruct((32, LANES), jnp.float32),
        in_specs=[vmem()] * 5,
        out_specs=vmem(),
        name="to_rank_order",
    )(place_at, *pieces)


def on_device(points, rank_source, thresholds, kept_tiles):
    bands = lax.axis_size("band")
    reps = lax.axis_size("rep")
    device = lax.axis_index("band").astype(jnp.int32)
    rep = lax.axis_index("rep").astype(jnp.int32)
    core = device & 1
    own_band = jnp.where(core == 0, device, bands - device)
    other_band = bands - 1 - own_band
    own_offset = jnp.where(own_band < bands // 2, 0, 2)
    other_offset = 2 - own_offset
    cross = (rep >= 2).astype(jnp.int32)
    left_offset = jnp.where(cross == 1, other_offset, own_offset)
    scalars = jnp.stack([
        device, rep * 16, rep, own_band, other_band, device, core,
        own_offset, other_offset, cross, left_offset,
    ]).astype(jnp.int32)
    codes = lax.dynamic_index_in_dim(kept_tiles, jnp.minimum(own_band, other_band), 0, keepdims=False)
    ids = jnp.arange(16, dtype=jnp.int32)
    a, c = ids // 4, ids % 4
    wanted = jnp.minimum(a, c) * 4 + jnp.maximum(a, c)
    keep = jnp.where(jnp.any(codes[:, None] == wanted[None, :], axis=0), 1.0, -1e30).astype(jnp.float32)

    rank2d = rank_source.reshape(2048, LANES)
    thr2d = thresholds.reshape(2048, LANES)

    def joint(move):
        return [
            (d * reps + r, e * reps + q)
            for d in range(bands)
            for r in range(reps)
            for e, q in (move(d, r),)
        ]

    def shift(value, move):
        return lax.ppermute(value, ("band", "rep"), joint(move))

    payload = send_rows(scalars, rank2d, points)
    own = lax.all_to_all(
        payload.reshape(bands, 16, 256), "band", split_axis=0, concat_axis=0, tiled=True
    ).reshape(1024, 256)
    rows, cols, place_at = place(scalars, rank2d, thr2d)

    def to_right(d, r):
        q = (r + 1) % reps
        return (d if q < 2 else d ^ 1), q

    other = shift(own, lambda d, r: (d ^ 1, r))
    right = shift(own, lambda d, r: (d, (r - 1) % reps))
    left = shift(own, to_right)

    near = near_pairs(scalars, keep, own, other, rows, cols)
    sums = far_pairs(scalars, keep, own, other, right, left, rows, cols, near)

    def from_left(d, r):
        return (d if r < 2 else d ^ 1), (r - 1) % reps

    total = sums[0] + shift(sums[1], lambda d, r: (d ^ 1, r))
    total = total + shift(sums[2], from_left)
    total = total + shift(sums[3], lambda d, r: (d, (r + 1) % reps))

    pieces = [
        shift(total, lambda d, r, s=s: (block_band(d), (r + s) % reps)) for s in range(reps)
    ]
    return to_rank_order(place_at, pieces).reshape(points.shape[0])


def solution(mesh):
    in_specs = (P("band", None), P(), P(), P())
    out_specs = P("band")
    return jax.shard_map(
        on_device, mesh=mesh, in_specs=in_specs, out_specs=out_specs, check_vma=False
    )
```

time: 2080 us -> 103 us (0.05)
  the two profiles are of different devices: /device:TPU:1 before, /device:TPU:33 now
where the time goes in v1:
time: 103 us; the launch traced here: 102 us
  starting transfers between devices  36.5 us (35%)
  Pallas kernels  35.5 us (34%)
  waiting for transfers between devices  25.9 us (25%)
  local copies, waits for them, and re-layouts  4.29 us (4%)
    ppermute x10, starting transfers between devices, shift(): return lax.ppermute(value, ('band', 'rep'), joint(move))  24.6 us
    all_to_all x1, waiting for transfers between devices, on_device(): lax.all_to_all(payload.reshape(bands, 16, 256), 'band', split_axis=0, con...  16.8 us
    pallas_call x1, Pallas kernels, far_pairs(): pl.pallas_call(far_kernel, out_shape=jax.ShapeDtypeStruct((4, 8, LANES),...  14.8 us
    all_to_all x1, starting transfers between devices, on_device(): lax.all_to_all(payload.reshape(bands, 16, 256), 'band', split_axis=0, con...  11.9 us
    ppermute x10, waiting for transfers between devices, shift(): return lax.ppermute(value, ('band', 'rep'), joint(move))  9.05 us
    pallas_call x1, Pallas kernels, near_pairs(): pl.pallas_call(near_kernel, out_shape=jax.ShapeDtypeStruct((2, 8, LANES),...  8.06 us
    pallas_call x1, Pallas kernels, send_rows(): pl.pallas_call(send_kernel, out_shape=jax.ShapeDtypeStruct((1024, 256), j...  7.39 us
    unnamed x20, local copies, waits for them, and re-layouts  4.01 us
  transfers between devices with their start and end apart: 11, of which 6 were waited for; matrix products, arithmetic and copies ran while one was open for 0% of the time, Pallas kernels for 11%

profile of v1, /device:TPU:33, one launch (start us, length us, event | category | flops | bytes accessed | tf_op | source)
XLA Modules:
  0.0 102.5 jit_solution(8932401504660204842)
XLA Ops:
  0.0 0.1 stack.44.s_ref
  0.1 1.6 %copy-done.1 = bf16[4096,256]{1,0:T(8,128)(2,1)S(1)} copy-done((bf16[4096,256]{1,0:T(8,128)(2,1)S(1)}, bf16[4096,256]{1,0:T(8,128)(2,1)}, u32[]{:S(2)}) %copy-start.1) | copy-done | bytes 2097176
  1.7 1.2 %copy-done.2 = s32[262144]{0:T(1024)S(1)} copy-done((s32[262144]{0:T(1024)S(1)}, s32[262144]{0:T(1024)}, u32[]{:S(2)}) %copy-start.2) | copy-done | bytes 1048600
  2.9 7.4 %send_rows.1 = bf16[1024,256]{1,0:T(8,128)(2,1)} custom-call(s32[11]{0:T(128)S(1)} %stack.44.s_ref, s32[2048,128]{1,0:T(8,128)S(1)} %bitcast.29, bf16[4096,256]{1,0:T(8,128)(2,1)S(1)} %copy-done.1), custom_call_target="tpu_custom_call" | custom-call | tf_op jit(solution)/shard_map/send_rows/pallas_call | solution.py:76
  10.3 11.9 %all-to-all-start = ((bf16[64,16,256]{2,1,0:T(8,128)(2,1)}), bf16[64,16,256]{2,1,0:T(8,128)(2,1)S(1)}, u32[]{:S(2)}, u32[]{:S(2)}) async-start(bf16[64,16,256]{2,1,0:T(8,128)(2,1)} %bitcast.12), calls=%async_computation | async-start | bytes 1048576 | tf_op jit(solution)/shard_map/all_to_all | solution.py:451
  22.2 0.2 dynamic-slice_reduce_fusion
  22.4 16.8 %all-to-all-done = bf16[64,16,256]{2,1,0:T(8,128)(2,1)S(1)} async-done(((bf16[64,16,256]{2,1,0:T(8,128)(2,1)}), bf16[64,16,256]{2,1,0:T(8,128)(2,1)S(1)}, u32[]{:S(2)}, u32[]{:S(2)}) %all-to-all-start) | async-done | bytes 524320 | tf_op jit(solution)/shard_map/all_to_all | solution.py:451
  39.3 0.1 collective-permute-start
  39.3 3.5 %place.1 = (f32[2,64,128]{2,1,0:T(8,128)S(1)}, f32[2,128,64]{2,1,0:T(8,128)S(1)}, s32[32,128]{1,0:T(8,128)S(1)}) custom-call(s32[11]{0:T(128)S(1)} %stack.44.s_ref, s32[2048,128]{1,0:T(8,128)S(1)} %bitcast.30, s32[2048,128]{1,0:T(8,128)S(1)} %bitcast.36), custom_call_target="tpu_custom_call" | custom-call | flops 2000000000 | bytes 10000000 | tf_op jit(solution)/shard_map/place/pallas_call | solution.py:142
  42.9 0.6 copy-done.4
  43.5 1.3 %collective-permute-start.2 = (bf16[1024,256]{1,0:T(8,128)(2,1)S(1)}, bf16[1024,256]{1,0:T(8,128)(2,1)S(1)}, u32[]{:S(2)}, u32[]{:S(2)}) collective-permute-start(bf16[1024,256]{1,0:T(8,128)(2,1)S(1)} %bitcast.32), channel_id=1, source_target_pairs={{0,1},{1,6},{2,7},{3,0},{4,5},{5,2},{6,3},{7,4},{8,9},{9,14},{10,1... | collective-permute-start | bytes 1572872 | tf_op jit(solution)/shard_map/ppermute | solution.py:448
  44.8 1.4 %collective-permute-start.1 = (bf16[1024,256]{1,0:T(8,128)(2,1)S(1)}, bf16[1024,256]{1,0:T(8,128)(2,1)S(1)}, u32[]{:S(2)}, u32[]{:S(2)}) collective-permute-start(bf16[1024,256]{1,0:T(8,128)(2,1)S(1)} %bitcast.33), channel_id=1, source_target_pairs={{0,3},{1,0},{2,1},{3,2},{4,7},{5,4},{6,5},{7,6},{8,11},{9,8},{10,9... | collective-permute-start | bytes 1572872 | tf_op jit(solution)/shard_map/ppermute | solution.py:448
  46.2 0.1 compare_reduce_fusion
  46.3 0.0 collective-permute-done.other_ref
  46.3 8.1 %near_pairs.1.near_ref = f32[2,8,128]{2,1,0:T(8,128)S(1)} custom-call(s32[11]{0:T(128)S(1)} %stack.44.s_ref, f32[16]{0:T(128)S(1)} %broadcast_select_fusion.keep_ref, bf16[1024,256]{1,0:T(8,128)(2,1)S(1)} %bitcast.34, bf16[1024,256]{1,0:T(8,128)(2,1)S(1)} %collective-permute-done.other_ref, f32[2,64,128]{2,1,0:T(8,128)S(1)} %get-tuple-element.9.row_ref, ...), custom_call_target="tpu_custom_call" | custom-call | flops 2000000000 | bytes 10000000 | tf_op jit(solution)/shard_map/near_pairs/pallas_call | solution.py:366
  54.4 3.5 %collective-permute-done.2.left_ref = bf16[1024,256]{1,0:T(8,128)(2,1)S(1)} collective-permute-done((bf16[1024,256]{1,0:T(8,128)(2,1)S(1)}, bf16[1024,256]{1,0:T(8,128)(2,1)S(1)}, u32[]{:S(2)}, u32[]{:S(2)}) %collective-permute-start.2) | collective-permute-done | bytes 524320 | tf_op jit(solution)/shard_map/ppermute | solution.py:448
  57.9 0.0 collective-permute-done.1.right_ref
  57.9 14.8 %far_pairs.1 = f32[4,8,128]{2,1,0:T(8,128)S(1)} custom-call(s32[11]{0:T(128)S(1)} %stack.44.s_ref, f32[16]{0:T(128)S(1)} %broadcast_select_fusion.keep_ref, bf16[1024,256]{1,0:T(8,128)(2,1)S(1)} %bitcast.35, bf16[1024,256]{1,0:T(8,128)(2,1)S(1)} %collective-permute-done.other_ref, bf16[1024,256]{1,0:T(8,128)(2,1)S(1)} %collective-permute-done.1.right_ref, ...), custom_call_target="tpu_custom_call" | custom-call | flops 4000000000 | bytes 10000000 | tf_op jit(solution)/shard_map/far_pairs/pallas_call | solution.py:379
  72.7 1.5 %collective-permute-start.3 = (f32[8,128]{1,0:T(8,128)S(1)}, f32[8,128]{1,0:T(8,128)S(1)}, u32[]{:S(2)}, u32[]{:S(2)}) collective-permute-start(f32[8,128]{1,0:T(8,128)S(1)} %get-tuple-element.11), channel_id=1, source_target_pairs={{0,4},{1,5},{2,6},{3,7},{4,0},{5,1},{6,2},{7,3},{8,12},{9,13},{10,... | collective-permute-start | bytes 12296 | tf_op jit(solution)/shard_map/ppermute | solution.py:448
  74.2 1.5 %collective-permute-start.5 = (f32[8,128]{1,0:T(8,128)S(1)}, f32[8,128]{1,0:T(8,128)S(1)}, u32[]{:S(2)}, u32[]{:S(2)}) collective-permute-start(f32[8,128]{1,0:T(8,128)S(1)} %get-tuple-element.12), channel_id=1, source_target_pairs={{0,1},{1,2},{2,3},{3,0},{4,5},{5,6},{6,7},{7,4},{8,9},{9,10},{10,1... | collective-permute-start | bytes 12296 | tf_op jit(solution)/shard_map/ppermute | solution.py:448
  75.7 1.2 %collective-permute-start.4 = (f32[8,128]{1,0:T(8,128)S(1)}, f32[8,128]{1,0:T(8,128)S(1)}, u32[]{:S(2)}, u32[]{:S(2)}) collective-permute-start(f32[8,128]{1,0:T(8,128)S(1)} %get-tuple-element.13), channel_id=1, source_target_pairs={{0,3},{1,0},{2,5},{3,6},{4,7},{5,4},{6,1},{7,2},{8,11},{9,8},{10,1... | collective-permute-start | bytes 12296 | tf_op jit(solution)/shard_map/ppermute | solution.py:448
  76.9 1.0 collective-permute-done.5
  77.9 0.5 collective-permute-done.4
  78.4 4.8 %collective-permute-start.9 = (f32[8,128]{1,0:T(8,128)S(1)}, f32[8,128]{1,0:T(8,128)S(1)}, u32[]{:S(2)}, u32[]{:S(2)}) collective-permute-start(f32[8,128]{1,0:T(8,128)S(1)} %fusion.2), channel_id=1, source_target_pairs={{0,3},{1,0},{2,1},{3,2},{4,255},{5,252},{6,253},{7,254},{8,11},{9,... | collective-permute-start | bytes 12296 | tf_op jit(solution)/shard_map/ppermute | solution.py:448
  83.3 4.3 %collective-permute-start.8 = (f32[8,128]{1,0:T(8,128)S(1)}, f32[8,128]{1,0:T(8,128)S(1)}, u32[]{:S(2)}, u32[]{:S(2)}) collective-permute-start(f32[8,128]{1,0:T(8,128)S(1)} %fusion.2), channel_id=1, source_target_pairs={{0,2},{1,3},{2,0},{3,1},{4,254},{5,255},{6,252},{7,253},{8,10},{9,... | collective-permute-start | bytes 12296 | tf_op jit(solution)/shard_map/ppermute | solution.py:448
  87.5 3.1 %collective-permute-start.7 = (f32[8,128]{1,0:T(8,128)S(1)}, f32[8,128]{1,0:T(8,128)S(1)}, u32[]{:S(2)}, u32[]{:S(2)}) collective-permute-start(f32[8,128]{1,0:T(8,128)S(1)} %fusion.2), channel_id=1, source_target_pairs={{0,1},{1,2},{2,3},{3,0},{4,253},{5,254},{6,255},{7,252},{8,9},{9,1... | collective-permute-start | bytes 12296 | tf_op jit(solution)/shard_map/ppermute | solution.py:448
  90.6 5.4 %collective-permute-start.6 = (f32[8,128]{1,0:T(8,128)S(1)}, f32[8,128]{1,0:T(8,128)S(1)}, u32[]{:S(2)}, u32[]{:S(2)}) collective-permute-start(f32[8,128]{1,0:T(8,128)S(1)} %fusion.2), channel_id=1, source_target_pairs={{0,0},{1,1},{2,2},{3,3},{4,252},{5,253},{6,254},{7,255},{8,8},{9,9... | collective-permute-start | bytes 12296 | tf_op jit(solution)/shard_map/ppermute | solution.py:448
  96.0 0.0 collective-permute-done.8.c_ref
  96.1 1.2 %collective-permute-done.7.b_ref = f32[8,128]{1,0:T(8,128)S(1)} collective-permute-done((f32[8,128]{1,0:T(8,128)S(1)}, f32[8,128]{1,0:T(8,128)S(1)}, u32[]{:S(2)}, u32[]{:S(2)}) %collective-permute-start.7) | collective-permute-done | bytes 4128 | tf_op jit(solution)/shard_map/ppermute | solution.py:448
  97.2 2.9 %collective-permute-done.6.a_ref = f32[8,128]{1,0:T(8,128)S(1)} collective-permute-done((f32[8,128]{1,0:T(8,128)S(1)}, f32[8,128]{1,0:T(8,128)S(1)}, u32[]{:S(2)}, u32[]{:S(2)}) %collective-permute-start.6) | collective-permute-done | bytes 4128 | tf_op jit(solution)/shard_map/ppermute | solution.py:448
  100.1 0.6 copy-done.9
  100.7 1.8 %to_rank_order.1 = f32[32,128]{1,0:T(8,128)} custom-call(s32[32,128]{1,0:T(8,128)} %copy-done.4, f32[8,128]{1,0:T(8,128)} %copy-done.9, f32[8,128]{1,0:T(8,128)} %copy-done.8, f32[8,128]{1,0:T(8,128)} %copy-done.7, f32[8,128]{1,0:T(8,128)} %copy-done.6), custom_call_target="tpu_custom_call" | custom-call | tf_op jit(solution)/shard_map/to_rank_order/pallas_call | solution.py:405
  (22 shorter events, 0.1 us)
Async XLA Ops:
  0.0 22.2 %copy-start = (s32[32,10]{0,1:T(8,128)S(1)}, s32[32,10]{0,1:T(8,128)}, u32[]{:S(2)}) copy-start(s32[32,10]{0,1:T(8,128)} %param.7) | copy-start | bytes 3844
  0.1 1.6 %copy-start.1 = (bf16[4096,256]{1,0:T(8,128)(2,1)S(1)}, bf16[4096,256]{1,0:T(8,128)(2,1)}, u32[]{:S(2)}) copy-start(bf16[4096,256]{1,0:T(8,128)(2,1)} %points_ref.1) | copy-start | bytes 6291460
  1.7 1.2 %copy-start.2 = (s32[262144]{0:T(1024)S(1)}, s32[262144]{0:T(1024)}, u32[]{:S(2)}) copy-start(s32[262144]{0:T(1024)} %param.5) | copy-start | bytes 3145732
  2.9 36.4 %copy-start.3 = (s32[262144]{0:T(1024)S(1)}, s32[262144]{0:T(1024)}, u32[]{:S(2)}) copy-start(s32[262144]{0:T(1024)} %param.5) | copy-start | bytes 3145732
  2.9 36.4 %copy-start.5 = (s32[262144]{0:T(1024)S(1)}, s32[262144]{0:T(1024)}, u32[]{:S(2)}) copy-start(s32[262144]{0:T(1024)} %param.6) | copy-start | bytes 3145732
  10.3 29.0 %all-to-all-start = ((bf16[64,16,256]{2,1,0:T(8,128)(2,1)}), bf16[64,16,256]{2,1,0:T(8,128)(2,1)S(1)}, u32[]{:S(2)}, u32[]{:S(2)}) async-start(bf16[64,16,256]{2,1,0:T(8,128)(2,1)} %bitcast.12), calls=%async_computation | async-start | bytes 1048576 | tf_op jit(solution)/shard_map/all_to_all | solution.py:451
  39.3 7.1 %collective-permute-start = (bf16[1024,256]{1,0:T(8,128)(2,1)S(1)}, bf16[1024,256]{1,0:T(8,128)(2,1)S(1)}, u32[]{:S(2)}, u32[]{:S(2)}) collective-permute-start(bf16[1024,256]{1,0:T(8,128)(2,1)S(1)} %bitcast.31), channel_id=1, source_target_pairs={{0,4},{1,5},{2,6},{3,7},{4,0},{5,1},{6,2},{7,3},{8,12},{9,13},{10,... | collective-permute-start | bytes 1572872 | tf_op jit(solution)/shard_map/ppermute | solution.py:448
  42.9 0.6 copy-start.4
  43.5 14.4 %collective-permute-start.2 = (bf16[1024,256]{1,0:T(8,128)(2,1)S(1)}, bf16[1024,256]{1,0:T(8,128)(2,1)S(1)}, u32[]{:S(2)}, u32[]{:S(2)}) collective-permute-start(bf16[1024,256]{1,0:T(8,128)(2,1)S(1)} %bitcast.32), channel_id=1, source_target_pairs={{0,1},{1,6},{2,7},{3,0},{4,5},{5,2},{6,3},{7,4},{8,9},{9,14},{10,1... | collective-permute-start | bytes 1572872 | tf_op jit(solution)/shard_map/ppermute | solution.py:448
  44.8 13.1 %collective-permute-start.1 = (bf16[1024,256]{1,0:T(8,128)(2,1)S(1)}, bf16[1024,256]{1,0:T(8,128)(2,1)S(1)}, u32[]{:S(2)}, u32[]{:S(2)}) collective-permute-start(bf16[1024,256]{1,0:T(8,128)(2,1)S(1)} %bitcast.33), channel_id=1, source_target_pairs={{0,3},{1,0},{2,1},{3,2},{4,7},{5,4},{6,5},{7,6},{8,11},{9,8},{10,9... | collective-permute-start | bytes 1572872 | tf_op jit(solution)/shard_map/ppermute | solution.py:448
  72.7 4.2 %collective-permute-start.3 = (f32[8,128]{1,0:T(8,128)S(1)}, f32[8,128]{1,0:T(8,128)S(1)}, u32[]{:S(2)}, u32[]{:S(2)}) collective-permute-start(f32[8,128]{1,0:T(8,128)S(1)} %get-tuple-element.11), channel_id=1, source_target_pairs={{0,4},{1,5},{2,6},{3,7},{4,0},{5,1},{6,2},{7,3},{8,12},{9,13},{10,... | collective-permute-start | bytes 12296 | tf_op jit(solution)/shard_map/ppermute | solution.py:448
  74.2 3.7 %collective-permute-start.5 = (f32[8,128]{1,0:T(8,128)S(1)}, f32[8,128]{1,0:T(8,128)S(1)}, u32[]{:S(2)}, u32[]{:S(2)}) collective-permute-start(f32[8,128]{1,0:T(8,128)S(1)} %get-tuple-element.12), channel_id=1, source_target_pairs={{0,1},{1,2},{2,3},{3,0},{4,5},{5,6},{6,7},{7,4},{8,9},{9,10},{10,1... | collective-permute-start | bytes 12296 | tf_op jit(solution)/shard_map/ppermute | solution.py:448
  75.7 2.8 %collective-permute-start.4 = (f32[8,128]{1,0:T(8,128)S(1)}, f32[8,128]{1,0:T(8,128)S(1)}, u32[]{:S(2)}, u32[]{:S(2)}) collective-permute-start(f32[8,128]{1,0:T(8,128)S(1)} %get-tuple-element.13), channel_id=1, source_target_pairs={{0,3},{1,0},{2,5},{3,6},{4,7},{5,4},{6,1},{7,2},{8,11},{9,8},{10,1... | collective-permute-start | bytes 12296 | tf_op jit(solution)/shard_map/ppermute | solution.py:448
  78.4 17.6 %collective-permute-start.9 = (f32[8,128]{1,0:T(8,128)S(1)}, f32[8,128]{1,0:T(8,128)S(1)}, u32[]{:S(2)}, u32[]{:S(2)}) collective-permute-start(f32[8,128]{1,0:T(8,128)S(1)} %fusion.2), channel_id=1, source_target_pairs={{0,3},{1,0},{2,1},{3,2},{4,255},{5,252},{6,253},{7,254},{8,11},{9,... | collective-permute-start | bytes 12296 | tf_op jit(solution)/shard_map/ppermute | solution.py:448
  83.3 12.8 %collective-permute-start.8 = (f32[8,128]{1,0:T(8,128)S(1)}, f32[8,128]{1,0:T(8,128)S(1)}, u32[]{:S(2)}, u32[]{:S(2)}) collective-permute-start(f32[8,128]{1,0:T(8,128)S(1)} %fusion.2), channel_id=1, source_target_pairs={{0,2},{1,3},{2,0},{3,1},{4,254},{5,255},{6,252},{7,253},{8,10},{9,... | collective-permute-start | bytes 12296 | tf_op jit(solution)/shard_map/ppermute | solution.py:448
  87.5 9.7 %collective-permute-start.7 = (f32[8,128]{1,0:T(8,128)S(1)}, f32[8,128]{1,0:T(8,128)S(1)}, u32[]{:S(2)}, u32[]{:S(2)}) collective-permute-start(f32[8,128]{1,0:T(8,128)S(1)} %fusion.2), channel_id=1, source_target_pairs={{0,1},{1,2},{2,3},{3,0},{4,253},{5,254},{6,255},{7,252},{8,9},{9,1... | collective-permute-start | bytes 12296 | tf_op jit(solution)/shard_map/ppermute | solution.py:448
  90.6 9.5 %collective-permute-start.6 = (f32[8,128]{1,0:T(8,128)S(1)}, f32[8,128]{1,0:T(8,128)S(1)}, u32[]{:S(2)}, u32[]{:S(2)}) collective-permute-start(f32[8,128]{1,0:T(8,128)S(1)} %fusion.2), channel_id=1, source_target_pairs={{0,0},{1,1},{2,2},{3,3},{4,252},{5,253},{6,254},{7,255},{8,8},{9,9... | collective-permute-start | bytes 12296 | tf_op jit(solution)/shard_map/ppermute | solution.py:448
  96.0 4.1 %copy-start.6 = (f32[8,128]{1,0:T(8,128)}, f32[8,128]{1,0:T(8,128)S(1)}, u32[]{:S(2)}) copy-start(f32[8,128]{1,0:T(8,128)S(1)} %collective-permute-done.9.d_ref) | copy-start | bytes 12292
  96.1 4.0 %copy-start.7 = (f32[8,128]{1,0:T(8,128)}, f32[8,128]{1,0:T(8,128)S(1)}, u32[]{:S(2)}) copy-start(f32[8,128]{1,0:T(8,128)S(1)} %collective-permute-done.8.c_ref) | copy-start | bytes 12292
  97.2 2.9 %copy-start.8 = (f32[8,128]{1,0:T(8,128)}, f32[8,128]{1,0:T(8,128)S(1)}, u32[]{:S(2)}) copy-start(f32[8,128]{1,0:T(8,128)S(1)} %collective-permute-done.7.b_ref) | copy-start | bytes 12292
  100.1 0.6 copy-start.9

commit v2 on v1

v2 whole, which is shorter than its diff:
```python
import jax
import jax.numpy as jnp
from jax import lax
from jax.experimental import pallas as pl
from jax.experimental.pallas import tpu as pltpu
from jax.sharding import PartitionSpec as P

TILE = 2048
LANES = 128
VMEM_LIMIT = 48 * 1024 * 1024
NT = (((1,), (1,)), ((), ()))


def prefix_matrix():
    row = lax.broadcasted_iota(jnp.int32, (LANES, 2 * LANES), 0)
    col = lax.broadcasted_iota(jnp.int32, (LANES, 2 * LANES), 1)
    return jnp.where((row <= col) | (col >= LANES), 1.0, 0.0).astype(jnp.bfloat16)


def block_band(device):
    return device if device % 2 == 0 else 64 - device


def smem():
    return pl.BlockSpec(memory_space=pltpu.SMEM)


def vmem():
    return pl.BlockSpec(memory_space=pltpu.VMEM)


def hbm():
    return pl.BlockSpec(memory_space=pltpu.HBM)


def send_kernel(s_ref, rank_hbm, points_hbm, out_ref, rank_ref, points_ref, acc_ref, row_ref,
                hot_a, hot_b, rank_sem, points_sem):
    def fetch_rank(g):
        rows = pl.ds(g * 256, 256)
        return pltpu.make_async_copy(rank_hbm.at[rows, :], rank_ref.at[rows, :], rank_sem.at[g])

    for g in range(8):
        fetch_rank(g).start()
    fetch_points = pltpu.make_async_copy(points_hbm, points_ref, points_sem)
    fetch_points.start()
    shard = s_ref[0]
    prefix = prefix_matrix()
    base = (s_ref[1] + 1).astype(jnp.float32)
    ones = jnp.ones((LANES, LANES), jnp.bfloat16)
    for g in range(8):
        fetch_rank(g).wait()
        source = [rank_ref[pl.ds(g * 256 + j, 8, stride=32), :] for j in range(32)]
        mine = [(source[j] >> 12) == shard for j in range(32)]
        marks = jnp.concatenate([jnp.where(m, 1.0, 0.0) for m in mine], axis=0).astype(jnp.bfloat16)
        counts = jnp.dot(marks, prefix, preferred_element_type=jnp.float32)
        carry = jnp.zeros((8, LANES), jnp.float32) - base
        accs = [jnp.zeros((8, LANES), jnp.int32) for _ in range(16)]
        for j in range(32):
            pos = jnp.where(mine[j], carry + counts[j * 8 : j * 8 + 8, :LANES], -1.0)
            loc = source[j] & 4095
            carry = carry + counts[j * 8 : j * 8 + 8, LANES:]
            for i in range(16):
                accs[i] = jnp.where(pos == float(i), loc, accs[i])
        for i in range(16):
            acc_ref[g * 128 + i * 8 : g * 128 + i * 8 + 8, :] = accs[i]

    acc = acc_ref[...]
    high = (acc >> 6).astype(jnp.float32).astype(jnp.bfloat16)
    low = (acc & 63).astype(jnp.float32).astype(jnp.bfloat16)
    row_ref[...] = 64.0 * jnp.dot(high, ones, preferred_element_type=jnp.float32) + jnp.dot(
        low, ones, preferred_element_type=jnp.float32
    )
    fetch_points.wait()
    lane = lax.broadcasted_iota(jnp.int32, (256, LANES), 1)
    one = jnp.ones((256, LANES), jnp.bfloat16)
    zero = jnp.zeros((256, LANES), jnp.bfloat16)
    for blk in range(4):
        hot_ref = hot_a if blk % 2 == 0 else hot_b
        parts = []
        for i in range(16):
            band = block_band(blk * 16 + i)
            parts.append(row_ref[pl.ds((band // 8) * 128 + band % 8, 16, stride=8), :])
        local = jnp.concatenate(parts, axis=0).astype(jnp.int32)
        chunk = (local >> 7).astype(jnp.float32).astype(jnp.bfloat16)
        hot = jnp.where((local & 127) == lane, 1.0, 0.0).astype(jnp.bfloat16)
        for ch in range(32):
            hot_ref[:, ch * 128 : (ch + 1) * 128] = jnp.where(chunk == one * ch, hot, zero)
        out_ref[blk * 256 : (blk + 1) * 256, :] = jnp.dot(
            hot_ref[...], points_ref[...], preferred_element_type=jnp.float32
        ).astype(jnp.bfloat16)


def send_rows(scalars, rank2d, points):
    return pl.pallas_call(
        send_kernel,
        out_shape=jax.ShapeDtypeStruct((1024, 256), jnp.bfloat16),
        in_specs=[smem(), hbm(), hbm()],
        out_specs=vmem(),
        scratch_shapes=[
            pltpu.VMEM((2048, LANES), jnp.int32),
            pltpu.VMEM((4096, 256), jnp.bfloat16),
            pltpu.VMEM((1024, LANES), jnp.int32),
            pltpu.VMEM((1024, LANES), jnp.float32),
            pltpu.VMEM((256, 4096), jnp.bfloat16),
            pltpu.VMEM((256, 4096), jnp.bfloat16),
            pltpu.SemaphoreType.DMA((8,)),
            pltpu.SemaphoreType.DMA,
        ],
        compiler_params=pltpu.CompilerParams(vmem_limit_bytes=VMEM_LIMIT),
        name="send_rows",
    )(scalars, rank2d, points)


def place_kernel(s_ref, rank_ref, thr_ref, row_ref, col_ref, place_ref, u_ref, v_ref):
    rep = s_ref[2]
    prefix = prefix_matrix()
    shard_iota = lax.broadcasted_iota(jnp.int32, (64, LANES), 0)
    u_iota = lax.broadcasted_iota(jnp.int32, (32, LANES), 0)
    v_iota = lax.broadcasted_iota(jnp.int32, (LANES, LANES), 0)
    for x in range(3):
        start = pl.multiple_of(s_ref[3 + x] * 32, 32)
        carry = jnp.zeros((64, LANES), jnp.float32)
        source = rank_ref[pl.ds(start, 32), :] >> 12
        thr = thr_ref[pl.ds(start, 32), :]
        for j in range(32):
            shard = source[j : j + 1, :]
            hot = shard == shard_iota
            counts = jnp.dot(
                jnp.where(hot, 1.0, 0.0).astype(jnp.bfloat16), prefix, preferred_element_type=jnp.float32
            )
            slot = jnp.sum(jnp.where(hot, carry + counts[:, :LANES], 0.0), axis=0, keepdims=True)
            slot = slot.astype(jnp.int32) - 1
            carry = carry + counts[:, LANES:]
            quarter = slot >> 4
            v = (shard & 7) * 16 + (slot & 15)
            if x == 2:
                place_ref[j : j + 1, :] = (((rep - quarter) & 3) * 8 + (shard >> 3)) * 128 + v
            else:
                u = ((quarter - rep) & 3) * 8 + (shard >> 3)
                u_hot = u == u_iota
                t = thr[j : j + 1, :]
                lanes = slice(j * LANES, (j + 1) * LANES)
                u_ref[0:32, lanes] = jnp.where(u_hot, (t >> 4).astype(jnp.float32), 0.0).astype(jnp.bfloat16)
                u_ref[32:64, lanes] = jnp.where(u_hot, (t & 15).astype(jnp.float32), 0.0).astype(jnp.bfloat16)
                u_ref[64:96, lanes] = jnp.where(u_hot, float(j >= 16), 0.0).astype(jnp.bfloat16)
                v_ref[:, lanes] = jnp.where(v == v_iota, 1.0, 0.0).astype(jnp.bfloat16)
        if x < 2:
            us = u_ref[...]
            vs = v_ref[...]
            rows = lax.dot_general(us, vs, NT, preferred_element_type=jnp.float32)
            cols = lax.dot_general(vs, us, NT, preferred_element_type=jnp.float32)
            row_ref[x, 0:32, :] = 1024.0 / (rows[0:32] * 16.0 + rows[32:64])
            row_ref[x, 32:64, :] = rows[64:96]
            col_ref[x, :, 0:32] = 1024.0 / (cols[:, 0:32] * 16.0 + cols[:, 32:64])
            col_ref[x, :, 32:64] = cols[:, 64:96]


def place(scalars, rank2d, thr2d):
    return pl.pallas_call(
        place_kernel,
        out_shape=(
            jax.ShapeDtypeStruct((2, 64, LANES), jnp.float32),
            jax.ShapeDtypeStruct((2, LANES, 64), jnp.float32),
            jax.ShapeDtypeStruct((32, LANES), jnp.int32),
        ),
        in_specs=[
            pl.BlockSpec(memory_space=pltpu.SMEM),
            pl.BlockSpec(memory_space=pltpu.VMEM),
            pl.BlockSpec(memory_space=pltpu.VMEM),
        ],
        out_specs=(pl.BlockSpec(memory_space=pltpu.VMEM),) * 3,
        scratch_shapes=[
            pltpu.VMEM((96, 4096), jnp.bfloat16),
            pltpu.VMEM((LANES, 4096), jnp.bfloat16),
        ],
        compiler_params=pltpu.CompilerParams(vmem_limit_bytes=VMEM_LIMIT),
        cost_estimate=pl.CostEstimate(flops=2 * 10**9, bytes_accessed=10**7, transcendentals=0),
        name="place",
    )(scalars, rank2d, thr2d)


def square_sums(block):
    values = block.astype(jnp.float32)
    square = values * values
    total = square[:, :LANES] + square[:, LANES:]
    high = total.astype(jnp.bfloat16)
    rest = total - high.astype(jnp.float32)
    middle = rest.astype(jnp.bfloat16)
    low = (rest - middle.astype(jnp.float32)).astype(jnp.bfloat16)
    return high, middle, low


def inverse_column(terms):
    ones = jnp.ones((LANES, LANES), jnp.bfloat16)
    high, middle, low = (jnp.dot(t, ones, preferred_element_type=jnp.float32) for t in terms)
    return lax.rsqrt(high + (middle + low) + 1e-06)


def inverse_row(terms):
    ones = jnp.ones((8, LANES), jnp.bfloat16)
    high, middle, low = (
        lax.dot_general(ones, t, NT, preferred_element_type=jnp.float32) for t in terms
    )
    return lax.rsqrt(high + (middle + low) + 1e-06)


def load_column_meta(at, col_ref, band, quarter, meta):
    for u in range(8):
        rows = slice(at + u * LANES, at + (u + 1) * LANES)
        i = quarter * 8 + u
        meta[1, rows, :] = jnp.broadcast_to(col_ref[band, :, i : i + 1], (LANES, LANES))
        meta[2, rows, :] = jnp.broadcast_to(col_ref[band, :, 32 + i : 33 + i], (LANES, LANES))


def load_row_meta(slot, row_ref, band, quarter, meta):
    for u in range(8):
        lanes = slice(u * LANES, (u + 1) * LANES)
        i = quarter * 8 + u
        meta[slot, 1, :, lanes] = jnp.broadcast_to(row_ref[band, i : i + 1, :], (8, LANES))
        meta[slot, 2, :, lanes] = jnp.broadcast_to(row_ref[band, 32 + i : 33 + i, :], (8, LANES))


def keep_rows(keep_ref, row_offset, col_offset, row_meta, slot, keep, at):
    upper = row_meta[slot, 2] > 0.5
    for t in range(2):
        code = (row_offset + t) * 4 + col_offset
        keep[at, t] = jnp.where(upper, keep_ref[code + 1], keep_ref[code])


def product(left_ref, left_at, right_ref, right_at, prod_ref):
    prod_ref[...] = lax.dot_general(
        left_ref[pl.ds(left_at, 256), :], right_ref[pl.ds(right_at, 512), :], NT,
        preferred_element_type=jnp.float32,
    )


def weigh(prod_ref, left_at, left_meta, right_at, right_meta, slot, keep, keep_at, row_sum, col_sum,
          diagonal):
    sums = [jnp.zeros((8, LANES), jnp.float32) for _ in range(4)]
    lanes = [pl.ds(pl.multiple_of(right_at + ch * LANES, LANES), LANES) for ch in range(4)]
    for i in range(8):
        rows = pl.ds(pl.multiple_of(left_at + i * 32, 32), 32)
        inv_i = left_meta[0, rows, :].reshape(4, 8, LANES)
        rho_i = left_meta[1, rows, :].reshape(4, 8, LANES)
        upper = left_meta[2, rows, :].reshape(4, 8, LANES) > 0.5
        total = row_sum[rows, :].reshape(4, 8, LANES)
        for ch in range(4):
            inv_j = right_meta[slot, 0, :, lanes[ch]][None]
            rho_j = right_meta[slot, 1, :, lanes[ch]][None]
            kept = jnp.where(upper, keep[keep_at, 1, :, lanes[ch]][None], keep[keep_at, 0, :, lanes[ch]][None])
            p = prod_ref[i * 32 : i * 32 + 32, ch * LANES : (ch + 1) * LANES].reshape(4, 8, LANES)
            near = (p * inv_i) * inv_j - 1.0
            w = jnp.maximum(near * jnp.maximum(rho_i, rho_j) + kept, 0.0)
            if diagonal:
                row_ids = lax.broadcasted_iota(jnp.int32, w.shape, 0) * 8 + lax.broadcasted_iota(jnp.int32, w.shape, 1)
                col_ids = lax.broadcasted_iota(jnp.int32, w.shape, 2)
                w = jnp.where(row_ids + (left_at + i * 32) == col_ids + (right_at + ch * LANES), 0.0, w)
            total = total + w
            if not diagonal:
                sums[ch] = sums[ch] + ((w[0] + w[1]) + (w[2] + w[3]))
        row_sum[rows, :] = total.reshape(32, LANES)
    if not diagonal:
        for ch in range(4):
            col_sum[:, lanes[ch]] += sums[ch]


def rows_to_lanes(row_sum, at):
    row = lax.broadcasted_iota(jnp.int32, (LANES, LANES), 0)
    lane = lax.broadcasted_iota(jnp.int32, (LANES, LANES), 1)
    out = []
    for u in range(8):
        total = jnp.sum(row_sum[at + u * LANES : at + (u + 1) * LANES, :], axis=1, keepdims=True)
        out.append(jnp.sum(jnp.where(row == lane, total, 0.0), axis=0, keepdims=True))
    return out


def cols_to_lanes(col_sum):
    return [
        jnp.sum(col_sum[:, u * LANES : (u + 1) * LANES], axis=0, keepdims=True) for u in range(8)
    ]


def near_kernel(s_ref, keep_ref, own_ref, other_ref, row_ref, col_ref, out_ref,
                left_meta, right_meta, keep, prod_a, prod_b, row_sum, col_sum):
    core = s_ref[6]
    own_offset = s_ref[7]
    other_offset = s_ref[8]
    terms = square_sums(own_ref[...])
    left_meta[0] = inverse_column(terms)
    right_meta[0, 0] = inverse_row(terms)
    right_meta[1, 0] = inverse_row(square_sums(other_ref[...]))
    load_column_meta(0, col_ref, 0, 0, left_meta)
    load_row_meta(0, row_ref, 0, 0, right_meta)
    load_row_meta(1, row_ref, 1, 0, right_meta)
    row_sum[...] = jnp.zeros_like(row_sum)
    col_sum[...] = jnp.zeros_like(col_sum)
    keep_rows(keep_ref, own_offset, own_offset, right_meta, 0, keep, 0)
    keep_rows(keep_ref, own_offset, other_offset, right_meta, 1, keep, 1)

    @pl.loop(0, 4)
    def _(i):
        at = pl.multiple_of(i * 256, 256)
        half = pl.multiple_of(((i >> 1) ^ core) * 512, 512)
        product(own_ref, at, own_ref, 0, prod_a)
        product(own_ref, at, own_ref, 512, prod_b)
        weigh(prod_a, at, left_meta, 0, right_meta, 0, keep, 0, row_sum, col_sum, True)
        product(own_ref, at, other_ref, half, prod_a)
        weigh(prod_b, at, left_meta, 512, right_meta, 0, keep, 0, row_sum, col_sum, True)
        weigh(prod_a, at, left_meta, half, right_meta, 1, keep, 1, row_sum, col_sum, False)

    for u, value in enumerate(rows_to_lanes(row_sum, 0)):
        out_ref[0, u : u + 1, :] = value
    for u, value in enumerate(cols_to_lanes(col_sum)):
        out_ref[1, u : u + 1, :] = value


def far_kernel(s_ref, keep_ref, own_hbm, other_hbm, left_hbm, right_ref, row_ref, col_ref, near_ref,
               stay_ref, move_ref, block_ref, left_meta, right_meta, keep, prod_a, prod_b, row_sum,
               col_sum, sems):
    own_offset = s_ref[7]
    other_offset = s_ref[8]
    cross = s_ref[9]
    left_offset = s_ref[10]
    copies = [
        pltpu.make_async_copy(source, block_ref.at[pl.ds(i * 1024, 1024), :], sems.at[i])
        for i, source in enumerate((own_hbm, other_hbm, left_hbm))
    ]
    for copy in copies:
        copy.start()
    right_meta[0, 0] = inverse_row(square_sums(right_ref[...]))
    load_column_meta(0, col_ref, 0, 0, left_meta)
    load_column_meta(1024, col_ref, 1, 0, left_meta)
    load_column_meta(2048, col_ref, cross, 3, left_meta)
    load_row_meta(0, row_ref, 0, 1, right_meta)
    for i, offset in enumerate((own_offset, other_offset, left_offset)):
        keep_rows(keep_ref, offset, own_offset, right_meta, 0, keep, i)
    row_sum[...] = jnp.zeros_like(row_sum)
    col_sum[...] = jnp.zeros_like(col_sum)
    for i, copy in enumerate(copies):
        copy.wait()
        left_meta[0, i * 1024 : (i + 1) * 1024, :] = inverse_column(
            square_sums(block_ref[i * 1024 : (i + 1) * 1024, :])
        )
    product(block_ref, 0, right_ref, 0, prod_a)

    @pl.loop(0, 12)
    def _(i):
        at = pl.multiple_of(i * 256, 256)
        after = pl.multiple_of(jnp.minimum(i + 1, 11) * 256, 256)
        block = i >> 2
        product(block_ref, at, right_ref, 512, prod_b)
        weigh(prod_a, at, left_meta, 0, right_meta, 0, keep, block, row_sum, col_sum, False)
        product(block_ref, after, right_ref, 0, prod_a)
        weigh(prod_b, at, left_meta, 512, right_meta, 0, keep, block, row_sum, col_sum, False)

    own = rows_to_lanes(row_sum, 0)
    other = rows_to_lanes(row_sum, 1024)
    left = rows_to_lanes(row_sum, 2048)
    right = cols_to_lanes(col_sum)
    for u in range(8):
        row = slice(u, u + 1)
        stay_ref[0, row, :] = own[u] + near_ref[0, row, :]
        stay_ref[1, row, :] = right[u]
        stay_ref[2, row, :] = jnp.where(cross == 0, left[u], 0.0)
        move_ref[0, row, :] = other[u] + near_ref[1, row, :]
        move_ref[1, row, :] = jnp.where(cross == 0, 0.0, left[u])


def pair_scratch(lefts, rights, keeps):
    return [
        pltpu.VMEM((3, lefts * 1024, LANES), jnp.float32),
        pltpu.VMEM((rights, 3, 8, 1024), jnp.float32),
        pltpu.VMEM((keeps, 2, 8, 1024), jnp.float32),
        pltpu.VMEM((256, 512), jnp.float32),
        pltpu.VMEM((256, 512), jnp.float32),
        pltpu.VMEM((lefts * 1024, LANES), jnp.float32),
        pltpu.VMEM((8, 1024), jnp.float32),
    ]


def near_pairs(scalars, keep, own, other, rows, cols):
    return pl.pallas_call(
        near_kernel,
        out_shape=jax.ShapeDtypeStruct((2, 8, LANES), jnp.float32),
        in_specs=[smem(), smem(), vmem(), vmem(), vmem(), vmem()],
        out_specs=vmem(),
        scratch_shapes=pair_scratch(1, 2, 2),
        compiler_params=pltpu.CompilerParams(vmem_limit_bytes=VMEM_LIMIT),
        cost_estimate=pl.CostEstimate(flops=2 * 10**9, bytes_accessed=10**7, transcendentals=0),
        name="near_pairs",
    )(scalars, keep, own, other, rows, cols)


def far_pairs(scalars, keep, own, other, left, right, rows, cols, near):
    return pl.pallas_call(
        far_kernel,
        out_shape=(
            jax.ShapeDtypeStruct((3, 8, LANES), jnp.float32),
            jax.ShapeDtypeStruct((2, 8, LANES), jnp.float32),
        ),
        in_specs=[smem(), smem(), hbm(), hbm(), hbm()] + [vmem()] * 4,
        out_specs=(vmem(), vmem()),
        scratch_shapes=[pltpu.VMEM((3072, 256), jnp.bfloat16)]
        + pair_scratch(3, 1, 3)
        + [pltpu.SemaphoreType.DMA((3,))],
        compiler_params=pltpu.CompilerParams(vmem_limit_bytes=VMEM_LIMIT),
        cost_estimate=pl.CostEstimate(flops=4 * 10**9, bytes_accessed=10**7, transcendentals=0),
        name="far_pairs",
    )(scalars, keep, own, other, left, right, rows, cols, near)


def rank_kernel(place_ref, *refs):
    pieces, out_ref = refs[:-1], refs[-1]
    place_at = place_ref[...]
    lane = place_at & 127
    which = place_at >> 7
    total = jnp.zeros((32, LANES), jnp.float32)
    for s in range(4):
        block = pieces[s][0] + pieces[(s + 1) % 4][1] + pieces[(s + 3) % 4][2]
        for u in range(8):
            row = jnp.broadcast_to(block[u : u + 1, :], (32, LANES))
            value = jnp.take_along_axis(row, lane, axis=1)
            total = jnp.where(which == s * 8 + u, value, total)
    out_ref[...] = total * (1.0 / TILE)


def to_rank_order(place_at, pieces):
    return pl.pallas_call(
        rank_kernel,
        out_shape=jax.ShapeDtypeStruct((32, LANES), jnp.float32),
        in_specs=[vmem()] * 5,
        out_specs=vmem(),
        name="to_rank_order",
    )(place_at, *pieces)


def on_device(points, rank_source, thresholds, kept_tiles):
    bands = lax.axis_size("band")
    reps = lax.axis_size("rep")
    device = lax.axis_index("band").astype(jnp.int32)
    rep = lax.axis_index("rep").astype(jnp.int32)
    core = device & 1
    own_band = jnp.where(core == 0, device, bands - device)
    other_band = bands - 1 - own_band
    own_offset = jnp.where(own_band < bands // 2, 0, 2)
    other_offset = 2 - own_offset
    cross = (rep >= 2).astype(jnp.int32)
    left_offset = jnp.where(cross == 1, other_offset, own_offset)
    scalars = jnp.stack([
        device, rep * 16, rep, own_band, other_band, device, core,
        own_offset, other_offset, cross, left_offset,
    ]).astype(jnp.int32)
    codes = lax.dynamic_index_in_dim(kept_tiles, jnp.minimum(own_band, other_band), 0, keepdims=False)
    ids = jnp.arange(16, dtype=jnp.int32)
    a, c = ids // 4, ids % 4
    wanted = jnp.minimum(a, c) * 4 + jnp.maximum(a, c)
    keep = jnp.where(jnp.any(codes[:, None] == wanted[None, :], axis=0), 1.0, -1e30).astype(jnp.float32)

    rank2d = rank_source.reshape(2048, LANES)
    thr2d = thresholds.reshape(2048, LANES)

    def joint(move):
        return [
            (d * reps + r, e * reps + q)
            for d in range(bands)
            for r in range(reps)
            for e, q in (move(d, r),)
        ]

    def shift(value, move):
        return lax.ppermute(value, ("band", "rep"), joint(move))

    payload = send_rows(scalars, rank2d, points)
    own = lax.all_to_all(
        payload.reshape(bands, 16, 256), "band", split_axis=0, concat_axis=0, tiled=True
    ).reshape(1024, 256)
    own, rows, cols, place_at = lax.optimization_barrier((own, *place(scalars, rank2d, thr2d)))

    def to_right(d, r):
        q = (r + 1) % reps
        return (d if q < 2 else d ^ 1), q

    other = shift(own, lambda d, r: (d ^ 1, r))
    right = shift(own, lambda d, r: (d, (r - 1) % reps))
    left = shift(own, to_right)

    near = near_pairs(scalars, keep, own, other, rows, cols)
    stay, move = far_pairs(scalars, keep, own, other, left, right, rows, cols, near)
    moved = shift(move, lambda d, r: (d ^ 1, r))
    sums = stay + jnp.stack([moved[0], jnp.zeros_like(moved[0]), moved[1]])
    home = shift(sums, lambda d, r: (block_band(d), r))
    pieces = [home] + [
        shift(home, lambda d, r, s=s: (d, (r + s) % reps)) for s in range(1, reps)
    ]
    return to_rank_order(place_at, pieces).reshape(points.shape[0])


def solution(mesh):
    in_specs = (P("band", None), P(), P(), P())
    out_specs = P("band")
    return jax.shard_map(
        on_device, mesh=mesh, in_specs=in_specs, out_specs=out_specs, check_vma=False
    )
```

time: 103 us -> 88 us (0.85)
  the two profiles are of different devices: /device:TPU:33 before, /device:TPU:1 now
where the time goes in v2:
time: 88 us; the launch traced here: 87.3 us
  Pallas kernels  29.8 us (34%)
  waiting for transfers between devices  27.1 us (31%)
  starting transfers between devices  25.7 us (29%)
  local copies, waits for them, and re-layouts  4.36 us (5%)
    all_to_all x1, waiting for transfers between devices, on_device(): lax.all_to_all(payload.reshape(bands, 16, 256), 'band', split_axis=0, con...  13.5 us
    ppermute x8, waiting for transfers between devices, shift(): return lax.ppermute(value, ('band', 'rep'), joint(move))  13.5 us
    all_to_all x1, starting transfers between devices, on_device(): lax.all_to_all(payload.reshape(bands, 16, 256), 'band', split_axis=0, con...  13 us
    ppermute x8, starting transfers between devices, shift(): return lax.ppermute(value, ('band', 'rep'), joint(move))  12.7 us
    pallas_call x1, Pallas kernels, far_pairs(): pl.pallas_call(far_kernel, out_shape=(jax.ShapeDtypeStruct((3, 8, LANES),...  10.6 us
    pallas_call x1, Pallas kernels, send_rows(): pl.pallas_call(send_kernel, out_shape=jax.ShapeDtypeStruct((1024, 256), j...  9.01 us
    pallas_call x1, Pallas kernels, near_pairs(): pl.pallas_call(near_kernel, out_shape=jax.ShapeDtypeStruct((2, 8, LANES),...  4.93 us
    unnamed x20, local copies, waits for them, and re-layouts  4.02 us
  transfers between devices with their start and end apart: 9, of which 6 were waited for; matrix products, arithmetic and copies ran while one was open for 0% of the time, Pallas kernels for 10%

profile of v2, /device:TPU:1, one launch (start us, length us, event | category | flops | bytes accessed | tf_op | source)
XLA Modules:
  0.0 87.3 jit_solution(6564955493589791240)
XLA Ops:
  0.0 0.1 stack.47.s_ref
  0.1 1.6 %copy-done.1 = bf16[4096,256]{1,0:T(8,128)(2,1)S(1)} copy-done((bf16[4096,256]{1,0:T(8,128)(2,1)S(1)}, bf16[4096,256]{1,0:T(8,128)(2,1)}, u32[]{:S(2)}) %copy-start.1) | copy-done | bytes 2097176
  1.7 1.2 %copy-done.2 = s32[262144]{0:T(1024)S(1)} copy-done((s32[262144]{0:T(1024)S(1)}, s32[262144]{0:T(1024)}, u32[]{:S(2)}) %copy-start.2) | copy-done | bytes 1048600
  2.9 9.0 %send_rows.1 = bf16[1024,256]{1,0:T(8,128)(2,1)} custom-call(s32[11]{0:T(128)S(1)} %stack.47.s_ref, s32[2048,128]{1,0:T(8,128)S(1)} %bitcast.16, bf16[4096,256]{1,0:T(8,128)(2,1)S(1)} %copy-done.1), custom_call_target="tpu_custom_call" | custom-call | tf_op jit(solution)/shard_map/send_rows/pallas_call | solution.py:94
  11.9 13.0 %all-to-all-start = ((bf16[64,16,256]{2,1,0:T(8,128)(2,1)}), bf16[64,16,256]{2,1,0:T(8,128)(2,1)S(1)}, u32[]{:S(2)}, u32[]{:S(2)}) async-start(bf16[64,16,256]{2,1,0:T(8,128)(2,1)} %bitcast.11), calls=%async_computation | async-start | bytes 1048576 | tf_op jit(solution)/shard_map/all_to_all | solution.py:474
  25.0 3.5 %place.1 = (f32[2,64,128]{2,1,0:T(8,128)S(1)}, f32[2,128,64]{2,1,0:T(8,128)S(1)}, s32[32,128]{1,0:T(8,128)S(1)}) custom-call(s32[11]{0:T(128)S(1)} %stack.47.s_ref, s32[2048,128]{1,0:T(8,128)S(1)} %bitcast.17, s32[2048,128]{1,0:T(8,128)S(1)} %bitcast.23), custom_call_target="tpu_custom_call" | custom-call | flops 2000000000 | bytes 10000000 | tf_op jit(solution)/shard_map/place/pallas_call | solution.py:159
  28.5 0.6 copy-done.4
  29.1 13.5 %all-to-all-done = bf16[64,16,256]{2,1,0:T(8,128)(2,1)S(1)} async-done(((bf16[64,16,256]{2,1,0:T(8,128)(2,1)}), bf16[64,16,256]{2,1,0:T(8,128)(2,1)S(1)}, u32[]{:S(2)}, u32[]{:S(2)}) %all-to-all-start) | async-done | bytes 524320 | tf_op jit(solution)/shard_map/all_to_all | solution.py:474
  42.7 0.4 collective-permute-start
  43.0 0.2 dynamic-slice_reduce_fusion
  43.2 1.4 %collective-permute-start.1 = (bf16[1024,256]{1,0:T(8,128)(2,1)S(1)}, bf16[1024,256]{1,0:T(8,128)(2,1)S(1)}, u32[]{:S(2)}, u32[]{:S(2)}) collective-permute-start(bf16[1024,256]{1,0:T(8,128)(2,1)S(1)} %bitcast.19), channel_id=1, source_target_pairs={{0,1},{1,6},{2,7},{3,0},{4,5},{5,2},{6,3},{7,4},{8,9},{9,14},{10,1... | collective-permute-start | bytes 1572872 | tf_op jit(solution)/shard_map/ppermute | solution.py:471
  44.6 1.7 %collective-permute-start.2 = (bf16[1024,256]{1,0:T(8,128)(2,1)S(1)}, bf16[1024,256]{1,0:T(8,128)(2,1)S(1)}, u32[]{:S(2)}, u32[]{:S(2)}) collective-permute-start(bf16[1024,256]{1,0:T(8,128)(2,1)S(1)} %bitcast.20), channel_id=1, source_target_pairs={{0,3},{1,0},{2,1},{3,2},{4,7},{5,4},{6,5},{7,6},{8,11},{9,8},{10,9... | collective-permute-start | bytes 1572872 | tf_op jit(solution)/shard_map/ppermute | solution.py:471
  46.3 0.1 compare_reduce_fusion
  46.4 0.0 collective-permute-done.other_ref.other_hbm
  46.4 4.9 %near_pairs.1.near_ref = f32[2,8,128]{2,1,0:T(8,128)S(1)} custom-call(s32[11]{0:T(128)S(1)} %stack.47.s_ref, f32[16]{0:T(128)S(1)} %broadcast_select_fusion.keep_ref, bf16[1024,256]{1,0:T(8,128)(2,1)S(1)} %bitcast.21, bf16[1024,256]{1,0:T(8,128)(2,1)S(1)} %collective-permute-done.other_ref.other_hbm, f32[2,64,128]{2,1,0:T(8,128)S(1)} %get-tuple-element.19.row_ref, ...), custom_call_target="tpu_custom_call" | custom-call | flops 2000000000 | bytes 10000000 | tf_op jit(solution)/shard_map/near_pairs/pallas_call | solution.py:382
  51.4 6.7 %collective-permute-done.1.left_hbm = bf16[1024,256]{1,0:T(8,128)(2,1)S(1)} collective-permute-done((bf16[1024,256]{1,0:T(8,128)(2,1)S(1)}, bf16[1024,256]{1,0:T(8,128)(2,1)S(1)}, u32[]{:S(2)}, u32[]{:S(2)}) %collective-permute-start.1) | collective-permute-done | bytes 524320 | tf_op jit(solution)/shard_map/ppermute | solution.py:471
  58.1 0.0 collective-permute-done.2.right_ref
  58.1 10.6 %far_pairs.1 = (f32[3,8,128]{2,1,0:T(8,128)S(1)}, f32[2,8,128]{2,1,0:T(8,128)S(1)}) custom-call(s32[11]{0:T(128)S(1)} %stack.47.s_ref, f32[16]{0:T(128)S(1)} %broadcast_select_fusion.keep_ref, bf16[1024,256]{1,0:T(8,128)(2,1)S(1)} %bitcast.22, bf16[1024,256]{1,0:T(8,128)(2,1)S(1)} %collective-permute-done.other_ref.other_hbm, ...), custom_call_target="tpu_custom_call" | custom-call | flops 4000000000 | bytes 10000000 | tf_op jit(solution)/shard_map/far_pairs/pallas_call | solution.py:395
  68.6 1.0 %collective-permute-start.3 = (f32[2,8,128]{2,1,0:T(8,128)S(1)}, f32[2,8,128]{2,1,0:T(8,128)S(1)}, u32[]{:S(2)}, u32[]{:S(2)}) collective-permute-start(f32[2,8,128]{2,1,0:T(8,128)S(1)} %get-tuple-element.22), channel_id=1, source_target_pairs={{0,4},{1,5},{2,6},{3,7},{4,0},{5,1},{6,2},{7,3},{8,12},{9,13},{10,... | collective-permute-start | bytes 24584 | tf_op jit(solution)/shard_map/ppermute | solution.py:471
  69.6 0.1 pad.1.clone
  69.7 0.8 collective-permute-done.3
  70.4 0.1 maximum_add_fusion
  70.5 3.6 %collective-permute-start.4 = (f32[3,8,128]{2,1,0:T(8,128)S(1)}, f32[3,8,128]{2,1,0:T(8,128)S(1)}, u32[]{:S(2)}, u32[]{:S(2)}) collective-permute-start(f32[3,8,128]{2,1,0:T(8,128)S(1)} %maximum_add_fusion), channel_id=1, source_target_pairs={{0,0},{1,1},{2,2},{3,3},{4,252},{5,253},{6,254},{7,255},{8,8},{9,9... | collective-permute-start | bytes 36872 | tf_op jit(solution)/shard_map/ppermute | solution.py:471
  74.1 4.2 %collective-permute-done.4.refs_0_ = f32[3,8,128]{2,1,0:T(8,128)S(1)} collective-permute-done((f32[3,8,128]{2,1,0:T(8,128)S(1)}, f32[3,8,128]{2,1,0:T(8,128)S(1)}, u32[]{:S(2)}, u32[]{:S(2)}) %collective-permute-start.4) | collective-permute-done | bytes 12320 | tf_op jit(solution)/shard_map/ppermute | solution.py:471
  78.3 1.3 %collective-permute-start.5 = (f32[3,8,128]{2,1,0:T(8,128)S(1)}, f32[3,8,128]{2,1,0:T(8,128)S(1)}, u32[]{:S(2)}, u32[]{:S(2)}) collective-permute-start(f32[3,8,128]{2,1,0:T(8,128)S(1)} %collective-permute-done.4.refs_0_), channel_id=1, source_target_pairs={{0,1},{1,2},{2,3},{3,0},{4,5},{5,6},{6,7},{7,4},{8,9},{9,10},{10,1... | collective-permute-start | bytes 36872 | tf_op jit(solution)/shard_map/ppermute | solution.py:471
  79.6 2.8 %collective-permute-start.6 = (f32[3,8,128]{2,1,0:T(8,128)S(1)}, f32[3,8,128]{2,1,0:T(8,128)S(1)}, u32[]{:S(2)}, u32[]{:S(2)}) collective-permute-start(f32[3,8,128]{2,1,0:T(8,128)S(1)} %collective-permute-done.4.refs_0_), channel_id=1, source_target_pairs={{0,2},{1,3},{2,0},{3,1},{4,6},{5,7},{6,4},{7,5},{8,10},{9,11},{10,... | collective-permute-start | bytes 36872 | tf_op jit(solution)/shard_map/ppermute | solution.py:471
  82.4 0.6 collective-permute-start.7
  83.0 0.0 collective-permute-done.5.refs_1_
  83.0 0.6 collective-permute-done.6.refs_2_
  83.6 1.3 %collective-permute-done.7.refs_3_ = f32[3,8,128]{2,1,0:T(8,128)S(1)} collective-permute-done((f32[3,8,128]{2,1,0:T(8,128)S(1)}, f32[3,8,128]{2,1,0:T(8,128)S(1)}, u32[]{:S(2)}, u32[]{:S(2)}) %collective-permute-start.7) | collective-permute-done | bytes 12320 | tf_op jit(solution)/shard_map/ppermute | solution.py:471
  84.9 0.6 copy-done.9
  85.5 1.8 %to_rank_order.1 = f32[32,128]{1,0:T(8,128)} custom-call(s32[32,128]{1,0:T(8,128)} %copy-done.4, f32[3,8,128]{2,1,0:T(8,128)} %copy-done.6, f32[3,8,128]{2,1,0:T(8,128)} %copy-done.7, f32[3,8,128]{2,1,0:T(8,128)} %copy-done.8, f32[3,8,128]{2,1,0:T(8,128)} %copy-done.9), custom_call_target="tpu_custom_call" | custom-call | tf_op jit(solution)/shard_map/to_rank_order/pallas_call | solution.py:428
  (19 shorter events, 0.0 us)
Async XLA Ops:
  0.0 43.0 %copy-start = (s32[32,10]{0,1:T(8,128)S(1)}, s32[32,10]{0,1:T(8,128)}, u32[]{:S(2)}) copy-start(s32[32,10]{0,1:T(8,128)} %param.7) | copy-start | bytes 3844
  0.1 1.6 %copy-start.1 = (bf16[4096,256]{1,0:T(8,128)(2,1)S(1)}, bf16[4096,256]{1,0:T(8,128)(2,1)}, u32[]{:S(2)}) copy-start(bf16[4096,256]{1,0:T(8,128)(2,1)} %points_hbm.1) | copy-start | bytes 6291460
  1.7 1.2 %copy-start.2 = (s32[262144]{0:T(1024)S(1)}, s32[262144]{0:T(1024)}, u32[]{:S(2)}) copy-start(s32[262144]{0:T(1024)} %param.5) | copy-start | bytes 3145732
  2.9 22.0 %copy-start.3 = (s32[262144]{0:T(1024)S(1)}, s32[262144]{0:T(1024)}, u32[]{:S(2)}) copy-start(s32[262144]{0:T(1024)} %param.5) | copy-start | bytes 3145732
  2.9 22.0 %copy-start.5 = (s32[262144]{0:T(1024)S(1)}, s32[262144]{0:T(1024)}, u32[]{:S(2)}) copy-start(s32[262144]{0:T(1024)} %param.6) | copy-start | bytes 3145732
  11.9 30.7 %all-to-all-start = ((bf16[64,16,256]{2,1,0:T(8,128)(2,1)}), bf16[64,16,256]{2,1,0:T(8,128)(2,1)S(1)}, u32[]{:S(2)}, u32[]{:S(2)}) async-start(bf16[64,16,256]{2,1,0:T(8,128)(2,1)} %bitcast.11), calls=%async_computation | async-start | bytes 1048576 | tf_op jit(solution)/shard_map/all_to_all | solution.py:474
  28.5 0.6 copy-start.4
  42.7 3.8 %collective-permute-start = (bf16[1024,256]{1,0:T(8,128)(2,1)S(1)}, bf16[1024,256]{1,0:T(8,128)(2,1)S(1)}, u32[]{:S(2)}, u32[]{:S(2)}) collective-permute-start(bf16[1024,256]{1,0:T(8,128)(2,1)S(1)} %bitcast.18), channel_id=1, source_target_pairs={{0,4},{1,5},{2,6},{3,7},{4,0},{5,1},{6,2},{7,3},{8,12},{9,13},{10,... | collective-permute-start | bytes 1572872 | tf_op jit(solution)/shard_map/ppermute | solution.py:471
  43.2 14.8 %collective-permute-start.1 = (bf16[1024,256]{1,0:T(8,128)(2,1)S(1)}, bf16[1024,256]{1,0:T(8,128)(2,1)S(1)}, u32[]{:S(2)}, u32[]{:S(2)}) collective-permute-start(bf16[1024,256]{1,0:T(8,128)(2,1)S(1)} %bitcast.19), channel_id=1, source_target_pairs={{0,1},{1,6},{2,7},{3,0},{4,5},{5,2},{6,3},{7,4},{8,9},{9,14},{10,1... | collective-permute-start | bytes 1572872 | tf_op jit(solution)/shard_map/ppermute | solution.py:471
  44.6 13.4 %collective-permute-start.2 = (bf16[1024,256]{1,0:T(8,128)(2,1)S(1)}, bf16[1024,256]{1,0:T(8,128)(2,1)S(1)}, u32[]{:S(2)}, u32[]{:S(2)}) collective-permute-start(bf16[1024,256]{1,0:T(8,128)(2,1)S(1)} %bitcast.20), channel_id=1, source_target_pairs={{0,3},{1,0},{2,1},{3,2},{4,7},{5,4},{6,5},{7,6},{8,11},{9,8},{10,9... | collective-permute-start | bytes 1572872 | tf_op jit(solution)/shard_map/ppermute | solution.py:471
  68.6 1.8 %collective-permute-start.3 = (f32[2,8,128]{2,1,0:T(8,128)S(1)}, f32[2,8,128]{2,1,0:T(8,128)S(1)}, u32[]{:S(2)}, u32[]{:S(2)}) collective-permute-start(f32[2,8,128]{2,1,0:T(8,128)S(1)} %get-tuple-element.22), channel_id=1, source_target_pairs={{0,4},{1,5},{2,6},{3,7},{4,0},{5,1},{6,2},{7,3},{8,12},{9,13},{10,... | collective-permute-start | bytes 24584 | tf_op jit(solution)/shard_map/ppermute | solution.py:471
  70.5 7.7 %collective-permute-start.4 = (f32[3,8,128]{2,1,0:T(8,128)S(1)}, f32[3,8,128]{2,1,0:T(8,128)S(1)}, u32[]{:S(2)}, u32[]{:S(2)}) collective-permute-start(f32[3,8,128]{2,1,0:T(8,128)S(1)} %maximum_add_fusion), channel_id=1, source_target_pairs={{0,0},{1,1},{2,2},{3,3},{4,252},{5,253},{6,254},{7,255},{8,8},{9,9... | collective-permute-start | bytes 36872 | tf_op jit(solution)/shard_map/ppermute | solution.py:471
  78.3 6.7 %copy-start.6 = (f32[3,8,128]{2,1,0:T(8,128)}, f32[3,8,128]{2,1,0:T(8,128)S(1)}, u32[]{:S(2)}) copy-start(f32[3,8,128]{2,1,0:T(8,128)S(1)} %collective-permute-done.4.refs_0_) | copy-start | bytes 36868
  78.3 4.7 %collective-permute-start.5 = (f32[3,8,128]{2,1,0:T(8,128)S(1)}, f32[3,8,128]{2,1,0:T(8,128)S(1)}, u32[]{:S(2)}, u32[]{:S(2)}) collective-permute-start(f32[3,8,128]{2,1,0:T(8,128)S(1)} %collective-permute-done.4.refs_0_), channel_id=1, source_target_pairs={{0,1},{1,2},{2,3},{3,0},{4,5},{5,6},{6,7},{7,4},{8,9},{9,10},{10,1... | collective-permute-start | bytes 36872 | tf_op jit(solution)/shard_map/ppermute | solution.py:471
  79.6 4.0 %collective-permute-start.6 = (f32[3,8,128]{2,1,0:T(8,128)S(1)}, f32[3,8,128]{2,1,0:T(8,128)S(1)}, u32[]{:S(2)}, u32[]{:S(2)}) collective-permute-start(f32[3,8,128]{2,1,0:T(8,128)S(1)} %collective-permute-done.4.refs_0_), channel_id=1, source_target_pairs={{0,2},{1,3},{2,0},{3,1},{4,6},{5,7},{6,4},{7,5},{8,10},{9,11},{10,... | collective-permute-start | bytes 36872 | tf_op jit(solution)/shard_map/ppermute | solution.py:471
  82.4 2.5 %collective-permute-start.7 = (f32[3,8,128]{2,1,0:T(8,128)S(1)}, f32[3,8,128]{2,1,0:T(8,128)S(1)}, u32[]{:S(2)}, u32[]{:S(2)}) collective-permute-start(f32[3,8,128]{2,1,0:T(8,128)S(1)} %collective-permute-done.4.refs_0_), channel_id=1, source_target_pairs={{0,3},{1,0},{2,1},{3,2},{4,7},{5,4},{6,5},{7,6},{8,11},{9,8},{10,9... | collective-permute-start | bytes 36872 | tf_op jit(solution)/shard_map/ppermute | solution.py:471
  83.0 1.9 %copy-start.7 = (f32[3,8,128]{2,1,0:T(8,128)}, f32[3,8,128]{2,1,0:T(8,128)S(1)}, u32[]{:S(2)}) copy-start(f32[3,8,128]{2,1,0:T(8,128)S(1)} %collective-permute-done.5.refs_1_) | copy-start | bytes 36868
  83.6 1.3 %copy-start.8 = (f32[3,8,128]{2,1,0:T(8,128)}, f32[3,8,128]{2,1,0:T(8,128)S(1)}, u32[]{:S(2)}) copy-start(f32[3,8,128]{2,1,0:T(8,128)S(1)} %collective-permute-done.6.refs_2_) | copy-start | bytes 36868
  84.9 0.6 copy-start.9

commit v3 on v2

--- a/solution.py
+++ b/solution.py
@@ -7,7 +7,7 @@
 
 TILE = 2048
 LANES = 128
-VMEM_LIMIT = 48 * 1024 * 1024
+VMEM_LIMIT = 60 * 1024 * 1024
 NT = (((1,), (1,)), ((), ()))
 
 
@@ -111,17 +111,27 @@
     )(scalars, rank2d, points)
 
 
-def place_kernel(s_ref, rank_ref, thr_ref, row_ref, col_ref, place_ref, u_ref, v_ref):
+def place_kernel(s_ref, rank_hbm, thr_hbm, row_ref, col_ref, place_ref, u_ref, v_ref, rank_ref, thr_ref, sems):
+    copies = []
+    for x in range(3):
+        start = pl.multiple_of(s_ref[3 + x] * 32, 32)
+        copies.append((
+            pltpu.make_async_copy(rank_hbm.at[pl.ds(start, 32), :], rank_ref.at[x], sems.at[x, 0]),
+            pltpu.make_async_copy(thr_hbm.at[pl.ds(start, 32), :], thr_ref.at[x], sems.at[x, 1]),
+        ))
+        for copy in copies[x]:
+            copy.start()
     rep = s_ref[2]
     prefix = prefix_matrix()
     shard_iota = lax.broadcasted_iota(jnp.int32, (64, LANES), 0)
     u_iota = lax.broadcasted_iota(jnp.int32, (32, LANES), 0)
     v_iota = lax.broadcasted_iota(jnp.int32, (LANES, LANES), 0)
     for x in range(3):
-        start = pl.multiple_of(s_ref[3 + x] * 32, 32)
+        for copy in copies[x]:
+            copy.wait()
         carry = jnp.zeros((64, LANES), jnp.float32)
-        source = rank_ref[pl.ds(start, 32), :] >> 12
-        thr = thr_ref[pl.ds(start, 32), :]
+        source = rank_ref[x] >> 12
+        thr = thr_ref[x]
         for j in range(32):
             shard = source[j : j + 1, :]
             hot = shard == shard_iota
@@ -163,15 +173,14 @@
             jax.ShapeDtypeStruct((2, LANES, 64), jnp.float32),
             jax.ShapeDtypeStruct((32, LANES), jnp.int32),
         ),
-        in_specs=[
-            pl.BlockSpec(memory_space=pltpu.SMEM),
-            pl.BlockSpec(memory_space=pltpu.VMEM),
-            pl.BlockSpec(memory_space=pltpu.VMEM),
-        ],
-        out_specs=(pl.BlockSpec(memory_space=pltpu.VMEM),) * 3,
+        in_specs=[smem(), hbm(), hbm()],
+        out_specs=(vmem(),) * 3,
         scratch_shapes=[
             pltpu.VMEM((96, 4096), jnp.bfloat16),
             pltpu.VMEM((LANES, 4096), jnp.bfloat16),
+            pltpu.VMEM((3, 32, LANES), jnp.int32),
+            pltpu.VMEM((3, 32, LANES), jnp.int32),
+            pltpu.SemaphoreType.DMA((3, 2)),
         ],
         compiler_params=pltpu.CompilerParams(vmem_limit_bytes=VMEM_LIMIT),
         cost_estimate=pl.CostEstimate(flops=2 * 10**9, bytes_accessed=10**7, transcendentals=0),
@@ -204,50 +213,47 @@
     return lax.rsqrt(high + (middle + low) + 1e-06)
 
 
-def load_column_meta(at, col_ref, band, quarter, meta):
+def load_column_meta(col_ref, band, quarter, meta):
     for u in range(8):
-        rows = slice(at + u * LANES, at + (u + 1) * LANES)
+        rows = slice(u * LANES, (u + 1) * LANES)
         i = quarter * 8 + u
         meta[1, rows, :] = jnp.broadcast_to(col_ref[band, :, i : i + 1], (LANES, LANES))
         meta[2, rows, :] = jnp.broadcast_to(col_ref[band, :, 32 + i : 33 + i], (LANES, LANES))
 
 
-def load_row_meta(slot, row_ref, band, quarter, meta):
+def load_row_meta(at, row_ref, band, quarter, keep_ref, row_offset, col_offset, meta, keep):
     for u in range(8):
-        lanes = slice(u * LANES, (u + 1) * LANES)
+        lanes = slice(at + u * LANES, at + (u + 1) * LANES)
         i = quarter * 8 + u
-        meta[slot, 1, :, lanes] = jnp.broadcast_to(row_ref[band, i : i + 1, :], (8, LANES))
-        meta[slot, 2, :, lanes] = jnp.broadcast_to(row_ref[band, 32 + i : 33 + i, :], (8, LANES))
-
-
-def keep_rows(keep_ref, row_offset, col_offset, row_meta, slot, keep, at):
-    upper = row_meta[slot, 2] > 0.5
-    for t in range(2):
-        code = (row_offset + t) * 4 + col_offset
-        keep[at, t] = jnp.where(upper, keep_ref[code + 1], keep_ref[code])
+        meta[1, :, lanes] = jnp.broadcast_to(row_ref[band, i : i + 1, :], (8, LANES))
+        upper = jnp.broadcast_to(row_ref[band, 32 + i : 33 + i, :], (8, LANES)) > 0.5
+        for t in range(2):
+            code = (row_offset + t) * 4 + col_offset
+            keep[t, :, lanes] = jnp.where(upper, keep_ref[code + 1], keep_ref[code])
 
 
 def product(left_ref, left_at, right_ref, right_at, prod_ref):
+    rows, cols = prod_ref.shape
     prod_ref[...] = lax.dot_general(
-        left_ref[pl.ds(left_at, 256), :], right_ref[pl.ds(right_at, 512), :], NT,
+        left_ref[pl.ds(left_at, rows), :], right_ref[pl.ds(right_at, cols), :], NT,
         preferred_element_type=jnp.float32,
     )
 
 
-def weigh(prod_ref, left_at, left_meta, right_at, right_meta, slot, keep, keep_at, row_sum, col_sum,
-          diagonal):
-    sums = [jnp.zeros((8, LANES), jnp.float32) for _ in range(4)]
-    lanes = [pl.ds(pl.multiple_of(right_at + ch * LANES, LANES), LANES) for ch in range(4)]
-    for i in range(8):
+def weigh(prod_ref, left_at, left_meta, right_at, right_meta, keep, row_sum, col_sum, diagonal):
+    chunks = prod_ref.shape[1] // LANES
+    sums = [jnp.zeros((8, LANES), jnp.float32) for _ in range(chunks)]
+    lanes = [pl.ds(pl.multiple_of(right_at + ch * LANES, LANES), LANES) for ch in range(chunks)]
+    for i in range(prod_ref.shape[0] // 32):
         rows = pl.ds(pl.multiple_of(left_at + i * 32, 32), 32)
         inv_i = left_meta[0, rows, :].reshape(4, 8, LANES)
         rho_i = left_meta[1, rows, :].reshape(4, 8, LANES)
         upper = left_meta[2, rows, :].reshape(4, 8, LANES) > 0.5
         total = row_sum[rows, :].reshape(4, 8, LANES)
-        for ch in range(4):
-            inv_j = right_meta[slot, 0, :, lanes[ch]][None]
-            rho_j = right_meta[slot, 1, :, lanes[ch]][None]
-            kept = jnp.where(upper, keep[keep_at, 1, :, lanes[ch]][None], keep[keep_at, 0, :, lanes[ch]][None])
+        for ch in range(chunks):
+            inv_j = right_meta[0, :, lanes[ch]][None]
+            rho_j = right_meta[1, :, lanes[ch]][None]
+            kept = jnp.where(upper, keep[1, :, lanes[ch]][None], keep[0, :, lanes[ch]][None])
             p = prod_ref[i * 32 : i * 32 + 32, ch * LANES : (ch + 1) * LANES].reshape(4, 8, LANES)
             near = (p * inv_i) * inv_j - 1.0
             w = jnp.maximum(near * jnp.maximum(rho_i, rho_j) + kept, 0.0)
@@ -260,42 +266,42 @@
                 sums[ch] = sums[ch] + ((w[0] + w[1]) + (w[2] + w[3]))
         row_sum[rows, :] = total.reshape(32, LANES)
     if not diagonal:
-        for ch in range(4):
+        for ch in range(chunks):
             col_sum[:, lanes[ch]] += sums[ch]
 
 
-def rows_to_lanes(row_sum, at):
+def rows_to_lanes(row_sum):
     row = lax.broadcasted_iota(jnp.int32, (LANES, LANES), 0)
     lane = lax.broadcasted_iota(jnp.int32, (LANES, LANES), 1)
     out = []
     for u in range(8):
-        total = jnp.sum(row_sum[at + u * LANES : at + (u + 1) * LANES, :], axis=1, keepdims=True)
+        total = jnp.sum(row_sum[u * LANES : (u + 1) * LANES, :], axis=1, keepdims=True)
         out.append(jnp.sum(jnp.where(row == lane, total, 0.0), axis=0, keepdims=True))
     return out
 
 
-def cols_to_lanes(col_sum):
+def cols_to_lanes(col_sum, at):
     return [
-        jnp.sum(col_sum[:, u * LANES : (u + 1) * LANES], axis=0, keepdims=True) for u in range(8)
+        jnp.sum(col_sum[:, at + u * LANES : at + (u + 1) * LANES], axis=0, keepdims=True)
+        for u in range(8)
     ]
 
 
-def near_kernel(s_ref, keep_ref, own_ref, other_ref, row_ref, col_ref, out_ref,
+def near_kernel(s_ref, keep_ref, own_ref, other_ref, row_ref, col_ref, out_ref, inverse_ref,
                 left_meta, right_meta, keep, prod_a, prod_b, row_sum, col_sum):
     core = s_ref[6]
     own_offset = s_ref[7]
     other_offset = s_ref[8]
     terms = square_sums(own_ref[...])
     left_meta[0] = inverse_column(terms)
-    right_meta[0, 0] = inverse_row(terms)
-    right_meta[1, 0] = inverse_row(square_sums(other_ref[...]))
-    load_column_meta(0, col_ref, 0, 0, left_meta)
-    load_row_meta(0, row_ref, 0, 0, right_meta)
-    load_row_meta(1, row_ref, 1, 0, right_meta)
+    right_meta[0, :, 0:1024] = inverse_row(terms)
+    right_meta[0, :, 1024:2048] = inverse_row(square_sums(other_ref[...]))
+    inverse_ref[...] = right_meta[0]
+    load_column_meta(col_ref, 0, 0, left_meta)
+    load_row_meta(0, row_ref, 0, 0, keep_ref, own_offset, own_offset, right_meta, keep)
+    load_row_meta(1024, row_ref, 1, 0, keep_ref, own_offset, other_offset, right_meta, keep)
     row_sum[...] = jnp.zeros_like(row_sum)
     col_sum[...] = jnp.zeros_like(col_sum)
-    keep_rows(keep_ref, own_offset, own_offset, right_meta, 0, keep, 0)
-    keep_rows(keep_ref, own_offset, other_offset, right_meta, 1, keep, 1)
 
     @pl.loop(0, 4)
     def _(i):
@@ -303,20 +309,21 @@
         half = pl.multiple_of(((i >> 1) ^ core) * 512, 512)
         product(own_ref, at, own_ref, 0, prod_a)
         product(own_ref, at, own_ref, 512, prod_b)
-        weigh(prod_a, at, left_meta, 0, right_meta, 0, keep, 0, row_sum, col_sum, True)
+        weigh(prod_a, at, left_meta, 0, right_meta, keep, row_sum, col_sum, True)
         product(own_ref, at, other_ref, half, prod_a)
-        weigh(prod_b, at, left_meta, 512, right_meta, 0, keep, 0, row_sum, col_sum, True)
-        weigh(prod_a, at, left_meta, half, right_meta, 1, keep, 1, row_sum, col_sum, False)
-
-    for u, value in enumerate(rows_to_lanes(row_sum, 0)):
-        out_ref[0, u : u + 1, :] = value
-    for u, value in enumerate(cols_to_lanes(col_sum)):
-        out_ref[1, u : u + 1, :] = value
+        weigh(prod_b, at, left_meta, 512, right_meta, keep, row_sum, col_sum, True)
+        weigh(prod_a, at, left_meta, 1024 + half, right_meta, keep, row_sum, col_sum, False)
+
+    own = rows_to_lanes(row_sum)
+    other = cols_to_lanes(col_sum, 1024)
+    for u in range(8):
+        out_ref[0, u : u + 1, :] = own[u]
+        out_ref[1, u : u + 1, :] = other[u]
 
 
 def far_kernel(s_ref, keep_ref, own_hbm, other_hbm, left_hbm, right_ref, row_ref, col_ref, near_ref,
-               stay_ref, move_ref, block_ref, left_meta, right_meta, keep, prod_a, prod_b, row_sum,
-               col_sum, sems):
+               inverse_ref, stay_ref, move_ref, block_ref, left_meta, right_meta, keep, prod_a,
+               prod_b, row_sum, col_sum, sems):
     own_offset = s_ref[7]
     other_offset = s_ref[8]
     cross = s_ref[9]
@@ -327,36 +334,39 @@
     ]
     for copy in copies:
         copy.start()
-    right_meta[0, 0] = inverse_row(square_sums(right_ref[...]))
-    load_column_meta(0, col_ref, 0, 0, left_meta)
-    load_column_meta(1024, col_ref, 1, 0, left_meta)
-    load_column_meta(2048, col_ref, cross, 3, left_meta)
-    load_row_meta(0, row_ref, 0, 1, right_meta)
-    for i, offset in enumerate((own_offset, other_offset, left_offset)):
-        keep_rows(keep_ref, offset, own_offset, right_meta, 0, keep, i)
+    left_meta[0] = inverse_column(square_sums(right_ref[...]))
+    load_column_meta(col_ref, 0, 1, left_meta)
+    load_row_meta(0, row_ref, 0, 0, keep_ref, own_offset, own_offset, right_meta, keep)
+    load_row_meta(1024, row_ref, 1, 0, keep_ref, own_offset, other_offset, right_meta, keep)
+    load_row_meta(2048, row_ref, cross, 3, keep_ref, own_offset, left_offset, right_meta, keep)
+    right_meta[0, :, 0:2048] = inverse_ref[...]
     row_sum[...] = jnp.zeros_like(row_sum)
     col_sum[...] = jnp.zeros_like(col_sum)
-    for i, copy in enumerate(copies):
+    for copy in copies:
         copy.wait()
-        left_meta[0, i * 1024 : (i + 1) * 1024, :] = inverse_column(
-            square_sums(block_ref[i * 1024 : (i + 1) * 1024, :])
-        )
-    product(block_ref, 0, right_ref, 0, prod_a)
-
-    @pl.loop(0, 12)
+    right_meta[0, :, 2048:3072] = inverse_row(square_sums(block_ref[2048:3072, :]))
+    rows, cols = prod_a.shape
+    steps = 1024 // rows
+    total = steps * (3072 // cols)
+    product(right_ref, 0, block_ref, 0, prod_a)
+
+    def place_of(t):
+        return pl.multiple_of((t % steps) * rows, rows), pl.multiple_of((t // steps) * cols, cols)
+
+    @pl.loop(0, total // 2)
     def _(i):
-        at = pl.multiple_of(i * 256, 256)
-        after = pl.multiple_of(jnp.minimum(i + 1, 11) * 256, 256)
-        block = i >> 2
-        product(block_ref, at, right_ref, 512, prod_b)
-        weigh(prod_a, at, left_meta, 0, right_meta, 0, keep, block, row_sum, col_sum, False)
-        product(block_ref, after, right_ref, 0, prod_a)
-        weigh(prod_b, at, left_meta, 512, right_meta, 0, keep, block, row_sum, col_sum, False)
-
-    own = rows_to_lanes(row_sum, 0)
-    other = rows_to_lanes(row_sum, 1024)
-    left = rows_to_lanes(row_sum, 2048)
-    right = cols_to_lanes(col_sum)
+        left_a, right_a = place_of(i * 2)
+        left_b, right_b = place_of(i * 2 + 1)
+        left_c, right_c = place_of(jnp.minimum(i * 2 + 2, total - 1))
+        product(right_ref, left_b, block_ref, right_b, prod_b)
+        weigh(prod_a, left_a, left_meta, right_a, right_meta, keep, row_sum, col_sum, False)
+        product(right_ref, left_c, block_ref, right_c, prod_a)
+        weigh(prod_b, left_b, left_meta, right_b, right_meta, keep, row_sum, col_sum, False)
+
+    right = rows_to_lanes(row_sum)
+    own = cols_to_lanes(col_sum, 0)
+    other = cols_to_lanes(col_sum, 1024)
+    left = cols_to_lanes(col_sum, 2048)
     for u in range(8):
         row = slice(u, u + 1)
         stay_ref[0, row, :] = own[u] + near_ref[0, row, :]
@@ -366,25 +376,31 @@
         move_ref[1, row, :] = jnp.where(cross == 0, 0.0, left[u])
 
 
-def pair_scratch(lefts, rights, keeps):
+FAR_TILE = (512, 512)
+
+
+def pair_scratch(columns, tile):
     return [
-        pltpu.VMEM((3, lefts * 1024, LANES), jnp.float32),
-        pltpu.VMEM((rights, 3, 8, 1024), jnp.float32),
-        pltpu.VMEM((keeps, 2, 8, 1024), jnp.float32),
-        pltpu.VMEM((256, 512), jnp.float32),
-        pltpu.VMEM((256, 512), jnp.float32),
-        pltpu.VMEM((lefts * 1024, LANES), jnp.float32),
-        pltpu.VMEM((8, 1024), jnp.float32),
+        pltpu.VMEM((3, 1024, LANES), jnp.float32),
+        pltpu.VMEM((2, 8, columns), jnp.float32),
+        pltpu.VMEM((2, 8, columns), jnp.float32),
+        pltpu.VMEM(tile, jnp.float32),
+        pltpu.VMEM(tile, jnp.float32),
+        pltpu.VMEM((1024, LANES), jnp.float32),
+        pltpu.VMEM((8, columns), jnp.float32),
     ]
 
 
 def near_pairs(scalars, keep, own, other, rows, cols):
     return pl.pallas_call(
         near_kernel,
-        out_shape=jax.ShapeDtypeStruct((2, 8, LANES), jnp.float32),
+        out_shape=(
+            jax.ShapeDtypeStruct((2, 8, LANES), jnp.float32),
+            jax.ShapeDtypeStruct((8, 2048), jnp.float32),
+        ),
         in_specs=[smem(), smem(), vmem(), vmem(), vmem(), vmem()],
-        out_specs=vmem(),
-        scratch_shapes=pair_scratch(1, 2, 2),
+        out_specs=(vmem(), vmem()),
+        scratch_shapes=pair_scratch(2048, (256, 512)),
         compiler_params=pltpu.CompilerParams(vmem_limit_bytes=VMEM_LIMIT),
         cost_estimate=pl.CostEstimate(flops=2 * 10**9, bytes_accessed=10**7, transcendentals=0),
         name="near_pairs",
@@ -398,15 +414,15 @@
             jax.ShapeDtypeStruct((3, 8, LANES), jnp.float32),
             jax.ShapeDtypeStruct((2, 8, LANES), jnp.float32),
         ),
-        in_specs=[smem(), smem(), hbm(), hbm(), hbm()] + [vmem()] * 4,
+        in_specs=[smem(), smem(), hbm(), hbm(), hbm()] + [vmem()] * 5,
         out_specs=(vmem(), vmem()),
         scratch_shapes=[pltpu.VMEM((3072, 256), jnp.bfloat16)]
-        + pair_scratch(3, 1, 3)
+        + pair_scratch(3072, FAR_TILE)
         + [pltpu.SemaphoreType.DMA((3,))],
         compiler_params=pltpu.CompilerParams(vmem_limit_bytes=VMEM_LIMIT),
         cost_estimate=pl.CostEstimate(flops=4 * 10**9, bytes_accessed=10**7, transcendentals=0),
         name="far_pairs",
-    )(scalars, keep, own, other, left, right, rows, cols, near)
+    )(scalars, keep, own, other, left, right, rows, cols, *near)
 
 
 def rank_kernel(place_ref, *refs):

time: 88 us -> 87.3 us (level)
  waiting for transfers between devices: 27.1 us -> 23.3 us
  Pallas kernels: 29.8 us -> 32.9 us
  other arithmetic: 0.18 us -> 1.45 us
  local copies, waits for them, and re-layouts: 4.36 us -> 3.35 us
    ppermute x8, waiting for transfers between devices: 13.5 us -> 11 us  [shift(): return lax.ppermute(value, ('band', 'rep'), joint(move))]
    pallas_call x1, Pallas kernels: 3.54 us -> 5.42 us  [place(): pl.pallas_call(place_kernel, out_shape=(jax.ShapeDtypeStruct((2, 64, LANE...]
    unnamed x20 -> x18, local copies, waits for them, and re-layouts: 4.02 us -> 2.41 us
    pallas_call x1, Pallas kernels: 4.93 us -> 6.47 us  [near_pairs(): pl.pallas_call(near_kernel, out_shape=(jax.ShapeDtypeStruct((2, 8, LANES)...]
    all_to_all x1, waiting for transfers between devices: 13.5 us -> 12.3 us  [on_device(): lax.all_to_all(payload.reshape(bands, 16, 256), 'band', split_axis=0, con...]
  transfers between devices with their start and end apart: 9 -> 9, of which waited for: 6 -> 6; matrix products, arithmetic and copies ran while one was open for 0% -> 1% of each run, Pallas kernels for 10% -> 14%
where the time goes in v3:
time: 87.3 us; the launch traced here: 86.5 us
  Pallas kernels  32.9 us (38%)
  starting transfers between devices  25.4 us (29%)
  waiting for transfers between devices  23.3 us (27%)
  local copies, waits for them, and re-layouts  3.35 us (4%)
  other arithmetic  1.45 us (2%)
    all_to_all x1, starting transfers between devices, on_device(): lax.all_to_all(payload.reshape(bands, 16, 256), 'band', split_axis=0, con...  13 us
    ppermute x8, starting transfers between devices, shift(): return lax.ppermute(value, ('band', 'rep'), joint(move))  12.4 us
    all_to_all x1, waiting for transfers between devices, on_device(): lax.all_to_all(payload.reshape(bands, 16, 256), 'band', split_axis=0, con...  12.3 us
    ppermute x8, waiting for transfers between devices, shift(): return lax.ppermute(value, ('band', 'rep'), joint(move))  11 us
    pallas_call x1, Pallas kernels, far_pairs(): pl.pallas_call(far_kernel, out_shape=(jax.ShapeDtypeStruct((3, 8, LANES),...  10.7 us
    pallas_call x1, Pallas kernels, send_rows(): pl.pallas_call(send_kernel, out_shape=jax.ShapeDtypeStruct((1024, 256), j...  8.54 us
    pallas_call x1, Pallas kernels, near_pairs(): pl.pallas_call(near_kernel, out_shape=(jax.ShapeDtypeStruct((2, 8, LANES)...  6.47 us
    pallas_call x1, Pallas kernels, place(): pl.pallas_call(place_kernel, out_shape=(jax.ShapeDtypeStruct((2, 64, LANE...  5.42 us
  transfers between devices with their start and end apart: 9, of which 6 were waited for; matrix products, arithmetic and copies ran while one was open for 1% of the time, Pallas kernels for 14%

profile of v3, /device:TPU:1, one launch (start us, length us, event | category | flops | bytes accessed | tf_op | source)
XLA Modules:
  0.0 86.5 jit_solution(9699333633078234213)
XLA Ops:
  0.0 0.7 stack.47.s_ref
  0.7 8.5 %send_rows.1 = bf16[1024,256]{1,0:T(8,128)(2,1)} custom-call(s32[11]{0:T(128)} %stack.47.s_ref, s32[2048,128]{1,0:T(8,128)} %bitcast.17, bf16[4096,256]{1,0:T(8,128)(2,1)} %points_hbm.1), custom_call_target="tpu_custom_call" | custom-call | tf_op jit(solution)/shard_map/send_rows/pallas_call | solution.py:94
  9.2 13.0 %all-to-all-start = ((bf16[64,16,256]{2,1,0:T(8,128)(2,1)}), bf16[64,16,256]{2,1,0:T(8,128)(2,1)S(1)}, u32[]{:S(2)}, u32[]{:S(2)}) async-start(bf16[64,16,256]{2,1,0:T(8,128)(2,1)} %bitcast.16), calls=%async_computation | async-start | bytes 1048576 | tf_op jit(solution)/shard_map/all_to_all | solution.py:490
  22.2 5.4 %place.1 = (f32[2,64,128]{2,1,0:T(8,128)}, f32[2,128,64]{2,1,0:T(8,128)}, s32[32,128]{1,0:T(8,128)}) custom-call(s32[11]{0:T(128)} %stack.47.s_ref, s32[2048,128]{1,0:T(8,128)} %bitcast.18, s32[2048,128]{1,0:T(8,128)} %bitcast.24), custom_call_target="tpu_custom_call" | custom-call | flops 2000000000 | bytes 10000000 | tf_op jit(solution)/shard_map/place/pallas_call | solution.py:169
  27.7 12.3 %all-to-all-done = bf16[64,16,256]{2,1,0:T(8,128)(2,1)S(1)} async-done(((bf16[64,16,256]{2,1,0:T(8,128)(2,1)}), bf16[64,16,256]{2,1,0:T(8,128)(2,1)S(1)}, u32[]{:S(2)}, u32[]{:S(2)}) %all-to-all-start) | async-done | bytes 524320 | tf_op jit(solution)/shard_map/all_to_all | solution.py:490
  40.0 0.4 collective-permute-start
  40.4 0.2 dynamic-slice_reduce_fusion
  40.5 1.4 %collective-permute-start.1 = (bf16[1024,256]{1,0:T(8,128)(2,1)S(1)}, bf16[1024,256]{1,0:T(8,128)(2,1)S(1)}, u32[]{:S(2)}, u32[]{:S(2)}) collective-permute-start(bf16[1024,256]{1,0:T(8,128)(2,1)S(1)} %bitcast.20), channel_id=1, source_target_pairs={{0,1},{1,6},{2,7},{3,0},{4,5},{5,2},{6,3},{7,4},{8,9},{9,14},{10,1... | collective-permute-start | bytes 1572872 | tf_op jit(solution)/shard_map/ppermute | solution.py:487
  41.9 1.7 %collective-permute-start.2 = (bf16[1024,256]{1,0:T(8,128)(2,1)S(1)}, bf16[1024,256]{1,0:T(8,128)(2,1)S(1)}, u32[]{:S(2)}, u32[]{:S(2)}) collective-permute-start(bf16[1024,256]{1,0:T(8,128)(2,1)S(1)} %bitcast.21), channel_id=1, source_target_pairs={{0,3},{1,0},{2,1},{3,2},{4,7},{5,4},{6,5},{7,6},{8,11},{9,8},{10,9... | collective-permute-start | bytes 1572872 | tf_op jit(solution)/shard_map/ppermute | solution.py:487
  43.6 0.1 compare_reduce_fusion
  43.7 0.6 broadcast_select_fusion.keep_ref
  44.3 0.0 collective-permute-done.other_ref.other_hbm
  44.3 0.8 copy-done.6
  45.1 6.5 %near_pairs.1 = (f32[2,8,128]{2,1,0:T(8,128)}, f32[8,2048]{1,0:T(8,128)}) custom-call(s32[11]{0:T(128)} %stack.47.s_ref, f32[16]{0:T(128)} %broadcast_select_fusion.keep_ref, bf16[1024,256]{1,0:T(8,128)(2,1)} %bitcast.22, bf16[1024,256]{1,0:T(8,128)(2,1)} %copy-done.6, f32[2,64,128]{2,1,0:T(8,128)} %get-tuple-element.21.row_ref, ...), custom_call_target="tpu_custom_call" | custom-call | flops 2000000000 | bytes 10000000 | tf_op jit(solution)/shard_map/near_pairs/pallas_call | solution.py:395
  51.6 3.8 %collective-permute-done.1.left_hbm = bf16[1024,256]{1,0:T(8,128)(2,1)S(1)} collective-permute-done((bf16[1024,256]{1,0:T(8,128)(2,1)S(1)}, bf16[1024,256]{1,0:T(8,128)(2,1)S(1)}, u32[]{:S(2)}, u32[]{:S(2)}) %collective-permute-start.1) | collective-permute-done | bytes 524320 | tf_op jit(solution)/shard_map/ppermute | solution.py:487
  55.4 0.0 collective-permute-done.2.right_ref
  55.4 0.8 copy-done.7
  56.2 0.2 copy-done.8
  56.4 10.7 %far_pairs.1 = (f32[3,8,128]{2,1,0:T(8,128)}, f32[2,8,128]{2,1,0:T(8,128)}) custom-call(s32[11]{0:T(128)} %stack.47.s_ref, f32[16]{0:T(128)} %broadcast_select_fusion.keep_ref, bf16[1024,256]{1,0:T(8,128)(2,1)} %bitcast.23, bf16[1024,256]{1,0:T(8,128)(2,1)} %copy-done.6, bf16[1024,256]{1,0:T(8,128)(2,1)} %copy-done.7, bf16[1024,256]{1,0:T(8,128)(2,1)} %copy-done.8, ...), custom_call_target="tpu_custom_call" | custom-call | flops 4000000000 | bytes 10000000 | tf_op jit(solution)/shard_map/far_pairs/pallas_call | solution.py:411
  67.1 1.0 %collective-permute-start.3 = (f32[2,8,128]{2,1,0:T(8,128)}, f32[2,8,128]{2,1,0:T(8,128)S(1)}, u32[]{:S(2)}, u32[]{:S(2)}) collective-permute-start(f32[2,8,128]{2,1,0:T(8,128)} %get-tuple-element.26), channel_id=1, source_target_pairs={{0,4},{1,5},{2,6},{3,7},{4,0},{5,1},{6,2},{7,3},{8,12},{9,13},{10,... | collective-permute-start | bytes 24584 | tf_op jit(solution)/shard_map/ppermute | solution.py:487
  68.0 0.1 pad.1.clone
  68.1 1.0 %collective-permute-done.3 = f32[2,8,128]{2,1,0:T(8,128)S(1)} collective-permute-done((f32[2,8,128]{2,1,0:T(8,128)}, f32[2,8,128]{2,1,0:T(8,128)S(1)}, u32[]{:S(2)}, u32[]{:S(2)}) %collective-permute-start.3) | collective-permute-done | bytes 8224 | tf_op jit(solution)/shard_map/ppermute | solution.py:487
  69.1 0.8 maximum_add_fusion
  69.9 3.4 %collective-permute-start.4 = (f32[3,8,128]{2,1,0:T(8,128)S(1)}, f32[3,8,128]{2,1,0:T(8,128)S(1)}, u32[]{:S(2)}, u32[]{:S(2)}) collective-permute-start(f32[3,8,128]{2,1,0:T(8,128)S(1)} %maximum_add_fusion), channel_id=1, source_target_pairs={{0,0},{1,1},{2,2},{3,3},{4,252},{5,253},{6,254},{7,255},{8,8},{9,9... | collective-permute-start | bytes 36872 | tf_op jit(solution)/shard_map/ppermute | solution.py:487
  73.3 4.3 %collective-permute-done.4.refs_0_ = f32[3,8,128]{2,1,0:T(8,128)S(1)} collective-permute-done((f32[3,8,128]{2,1,0:T(8,128)S(1)}, f32[3,8,128]{2,1,0:T(8,128)S(1)}, u32[]{:S(2)}, u32[]{:S(2)}) %collective-permute-start.4) | collective-permute-done | bytes 12320 | tf_op jit(solution)/shard_map/ppermute | solution.py:487
  77.6 1.2 %collective-permute-start.5 = (f32[3,8,128]{2,1,0:T(8,128)S(1)}, f32[3,8,128]{2,1,0:T(8,128)S(1)}, u32[]{:S(2)}, u32[]{:S(2)}) collective-permute-start(f32[3,8,128]{2,1,0:T(8,128)S(1)} %collective-permute-done.4.refs_0_), channel_id=1, source_target_pairs={{0,1},{1,2},{2,3},{3,0},{4,5},{5,6},{6,7},{7,4},{8,9},{9,10},{10,1... | collective-permute-start | bytes 36872 | tf_op jit(solution)/shard_map/ppermute | solution.py:487
  78.8 2.8 %collective-permute-start.6 = (f32[3,8,128]{2,1,0:T(8,128)S(1)}, f32[3,8,128]{2,1,0:T(8,128)S(1)}, u32[]{:S(2)}, u32[]{:S(2)}) collective-permute-start(f32[3,8,128]{2,1,0:T(8,128)S(1)} %collective-permute-done.4.refs_0_), channel_id=1, source_target_pairs={{0,2},{1,3},{2,0},{3,1},{4,6},{5,7},{6,4},{7,5},{8,10},{9,11},{10,... | collective-permute-start | bytes 36872 | tf_op jit(solution)/shard_map/ppermute | solution.py:487
  81.5 0.6 collective-permute-start.7
  82.2 0.6 collective-permute-done.6.refs_2_
  82.8 1.3 %collective-permute-done.7.refs_3_ = f32[3,8,128]{2,1,0:T(8,128)S(1)} collective-permute-done((f32[3,8,128]{2,1,0:T(8,128)S(1)}, f32[3,8,128]{2,1,0:T(8,128)S(1)}, u32[]{:S(2)}, u32[]{:S(2)}) %collective-permute-start.7) | collective-permute-done | bytes 12320 | tf_op jit(solution)/shard_map/ppermute | solution.py:487
  84.1 0.6 copy-done.5
  84.7 1.8 %to_rank_order.1 = f32[32,128]{1,0:T(8,128)} custom-call(s32[32,128]{1,0:T(8,128)} %get-tuple-element.19.place_ref, f32[3,8,128]{2,1,0:T(8,128)} %copy-done.2, f32[3,8,128]{2,1,0:T(8,128)} %copy-done.3, f32[3,8,128]{2,1,0:T(8,128)} %copy-done.4, f32[3,8,128]{2,1,0:T(8,128)} %copy-done.5), custom_call_target="tpu_custom_call" | custom-call | tf_op jit(solution)/shard_map/to_rank_order/pallas_call | solution.py:444
  (17 shorter events, 0.0 us)
Async XLA Ops:
  0.0 40.4 %copy-start = (s32[32,10]{0,1:T(8,128)S(1)}, s32[32,10]{0,1:T(8,128)}, u32[]{:S(2)}) copy-start(s32[32,10]{0,1:T(8,128)} %param.7) | copy-start | bytes 3844
  9.2 30.7 %all-to-all-start = ((bf16[64,16,256]{2,1,0:T(8,128)(2,1)}), bf16[64,16,256]{2,1,0:T(8,128)(2,1)S(1)}, u32[]{:S(2)}, u32[]{:S(2)}) async-start(bf16[64,16,256]{2,1,0:T(8,128)(2,1)} %bitcast.16), calls=%async_computation | async-start | bytes 1048576 | tf_op jit(solution)/shard_map/all_to_all | solution.py:490
  40.0 4.4 %copy-start.1 = (bf16[64,16,256]{2,1,0:T(8,128)(2,1)}, bf16[64,16,256]{2,1,0:T(8,128)(2,1)S(1)}, u32[]{:S(2)}) copy-start(bf16[64,16,256]{2,1,0:T(8,128)(2,1)S(1)} %all-to-all-done) | copy-start | bytes 1572868
  40.0 4.3 %collective-permute-start = (bf16[1024,256]{1,0:T(8,128)(2,1)S(1)}, bf16[1024,256]{1,0:T(8,128)(2,1)S(1)}, u32[]{:S(2)}, u32[]{:S(2)}) collective-permute-start(bf16[1024,256]{1,0:T(8,128)(2,1)S(1)} %bitcast.19), channel_id=1, source_target_pairs={{0,4},{1,5},{2,6},{3,7},{4,0},{5,1},{6,2},{7,3},{8,12},{9,13},{10,... | collective-permute-start | bytes 1572872 | tf_op jit(solution)/shard_map/ppermute | solution.py:487
  40.5 14.8 %collective-permute-start.1 = (bf16[1024,256]{1,0:T(8,128)(2,1)S(1)}, bf16[1024,256]{1,0:T(8,128)(2,1)S(1)}, u32[]{:S(2)}, u32[]{:S(2)}) collective-permute-start(bf16[1024,256]{1,0:T(8,128)(2,1)S(1)} %bitcast.20), channel_id=1, source_target_pairs={{0,1},{1,6},{2,7},{3,0},{4,5},{5,2},{6,3},{7,4},{8,9},{9,14},{10,1... | collective-permute-start | bytes 1572872 | tf_op jit(solution)/shard_map/ppermute | solution.py:487
  41.9 13.4 %collective-permute-start.2 = (bf16[1024,256]{1,0:T(8,128)(2,1)S(1)}, bf16[1024,256]{1,0:T(8,128)(2,1)S(1)}, u32[]{:S(2)}, u32[]{:S(2)}) collective-permute-start(bf16[1024,256]{1,0:T(8,128)(2,1)S(1)} %bitcast.21), channel_id=1, source_target_pairs={{0,3},{1,0},{2,1},{3,2},{4,7},{5,4},{6,5},{7,6},{8,11},{9,8},{10,9... | collective-permute-start | bytes 1572872 | tf_op jit(solution)/shard_map/ppermute | solution.py:487
  44.3 0.8 copy-start.6
  55.4 0.8 copy-start.7
  55.4 1.0 %copy-start.8 = (bf16[1024,256]{1,0:T(8,128)(2,1)}, bf16[1024,256]{1,0:T(8,128)(2,1)S(1)}, u32[]{:S(2)}) copy-start(bf16[1024,256]{1,0:T(8,128)(2,1)S(1)} %collective-permute-done.2.right_ref) | copy-start | bytes 1572868
  67.1 2.0 %collective-permute-start.3 = (f32[2,8,128]{2,1,0:T(8,128)}, f32[2,8,128]{2,1,0:T(8,128)S(1)}, u32[]{:S(2)}, u32[]{:S(2)}) collective-permute-start(f32[2,8,128]{2,1,0:T(8,128)} %get-tuple-element.26), channel_id=1, source_target_pairs={{0,4},{1,5},{2,6},{3,7},{4,0},{5,1},{6,2},{7,3},{8,12},{9,13},{10,... | collective-permute-start | bytes 24584 | tf_op jit(solution)/shard_map/ppermute | solution.py:487
  69.9 7.7 %collective-permute-start.4 = (f32[3,8,128]{2,1,0:T(8,128)S(1)}, f32[3,8,128]{2,1,0:T(8,128)S(1)}, u32[]{:S(2)}, u32[]{:S(2)}) collective-permute-start(f32[3,8,128]{2,1,0:T(8,128)S(1)} %maximum_add_fusion), channel_id=1, source_target_pairs={{0,0},{1,1},{2,2},{3,3},{4,252},{5,253},{6,254},{7,255},{8,8},{9,9... | collective-permute-start | bytes 36872 | tf_op jit(solution)/shard_map/ppermute | solution.py:487
  77.6 6.5 %copy-start.2 = (f32[3,8,128]{2,1,0:T(8,128)}, f32[3,8,128]{2,1,0:T(8,128)S(1)}, u32[]{:S(2)}) copy-start(f32[3,8,128]{2,1,0:T(8,128)S(1)} %collective-permute-done.4.refs_0_) | copy-start | bytes 36868
  77.6 4.6 %collective-permute-start.5 = (f32[3,8,128]{2,1,0:T(8,128)S(1)}, f32[3,8,128]{2,1,0:T(8,128)S(1)}, u32[]{:S(2)}, u32[]{:S(2)}) collective-permute-start(f32[3,8,128]{2,1,0:T(8,128)S(1)} %collective-permute-done.4.refs_0_), channel_id=1, source_target_pairs={{0,1},{1,2},{2,3},{3,0},{4,5},{5,6},{6,7},{7,4},{8,9},{9,10},{10,1... | collective-permute-start | bytes 36872 | tf_op jit(solution)/shard_map/ppermute | solution.py:487
  78.8 4.0 %collective-permute-start.6 = (f32[3,8,128]{2,1,0:T(8,128)S(1)}, f32[3,8,128]{2,1,0:T(8,128)S(1)}, u32[]{:S(2)}, u32[]{:S(2)}) collective-permute-start(f32[3,8,128]{2,1,0:T(8,128)S(1)} %collective-permute-done.4.refs_0_), channel_id=1, source_target_pairs={{0,2},{1,3},{2,0},{3,1},{4,6},{5,7},{6,4},{7,5},{8,10},{9,11},{10,... | collective-permute-start | bytes 36872 | tf_op jit(solution)/shard_map/ppermute | solution.py:487
  81.5 2.5 %collective-permute-start.7 = (f32[3,8,128]{2,1,0:T(8,128)S(1)}, f32[3,8,128]{2,1,0:T(8,128)S(1)}, u32[]{:S(2)}, u32[]{:S(2)}) collective-permute-start(f32[3,8,128]{2,1,0:T(8,128)S(1)} %collective-permute-done.4.refs_0_), channel_id=1, source_target_pairs={{0,3},{1,0},{2,1},{3,2},{4,7},{5,4},{6,5},{7,6},{8,11},{9,8},{10,9... | collective-permute-start | bytes 36872 | tf_op jit(solution)/shard_map/ppermute | solution.py:487
  82.2 1.9 %copy-start.3 = (f32[3,8,128]{2,1,0:T(8,128)}, f32[3,8,128]{2,1,0:T(8,128)S(1)}, u32[]{:S(2)}) copy-start(f32[3,8,128]{2,1,0:T(8,128)S(1)} %collective-permute-done.5.refs_1_) | copy-start | bytes 36868
  82.8 1.3 %copy-start.4 = (f32[3,8,128]{2,1,0:T(8,128)}, f32[3,8,128]{2,1,0:T(8,128)S(1)}, u32[]{:S(2)}) copy-start(f32[3,8,128]{2,1,0:T(8,128)S(1)} %collective-permute-done.6.refs_2_) | copy-start | bytes 36868
  84.1 0.6 copy-start.5

commit v4 on v3

--- a/solution.py
+++ b/solution.py
@@ -7,7 +7,8 @@
 
 TILE = 2048
 LANES = 128
-VMEM_LIMIT = 60 * 1024 * 1024
+SEND_VMEM = 60 * 1024 * 1024
+VMEM = 28 * 1024 * 1024
 NT = (((1,), (1,)), ((), ()))
 
 
@@ -33,8 +34,8 @@
     return pl.BlockSpec(memory_space=pltpu.HBM)
 
 
-def send_kernel(s_ref, rank_hbm, points_hbm, out_ref, rank_ref, points_ref, acc_ref, row_ref,
-                hot_a, hot_b, rank_sem, points_sem):
+def send_kernel(rank_hbm, points_hbm, out_ref, rank_ref, points_ref, acc_ref, row_ref,
+                hot_ref, rank_sem, points_sem):
     def fetch_rank(g):
         rows = pl.ds(g * 256, 256)
         return pltpu.make_async_copy(rank_hbm.at[rows, :], rank_ref.at[rows, :], rank_sem.at[g])
@@ -43,9 +44,9 @@
         fetch_rank(g).start()
     fetch_points = pltpu.make_async_copy(points_hbm, points_ref, points_sem)
     fetch_points.start()
-    shard = s_ref[0]
+    shard = lax.axis_index("band")
     prefix = prefix_matrix()
-    base = (s_ref[1] + 1).astype(jnp.float32)
+    base = (lax.axis_index("rep") * 16 + 1).astype(jnp.float32)
     ones = jnp.ones((LANES, LANES), jnp.bfloat16)
     for g in range(8):
         fetch_rank(g).wait()
@@ -71,44 +72,41 @@
         low, ones, preferred_element_type=jnp.float32
     )
     fetch_points.wait()
-    lane = lax.broadcasted_iota(jnp.int32, (256, LANES), 1)
-    one = jnp.ones((256, LANES), jnp.bfloat16)
-    zero = jnp.zeros((256, LANES), jnp.bfloat16)
-    for blk in range(4):
-        hot_ref = hot_a if blk % 2 == 0 else hot_b
-        parts = []
-        for i in range(16):
-            band = block_band(blk * 16 + i)
-            parts.append(row_ref[pl.ds((band // 8) * 128 + band % 8, 16, stride=8), :])
-        local = jnp.concatenate(parts, axis=0).astype(jnp.int32)
-        chunk = (local >> 7).astype(jnp.float32).astype(jnp.bfloat16)
-        hot = jnp.where((local & 127) == lane, 1.0, 0.0).astype(jnp.bfloat16)
-        for ch in range(32):
-            hot_ref[:, ch * 128 : (ch + 1) * 128] = jnp.where(chunk == one * ch, hot, zero)
-        out_ref[blk * 256 : (blk + 1) * 256, :] = jnp.dot(
-            hot_ref[...], points_ref[...], preferred_element_type=jnp.float32
-        ).astype(jnp.bfloat16)
-
-
-def send_rows(scalars, rank2d, points):
+    lane = lax.broadcasted_iota(jnp.int32, (1024, LANES), 1)
+    one = jnp.ones((1024, LANES), jnp.bfloat16)
+    zero = jnp.zeros((1024, LANES), jnp.bfloat16)
+    parts = []
+    for i in range(64):
+        band = block_band(i)
+        parts.append(row_ref[pl.ds((band // 8) * 128 + band % 8, 16, stride=8), :])
+    local = jnp.concatenate(parts, axis=0).astype(jnp.int32)
+    chunk = (local >> 7).astype(jnp.float32).astype(jnp.bfloat16)
+    hot = jnp.where((local & 127) == lane, 1.0, 0.0).astype(jnp.bfloat16)
+    for ch in range(32):
+        hot_ref[:, ch * 128 : (ch + 1) * 128] = jnp.where(chunk == one * ch, hot, zero)
+    out_ref[...] = jnp.dot(
+        hot_ref[...], points_ref[...], preferred_element_type=jnp.float32
+    ).astype(jnp.bfloat16)
+
+
+def send_rows(rank2d, points):
     return pl.pallas_call(
         send_kernel,
         out_shape=jax.ShapeDtypeStruct((1024, 256), jnp.bfloat16),
-        in_specs=[smem(), hbm(), hbm()],
+        in_specs=[hbm(), hbm()],
         out_specs=vmem(),
         scratch_shapes=[
             pltpu.VMEM((2048, LANES), jnp.int32),
             pltpu.VMEM((4096, 256), jnp.bfloat16),
             pltpu.VMEM((1024, LANES), jnp.int32),
             pltpu.VMEM((1024, LANES), jnp.float32),
-            pltpu.VMEM((256, 4096), jnp.bfloat16),
-            pltpu.VMEM((256, 4096), jnp.bfloat16),
+            pltpu.VMEM((1024, 4096), jnp.bfloat16),
             pltpu.SemaphoreType.DMA((8,)),
             pltpu.SemaphoreType.DMA,
         ],
-        compiler_params=pltpu.CompilerParams(vmem_limit_bytes=VMEM_LIMIT),
+        compiler_params=pltpu.CompilerParams(vmem_limit_bytes=SEND_VMEM),
         name="send_rows",
-    )(scalars, rank2d, points)
+    )(rank2d, points)
 
 
 def place_kernel(s_ref, rank_hbm, thr_hbm, row_ref, col_ref, place_ref, u_ref, v_ref, rank_ref, thr_ref, sems):
@@ -182,7 +180,7 @@
             pltpu.VMEM((3, 32, LANES), jnp.int32),
             pltpu.SemaphoreType.DMA((3, 2)),
         ],
-        compiler_params=pltpu.CompilerParams(vmem_limit_bytes=VMEM_LIMIT),
+        compiler_params=pltpu.CompilerParams(vmem_limit_bytes=VMEM),
         cost_estimate=pl.CostEstimate(flops=2 * 10**9, bytes_accessed=10**7, transcendentals=0),
         name="place",
     )(scalars, rank2d, thr2d)
@@ -401,7 +399,7 @@
         in_specs=[smem(), smem(), vmem(), vmem(), vmem(), vmem()],
         out_specs=(vmem(), vmem()),
         scratch_shapes=pair_scratch(2048, (256, 512)),
-        compiler_params=pltpu.CompilerParams(vmem_limit_bytes=VMEM_LIMIT),
+        compiler_params=pltpu.CompilerParams(vmem_limit_bytes=VMEM),
         cost_estimate=pl.CostEstimate(flops=2 * 10**9, bytes_accessed=10**7, transcendentals=0),
         name="near_pairs",
     )(scalars, keep, own, other, rows, cols)
@@ -419,7 +417,7 @@
         scratch_shapes=[pltpu.VMEM((3072, 256), jnp.bfloat16)]
         + pair_scratch(3072, FAR_TILE)
         + [pltpu.SemaphoreType.DMA((3,))],
-        compiler_params=pltpu.CompilerParams(vmem_limit_bytes=VMEM_LIMIT),
+        compiler_params=pltpu.CompilerParams(vmem_limit_bytes=VMEM),
         cost_estimate=pl.CostEstimate(flops=4 * 10**9, bytes_accessed=10**7, transcendentals=0),
         name="far_pairs",
     )(scalars, keep, own, other, left, right, rows, cols, *near)
@@ -446,6 +444,7 @@
         out_shape=jax.ShapeDtypeStruct((32, LANES), jnp.float32),
         in_specs=[vmem()] * 5,
         out_specs=vmem(),
+        compiler_params=pltpu.CompilerParams(vmem_limit_bytes=VMEM),
         name="to_rank_order",
     )(place_at, *pieces)
 
@@ -486,7 +485,7 @@
     def shift(value, move):
         return lax.ppermute(value, ("band", "rep"), joint(move))
 
-    payload = send_rows(scalars, rank2d, points)
+    payload = send_rows(rank2d, points)
     own = lax.all_to_all(
         payload.reshape(bands, 16, 256), "band", split_axis=0, concat_axis=0, tiled=True
     ).reshape(1024, 256)

time: 87.3 us -> 79.8 us (0.914)
  Pallas kernels: 32.9 us -> 26.1 us
  waiting for transfers between devices: 23.3 us -> 26.8 us
  local copies, waits for them, and re-layouts: 3.35 us -> 0.36 us
  other arithmetic: 1.45 us -> 0.18 us
    unnamed x18 -> x6, local copies, waits for them, and re-layouts: 2.41 us -> 0.01 us
    ppermute x8, waiting for transfers between devices: 11 us -> 13.3 us  [shift(): return lax.ppermute(value, ('band', 'rep'), joint(move))]
    pallas_call x1, Pallas kernels: 10.7 us -> 8.63 us  [far_pairs(): pl.pallas_call(far_kernel, out_shape=(jax.ShapeDtypeStruct((3, 8, LANES),...]
    pallas_call x1, Pallas kernels: 8.54 us -> 7.15 us  [send_rows(): pl.pallas_call(send_kernel, out_shape=jax.ShapeDtypeStruct((1024, 256), j...]
    pallas_call x1, Pallas kernels: 6.47 us -> 5.16 us  [near_pairs(): pl.pallas_call(near_kernel, out_shape=(jax.ShapeDtypeStruct((2, 8, LANES)...]
    pallas_call x1, Pallas kernels: 5.42 us -> 4.12 us  [place(): pl.pallas_call(place_kernel, out_shape=(jax.ShapeDtypeStruct((2, 64, LANE...]
    all_to_all x1, waiting for transfers between devices: 12.3 us -> 13.5 us  [on_device(): lax.all_to_all(payload.reshape(bands, 16, 256), 'band', split_axis=0, con...]
  transfers between devices with their start and end apart: 9 -> 9, of which waited for: 6 -> 6; matrix products, arithmetic and copies ran while one was open for 1% -> 1% of each run, Pallas kernels for 14% -> 12%
where the time goes in v4:
time: 79.8 us; the launch traced here: 79.3 us
  waiting for transfers between devices  26.8 us (34%)
  Pallas kernels  26.1 us (33%)
  starting transfers between devices  25.8 us (32%)
    all_to_all x1, waiting for transfers between devices, on_device(): lax.all_to_all(payload.reshape(bands, 16, 256), 'band', split_axis=0, con...  13.5 us
    ppermute x8, waiting for transfers between devices, shift(): return lax.ppermute(value, ('band', 'rep'), joint(move))  13.3 us
    all_to_all x1, starting transfers between devices, on_device(): lax.all_to_all(payload.reshape(bands, 16, 256), 'band', split_axis=0, con...  13 us
    ppermute x8, starting transfers between devices, shift(): return lax.ppermute(value, ('band', 'rep'), joint(move))  12.8 us
    pallas_call x1, Pallas kernels, far_pairs(): pl.pallas_call(far_kernel, out_shape=(jax.ShapeDtypeStruct((3, 8, LANES),...  8.63 us
    pallas_call x1, Pallas kernels, send_rows(): pl.pallas_call(send_kernel, out_shape=jax.ShapeDtypeStruct((1024, 256), j...  7.15 us
    pallas_call x1, Pallas kernels, near_pairs(): pl.pallas_call(near_kernel, out_shape=(jax.ShapeDtypeStruct((2, 8, LANES)...  5.16 us
    pallas_call x1, Pallas kernels, place(): pl.pallas_call(place_kernel, out_shape=(jax.ShapeDtypeStruct((2, 64, LANE...  4.12 us
  transfers between devices with their start and end apart: 9, of which 6 were waited for; matrix products, arithmetic and copies ran while one was open for 1% of the time, Pallas kernels for 12%

profile of v4, /device:TPU:1, one launch (start us, length us, event | category | flops | bytes accessed | tf_op | source)
XLA Modules:
  0.0 79.3 jit_solution(7495751002888433503)
XLA Ops:
  0.0 0.0 copy-start
  0.0 7.2 %send_rows.1 = bf16[1024,256]{1,0:T(8,128)(2,1)} custom-call(s32[2048,128]{1,0:T(8,128)} %bitcast.16, bf16[4096,256]{1,0:T(8,128)(2,1)} %points_hbm.1), custom_call_target="tpu_custom_call" | custom-call | tf_op jit(solution)/shard_map/send_rows/pallas_call | solution.py:93
  7.2 13.0 %all-to-all-start = ((bf16[64,16,256]{2,1,0:T(8,128)(2,1)}), bf16[64,16,256]{2,1,0:T(8,128)(2,1)S(1)}, u32[]{:S(2)}, u32[]{:S(2)}) async-start(bf16[64,16,256]{2,1,0:T(8,128)(2,1)} %bitcast.24), calls=%async_computation | async-start | bytes 1048576 | tf_op jit(solution)/shard_map/all_to_all | solution.py:489
  20.2 0.1 stack.47.s_ref
  20.3 0.0 copy-done.1
  20.3 0.0 copy-done.2
  20.3 4.1 %place.1 = (f32[2,64,128]{2,1,0:T(8,128)S(1)}, f32[2,128,64]{2,1,0:T(8,128)S(1)}, s32[32,128]{1,0:T(8,128)S(1)}) custom-call(s32[11]{0:T(128)S(1)} %stack.47.s_ref, s32[2048,128]{1,0:T(8,128)S(1)} %bitcast.17, s32[2048,128]{1,0:T(8,128)S(1)} %bitcast.23), custom_call_target="tpu_custom_call" | custom-call | flops 2000000000 | bytes 10000000 | tf_op jit(solution)/shard_map/place/pallas_call | solution.py:167
  24.4 13.5 %all-to-all-done = bf16[64,16,256]{2,1,0:T(8,128)(2,1)S(1)} async-done(((bf16[64,16,256]{2,1,0:T(8,128)(2,1)}), bf16[64,16,256]{2,1,0:T(8,128)(2,1)S(1)}, u32[]{:S(2)}, u32[]{:S(2)}) %all-to-all-start) | async-done | bytes 524320 | tf_op jit(solution)/shard_map/all_to_all | solution.py:489
  37.9 0.4 collective-permute-start
  38.3 0.0 copy-done
  38.3 0.2 dynamic-slice_reduce_fusion
  38.5 1.4 %collective-permute-start.1 = (bf16[1024,256]{1,0:T(8,128)(2,1)S(1)}, bf16[1024,256]{1,0:T(8,128)(2,1)S(1)}, u32[]{:S(2)}, u32[]{:S(2)}) collective-permute-start(bf16[1024,256]{1,0:T(8,128)(2,1)S(1)} %bitcast.19), channel_id=1, source_target_pairs={{0,1},{1,6},{2,7},{3,0},{4,5},{5,2},{6,3},{7,4},{8,9},{9,14},{10,1... | collective-permute-start | bytes 1572872 | tf_op jit(solution)/shard_map/ppermute | solution.py:486
  39.9 1.7 %collective-permute-start.2 = (bf16[1024,256]{1,0:T(8,128)(2,1)S(1)}, bf16[1024,256]{1,0:T(8,128)(2,1)S(1)}, u32[]{:S(2)}, u32[]{:S(2)}) collective-permute-start(bf16[1024,256]{1,0:T(8,128)(2,1)S(1)} %bitcast.20), channel_id=1, source_target_pairs={{0,3},{1,0},{2,1},{3,2},{4,7},{5,4},{6,5},{7,6},{8,11},{9,8},{10,9... | collective-permute-start | bytes 1572872 | tf_op jit(solution)/shard_map/ppermute | solution.py:486
  41.6 0.1 compare_reduce_fusion
  41.7 0.0 collective-permute-done.other_ref.other_hbm
  41.7 5.2 %near_pairs.1 = (f32[2,8,128]{2,1,0:T(8,128)S(1)}, f32[8,2048]{1,0:T(8,128)S(1)}) custom-call(s32[11]{0:T(128)S(1)} %stack.47.s_ref, f32[16]{0:T(128)S(1)} %broadcast_select_fusion.keep_ref, bf16[1024,256]{1,0:T(8,128)(2,1)S(1)} %bitcast.21, bf16[1024,256]{1,0:T(8,128)(2,1)S(1)} %collective-permute-done.other_ref.other_hbm, ...), custom_call_target="tpu_custom_call" | custom-call | flops 2000000000 | bytes 10000000 | tf_op jit(solution)/shard_map/near_pairs/pallas_call | solution.py:393
  46.8 6.5 %collective-permute-done.1.left_hbm = bf16[1024,256]{1,0:T(8,128)(2,1)S(1)} collective-permute-done((bf16[1024,256]{1,0:T(8,128)(2,1)S(1)}, bf16[1024,256]{1,0:T(8,128)(2,1)S(1)}, u32[]{:S(2)}, u32[]{:S(2)}) %collective-permute-start.1) | collective-permute-done | bytes 524320 | tf_op jit(solution)/shard_map/ppermute | solution.py:486
  53.3 0.0 collective-permute-done.2.right_ref
  53.3 8.6 %far_pairs.1 = (f32[3,8,128]{2,1,0:T(8,128)S(1)}, f32[2,8,128]{2,1,0:T(8,128)S(1)}) custom-call(s32[11]{0:T(128)S(1)} %stack.47.s_ref, f32[16]{0:T(128)S(1)} %broadcast_select_fusion.keep_ref, bf16[1024,256]{1,0:T(8,128)(2,1)S(1)} %bitcast.22, bf16[1024,256]{1,0:T(8,128)(2,1)S(1)} %collective-permute-done.other_ref.other_hbm, ...), custom_call_target="tpu_custom_call" | custom-call | flops 4000000000 | bytes 10000000 | tf_op jit(solution)/shard_map/far_pairs/pallas_call | solution.py:409
  61.9 1.0 %collective-permute-start.3 = (f32[2,8,128]{2,1,0:T(8,128)S(1)}, f32[2,8,128]{2,1,0:T(8,128)S(1)}, u32[]{:S(2)}, u32[]{:S(2)}) collective-permute-start(f32[2,8,128]{2,1,0:T(8,128)S(1)} %get-tuple-element.26), channel_id=1, source_target_pairs={{0,4},{1,5},{2,6},{3,7},{4,0},{5,1},{6,2},{7,3},{8,12},{9,13},{10,... | collective-permute-start | bytes 24584 | tf_op jit(solution)/shard_map/ppermute | solution.py:486
  62.9 0.1 pad.1.clone
  63.0 0.8 collective-permute-done.3
  63.8 0.1 maximum_add_fusion
  63.8 3.6 %collective-permute-start.4 = (f32[3,8,128]{2,1,0:T(8,128)S(1)}, f32[3,8,128]{2,1,0:T(8,128)S(1)}, u32[]{:S(2)}, u32[]{:S(2)}) collective-permute-start(f32[3,8,128]{2,1,0:T(8,128)S(1)} %maximum_add_fusion), channel_id=1, source_target_pairs={{0,0},{1,1},{2,2},{3,3},{4,252},{5,253},{6,254},{7,255},{8,8},{9,9... | collective-permute-start | bytes 36872 | tf_op jit(solution)/shard_map/ppermute | solution.py:486
  67.4 4.2 %collective-permute-done.4.refs_0_ = f32[3,8,128]{2,1,0:T(8,128)S(1)} collective-permute-done((f32[3,8,128]{2,1,0:T(8,128)S(1)}, f32[3,8,128]{2,1,0:T(8,128)S(1)}, u32[]{:S(2)}, u32[]{:S(2)}) %collective-permute-start.4) | collective-permute-done | bytes 12320 | tf_op jit(solution)/shard_map/ppermute | solution.py:486
  71.6 1.3 %collective-permute-start.5 = (f32[3,8,128]{2,1,0:T(8,128)S(1)}, f32[3,8,128]{2,1,0:T(8,128)S(1)}, u32[]{:S(2)}, u32[]{:S(2)}) collective-permute-start(f32[3,8,128]{2,1,0:T(8,128)S(1)} %collective-permute-done.4.refs_0_), channel_id=1, source_target_pairs={{0,1},{1,2},{2,3},{3,0},{4,5},{5,6},{6,7},{7,4},{8,9},{9,10},{10,1... | collective-permute-start | bytes 36872 | tf_op jit(solution)/shard_map/ppermute | solution.py:486
  72.9 2.8 %collective-permute-start.6 = (f32[3,8,128]{2,1,0:T(8,128)S(1)}, f32[3,8,128]{2,1,0:T(8,128)S(1)}, u32[]{:S(2)}, u32[]{:S(2)}) collective-permute-start(f32[3,8,128]{2,1,0:T(8,128)S(1)} %collective-permute-done.4.refs_0_), channel_id=1, source_target_pairs={{0,2},{1,3},{2,0},{3,1},{4,6},{5,7},{6,4},{7,5},{8,10},{9,11},{10,... | collective-permute-start | bytes 36872 | tf_op jit(solution)/shard_map/ppermute | solution.py:486
  75.7 0.6 collective-permute-start.7
  76.3 0.0 collective-permute-done.5.refs_1_
  76.3 0.7 collective-permute-done.6.refs_2_
  77.0 1.3 %collective-permute-done.7.refs_3_ = f32[3,8,128]{2,1,0:T(8,128)S(1)} collective-permute-done((f32[3,8,128]{2,1,0:T(8,128)S(1)}, f32[3,8,128]{2,1,0:T(8,128)S(1)}, u32[]{:S(2)}, u32[]{:S(2)}) %collective-permute-start.7) | collective-permute-done | bytes 12320 | tf_op jit(solution)/shard_map/ppermute | solution.py:486
  78.2 1.0 %to_rank_order.1 = f32[32,128]{1,0:T(8,128)} custom-call(s32[32,128]{1,0:T(8,128)S(1)} %get-tuple-element.19.place_ref, f32[3,8,128]{2,1,0:T(8,128)S(1)} %collective-permute-done.4.refs_0_, f32[3,8,128]{2,1,0:T(8,128)S(1)} %collective-permute-done.5.refs_1_, f32[3,8,128]{2,1,0:T(8,128)S(1)} %collective-permute-done.6.refs_2_, ...), custom_call_target="tpu_custom_call" | custom-call | tf_op jit(solution)/shard_map/to_rank_order/pallas_call | solution.py:442
  (5 shorter events, 0.0 us)
Async XLA Ops:
  0.0 38.3 %copy-start = (s32[32,10]{0,1:T(8,128)S(1)}, s32[32,10]{0,1:T(8,128)}, u32[]{:S(2)}) copy-start(s32[32,10]{0,1:T(8,128)} %param.7) | copy-start | bytes 3844
  0.0 20.3 %copy-start.1 = (s32[262144]{0:T(1024)S(1)}, s32[262144]{0:T(1024)}, u32[]{:S(2)}) copy-start(s32[262144]{0:T(1024)} %param.5) | copy-start | bytes 3145732
  0.0 20.3 %copy-start.2 = (s32[262144]{0:T(1024)S(1)}, s32[262144]{0:T(1024)}, u32[]{:S(2)}) copy-start(s32[262144]{0:T(1024)} %param.6) | copy-start | bytes 3145732
  7.2 30.7 %all-to-all-start = ((bf16[64,16,256]{2,1,0:T(8,128)(2,1)}), bf16[64,16,256]{2,1,0:T(8,128)(2,1)S(1)}, u32[]{:S(2)}, u32[]{:S(2)}) async-start(bf16[64,16,256]{2,1,0:T(8,128)(2,1)} %bitcast.24), calls=%async_computation | async-start | bytes 1048576 | tf_op jit(solution)/shard_map/all_to_all | solution.py:489
  37.9 3.8 %collective-permute-start = (bf16[1024,256]{1,0:T(8,128)(2,1)S(1)}, bf16[1024,256]{1,0:T(8,128)(2,1)S(1)}, u32[]{:S(2)}, u32[]{:S(2)}) collective-permute-start(bf16[1024,256]{1,0:T(8,128)(2,1)S(1)} %bitcast.18), channel_id=1, source_target_pairs={{0,4},{1,5},{2,6},{3,7},{4,0},{5,1},{6,2},{7,3},{8,12},{9,13},{10,... | collective-permute-start | bytes 1572872 | tf_op jit(solution)/shard_map/ppermute | solution.py:486
  38.5 14.8 %collective-permute-start.1 = (bf16[1024,256]{1,0:T(8,128)(2,1)S(1)}, bf16[1024,256]{1,0:T(8,128)(2,1)S(1)}, u32[]{:S(2)}, u32[]{:S(2)}) collective-permute-start(bf16[1024,256]{1,0:T(8,128)(2,1)S(1)} %bitcast.19), channel_id=1, source_target_pairs={{0,1},{1,6},{2,7},{3,0},{4,5},{5,2},{6,3},{7,4},{8,9},{9,14},{10,1... | collective-permute-start | bytes 1572872 | tf_op jit(solution)/shard_map/ppermute | solution.py:486
  39.9 13.4 %collective-permute-start.2 = (bf16[1024,256]{1,0:T(8,128)(2,1)S(1)}, bf16[1024,256]{1,0:T(8,128)(2,1)S(1)}, u32[]{:S(2)}, u32[]{:S(2)}) collective-permute-start(bf16[1024,256]{1,0:T(8,128)(2,1)S(1)} %bitcast.20), channel_id=1, source_target_pairs={{0,3},{1,0},{2,1},{3,2},{4,7},{5,4},{6,5},{7,6},{8,11},{9,8},{10,9... | collective-permute-start | bytes 1572872 | tf_op jit(solution)/shard_map/ppermute | solution.py:486
  61.9 1.8 %collective-permute-start.3 = (f32[2,8,128]{2,1,0:T(8,128)S(1)}, f32[2,8,128]{2,1,0:T(8,128)S(1)}, u32[]{:S(2)}, u32[]{:S(2)}) collective-permute-start(f32[2,8,128]{2,1,0:T(8,128)S(1)} %get-tuple-element.26), channel_id=1, source_target_pairs={{0,4},{1,5},{2,6},{3,7},{4,0},{5,1},{6,2},{7,3},{8,12},{9,13},{10,... | collective-permute-start | bytes 24584 | tf_op jit(solution)/shard_map/ppermute | solution.py:486
  63.8 7.7 %collective-permute-start.4 = (f32[3,8,128]{2,1,0:T(8,128)S(1)}, f32[3,8,128]{2,1,0:T(8,128)S(1)}, u32[]{:S(2)}, u32[]{:S(2)}) collective-permute-start(f32[3,8,128]{2,1,0:T(8,128)S(1)} %maximum_add_fusion), channel_id=1, source_target_pairs={{0,0},{1,1},{2,2},{3,3},{4,252},{5,253},{6,254},{7,255},{8,8},{9,9... | collective-permute-start | bytes 36872 | tf_op jit(solution)/shard_map/ppermute | solution.py:486
  71.6 4.7 %collective-permute-start.5 = (f32[3,8,128]{2,1,0:T(8,128)S(1)}, f32[3,8,128]{2,1,0:T(8,128)S(1)}, u32[]{:S(2)}, u32[]{:S(2)}) collective-permute-start(f32[3,8,128]{2,1,0:T(8,128)S(1)} %collective-permute-done.4.refs_0_), channel_id=1, source_target_pairs={{0,1},{1,2},{2,3},{3,0},{4,5},{5,6},{6,7},{7,4},{8,9},{9,10},{10,1... | collective-permute-start | bytes 36872 | tf_op jit(solution)/shard_map/ppermute | solution.py:486
  72.9 4.0 %collective-permute-start.6 = (f32[3,8,128]{2,1,0:T(8,128)S(1)}, f32[3,8,128]{2,1,0:T(8,128)S(1)}, u32[]{:S(2)}, u32[]{:S(2)}) collective-permute-start(f32[3,8,128]{2,1,0:T(8,128)S(1)} %collective-permute-done.4.refs_0_), channel_id=1, source_target_pairs={{0,2},{1,3},{2,0},{3,1},{4,6},{5,7},{6,4},{7,5},{8,10},{9,11},{10,... | collective-permute-start | bytes 36872 | tf_op jit(solution)/shard_map/ppermute | solution.py:486
  75.7 2.5 %collective-permute-start.7 = (f32[3,8,128]{2,1,0:T(8,128)S(1)}, f32[3,8,128]{2,1,0:T(8,128)S(1)}, u32[]{:S(2)}, u32[]{:S(2)}) collective-permute-start(f32[3,8,128]{2,1,0:T(8,128)S(1)} %collective-permute-done.4.refs_0_), channel_id=1, source_target_pairs={{0,3},{1,0},{2,1},{3,2},{4,7},{5,4},{6,5},{7,6},{8,11},{9,8},{10,9... | collective-permute-start | bytes 36872 | tf_op jit(solution)/shard_map/ppermute | solution.py:486

commit v5 on v4

--- a/solution.py
+++ b/solution.py
@@ -19,7 +19,8 @@
 
 
 def block_band(device):
-    return device if device % 2 == 0 else 64 - device
+    host = device ^ 8
+    return host if host % 2 == 0 else 64 - host
 
 
 def smem():
@@ -455,7 +456,8 @@
     device = lax.axis_index("band").astype(jnp.int32)
     rep = lax.axis_index("rep").astype(jnp.int32)
     core = device & 1
-    own_band = jnp.where(core == 0, device, bands - device)
+    host = device ^ 8
+    own_band = jnp.where(core == 0, host, bands - host)
     other_band = bands - 1 - own_band
     own_offset = jnp.where(own_band < bands // 2, 0, 2)
     other_offset = 2 - own_offset

time: 79.8 us -> 78.5 us (0.984)
  starting transfers between devices: 25.8 us -> 24.6 us
    ppermute x8, starting transfers between devices: 12.8 us -> 11.6 us  [shift(): return lax.ppermute(value, ('band', 'rep'), joint(move))]
where the time goes in v5:
time: 78.5 us; the launch traced here: 78.3 us
  waiting for transfers between devices  27 us (34%)
  Pallas kernels  26.1 us (33%)
  starting transfers between devices  24.6 us (31%)
    ppermute x8, waiting for transfers between devices, shift(): return lax.ppermute(value, ('band', 'rep'), joint(move))  13.5 us
    all_to_all x1, waiting for transfers between devices, on_device(): lax.all_to_all(payload.reshape(bands, 16, 256), 'band', split_axis=0, con...  13.5 us
    all_to_all x1, starting transfers between devices, on_device(): lax.all_to_all(payload.reshape(bands, 16, 256), 'band', split_axis=0, con...  13 us
    ppermute x8, starting transfers between devices, shift(): return lax.ppermute(value, ('band', 'rep'), joint(move))  11.6 us
    pallas_call x1, Pallas kernels, far_pairs(): pl.pallas_call(far_kernel, out_shape=(jax.ShapeDtypeStruct((3, 8, LANES),...  8.63 us
    pallas_call x1, Pallas kernels, send_rows(): pl.pallas_call(send_kernel, out_shape=jax.ShapeDtypeStruct((1024, 256), j...  7.15 us
    pallas_call x1, Pallas kernels, near_pairs(): pl.pallas_call(near_kernel, out_shape=(jax.ShapeDtypeStruct((2, 8, LANES)...  5.16 us
    pallas_call x1, Pallas kernels, place(): pl.pallas_call(place_kernel, out_shape=(jax.ShapeDtypeStruct((2, 64, LANE...  4.12 us
  transfers between devices with their start and end apart: 9, of which 6 were waited for; matrix products, arithmetic and copies ran while one was open for 1% of the time, Pallas kernels for 12%

profile of v5, /device:TPU:1, one launch (start us, length us, event | category | flops | bytes accessed | tf_op | source)
XLA Modules:
  0.0 78.3 jit_solution(1825542604935828300)
XLA Ops:
  0.0 0.0 copy-start
  0.0 7.2 %send_rows.1 = bf16[1024,256]{1,0:T(8,128)(2,1)} custom-call(s32[2048,128]{1,0:T(8,128)} %bitcast.16, bf16[4096,256]{1,0:T(8,128)(2,1)} %points_hbm.1), custom_call_target="tpu_custom_call" | custom-call | tf_op jit(solution)/shard_map/send_rows/pallas_call | solution.py:94
  7.2 13.0 %all-to-all-start = ((bf16[64,16,256]{2,1,0:T(8,128)(2,1)}), bf16[64,16,256]{2,1,0:T(8,128)(2,1)S(1)}, u32[]{:S(2)}, u32[]{:S(2)}) async-start(bf16[64,16,256]{2,1,0:T(8,128)(2,1)} %bitcast.24), calls=%async_computation | async-start | bytes 1048576 | tf_op jit(solution)/shard_map/all_to_all | solution.py:491
  20.2 0.1 stack.47.s_ref
  20.3 0.0 copy-done.1
  20.3 0.0 copy-done.2
  20.3 4.1 %place.1 = (f32[2,64,128]{2,1,0:T(8,128)S(1)}, f32[2,128,64]{2,1,0:T(8,128)S(1)}, s32[32,128]{1,0:T(8,128)S(1)}) custom-call(s32[11]{0:T(128)S(1)} %stack.47.s_ref, s32[2048,128]{1,0:T(8,128)S(1)} %bitcast.17, s32[2048,128]{1,0:T(8,128)S(1)} %bitcast.23), custom_call_target="tpu_custom_call" | custom-call | flops 2000000000 | bytes 10000000 | tf_op jit(solution)/shard_map/place/pallas_call | solution.py:168
  24.4 13.5 %all-to-all-done = bf16[64,16,256]{2,1,0:T(8,128)(2,1)S(1)} async-done(((bf16[64,16,256]{2,1,0:T(8,128)(2,1)}), bf16[64,16,256]{2,1,0:T(8,128)(2,1)S(1)}, u32[]{:S(2)}, u32[]{:S(2)}) %all-to-all-start) | async-done | bytes 524320 | tf_op jit(solution)/shard_map/all_to_all | solution.py:491
  37.9 0.4 collective-permute-start
  38.3 0.0 copy-done
  38.3 0.2 dynamic-slice_reduce_fusion
  38.5 1.4 %collective-permute-start.1 = (bf16[1024,256]{1,0:T(8,128)(2,1)S(1)}, bf16[1024,256]{1,0:T(8,128)(2,1)S(1)}, u32[]{:S(2)}, u32[]{:S(2)}) collective-permute-start(bf16[1024,256]{1,0:T(8,128)(2,1)S(1)} %bitcast.19), channel_id=1, source_target_pairs={{0,1},{1,6},{2,7},{3,0},{4,5},{5,2},{6,3},{7,4},{8,9},{9,14},{10,1... | collective-permute-start | bytes 1572872 | tf_op jit(solution)/shard_map/ppermute | solution.py:488
  39.9 1.7 %collective-permute-start.2 = (bf16[1024,256]{1,0:T(8,128)(2,1)S(1)}, bf16[1024,256]{1,0:T(8,128)(2,1)S(1)}, u32[]{:S(2)}, u32[]{:S(2)}) collective-permute-start(bf16[1024,256]{1,0:T(8,128)(2,1)S(1)} %bitcast.20), channel_id=1, source_target_pairs={{0,3},{1,0},{2,1},{3,2},{4,7},{5,4},{6,5},{7,6},{8,11},{9,8},{10,9... | collective-permute-start | bytes 1572872 | tf_op jit(solution)/shard_map/ppermute | solution.py:488
  41.6 0.1 compare_reduce_fusion
  41.7 0.0 collective-permute-done.other_ref.other_hbm
  41.7 5.2 %near_pairs.1 = (f32[2,8,128]{2,1,0:T(8,128)S(1)}, f32[8,2048]{1,0:T(8,128)S(1)}) custom-call(s32[11]{0:T(128)S(1)} %stack.47.s_ref, f32[16]{0:T(128)S(1)} %broadcast_select_fusion.keep_ref, bf16[1024,256]{1,0:T(8,128)(2,1)S(1)} %bitcast.21, bf16[1024,256]{1,0:T(8,128)(2,1)S(1)} %collective-permute-done.other_ref.other_hbm, ...), custom_call_target="tpu_custom_call" | custom-call | flops 2000000000 | bytes 10000000 | tf_op jit(solution)/shard_map/near_pairs/pallas_call | solution.py:394
  46.8 6.5 %collective-permute-done.1.left_hbm = bf16[1024,256]{1,0:T(8,128)(2,1)S(1)} collective-permute-done((bf16[1024,256]{1,0:T(8,128)(2,1)S(1)}, bf16[1024,256]{1,0:T(8,128)(2,1)S(1)}, u32[]{:S(2)}, u32[]{:S(2)}) %collective-permute-start.1) | collective-permute-done | bytes 524320 | tf_op jit(solution)/shard_map/ppermute | solution.py:488
  53.3 0.0 collective-permute-done.2.right_ref
  53.3 8.6 %far_pairs.1 = (f32[3,8,128]{2,1,0:T(8,128)S(1)}, f32[2,8,128]{2,1,0:T(8,128)S(1)}) custom-call(s32[11]{0:T(128)S(1)} %stack.47.s_ref, f32[16]{0:T(128)S(1)} %broadcast_select_fusion.keep_ref, bf16[1024,256]{1,0:T(8,128)(2,1)S(1)} %bitcast.22, bf16[1024,256]{1,0:T(8,128)(2,1)S(1)} %collective-permute-done.other_ref.other_hbm, ...), custom_call_target="tpu_custom_call" | custom-call | flops 4000000000 | bytes 10000000 | tf_op jit(solution)/shard_map/far_pairs/pallas_call | solution.py:410
  61.9 1.0 %collective-permute-start.3 = (f32[2,8,128]{2,1,0:T(8,128)S(1)}, f32[2,8,128]{2,1,0:T(8,128)S(1)}, u32[]{:S(2)}, u32[]{:S(2)}) collective-permute-start(f32[2,8,128]{2,1,0:T(8,128)S(1)} %get-tuple-element.26), channel_id=1, source_target_pairs={{0,4},{1,5},{2,6},{3,7},{4,0},{5,1},{6,2},{7,3},{8,12},{9,13},{10,... | collective-permute-start | bytes 24584 | tf_op jit(solution)/shard_map/ppermute | solution.py:488
  62.9 0.1 pad.1.clone
  63.0 0.8 collective-permute-done.3
  63.8 0.1 maximum_add_fusion
  63.8 2.4 %collective-permute-start.4 = (f32[3,8,128]{2,1,0:T(8,128)S(1)}, f32[3,8,128]{2,1,0:T(8,128)S(1)}, u32[]{:S(2)}, u32[]{:S(2)}) collective-permute-start(f32[3,8,128]{2,1,0:T(8,128)S(1)} %maximum_add_fusion), channel_id=1, source_target_pairs={{0,32},{1,33},{2,34},{3,35},{4,220},{5,221},{6,222},{7,223},{8,40}... | collective-permute-start | bytes 36872 | tf_op jit(solution)/shard_map/ppermute | solution.py:488
  66.2 4.4 %collective-permute-done.4.refs_0_ = f32[3,8,128]{2,1,0:T(8,128)S(1)} collective-permute-done((f32[3,8,128]{2,1,0:T(8,128)S(1)}, f32[3,8,128]{2,1,0:T(8,128)S(1)}, u32[]{:S(2)}, u32[]{:S(2)}) %collective-permute-start.4) | collective-permute-done | bytes 12320 | tf_op jit(solution)/shard_map/ppermute | solution.py:488
  70.6 1.3 %collective-permute-start.5 = (f32[3,8,128]{2,1,0:T(8,128)S(1)}, f32[3,8,128]{2,1,0:T(8,128)S(1)}, u32[]{:S(2)}, u32[]{:S(2)}) collective-permute-start(f32[3,8,128]{2,1,0:T(8,128)S(1)} %collective-permute-done.4.refs_0_), channel_id=1, source_target_pairs={{0,1},{1,2},{2,3},{3,0},{4,5},{5,6},{6,7},{7,4},{8,9},{9,10},{10,1... | collective-permute-start | bytes 36872 | tf_op jit(solution)/shard_map/ppermute | solution.py:488
  71.9 2.8 %collective-permute-start.6 = (f32[3,8,128]{2,1,0:T(8,128)S(1)}, f32[3,8,128]{2,1,0:T(8,128)S(1)}, u32[]{:S(2)}, u32[]{:S(2)}) collective-permute-start(f32[3,8,128]{2,1,0:T(8,128)S(1)} %collective-permute-done.4.refs_0_), channel_id=1, source_target_pairs={{0,2},{1,3},{2,0},{3,1},{4,6},{5,7},{6,4},{7,5},{8,10},{9,11},{10,... | collective-permute-start | bytes 36872 | tf_op jit(solution)/shard_map/ppermute | solution.py:488
  74.7 0.6 collective-permute-start.7
  75.3 0.0 collective-permute-done.5.refs_1_
  75.3 0.7 collective-permute-done.6.refs_2_
  76.0 1.3 %collective-permute-done.7.refs_3_ = f32[3,8,128]{2,1,0:T(8,128)S(1)} collective-permute-done((f32[3,8,128]{2,1,0:T(8,128)S(1)}, f32[3,8,128]{2,1,0:T(8,128)S(1)}, u32[]{:S(2)}, u32[]{:S(2)}) %collective-permute-start.7) | collective-permute-done | bytes 12320 | tf_op jit(solution)/shard_map/ppermute | solution.py:488
  77.3 1.0 %to_rank_order.1 = f32[32,128]{1,0:T(8,128)} custom-call(s32[32,128]{1,0:T(8,128)S(1)} %get-tuple-element.19.place_ref, f32[3,8,128]{2,1,0:T(8,128)S(1)} %collective-permute-done.4.refs_0_, f32[3,8,128]{2,1,0:T(8,128)S(1)} %collective-permute-done.5.refs_1_, f32[3,8,128]{2,1,0:T(8,128)S(1)} %collective-permute-done.6.refs_2_, ...), custom_call_target="tpu_custom_call" | custom-call | tf_op jit(solution)/shard_map/to_rank_order/pallas_call | solution.py:443
  (5 shorter events, 0.0 us)
Async XLA Ops:
  0.0 38.3 %copy-start = (s32[32,10]{0,1:T(8,128)S(1)}, s32[32,10]{0,1:T(8,128)}, u32[]{:S(2)}) copy-start(s32[32,10]{0,1:T(8,128)} %param.7) | copy-start | bytes 3844
  0.0 20.3 %copy-start.1 = (s32[262144]{0:T(1024)S(1)}, s32[262144]{0:T(1024)}, u32[]{:S(2)}) copy-start(s32[262144]{0:T(1024)} %param.5) | copy-start | bytes 3145732
  0.0 20.3 %copy-start.2 = (s32[262144]{0:T(1024)S(1)}, s32[262144]{0:T(1024)}, u32[]{:S(2)}) copy-start(s32[262144]{0:T(1024)} %param.6) | copy-start | bytes 3145732
  7.2 30.7 %all-to-all-start = ((bf16[64,16,256]{2,1,0:T(8,128)(2,1)}), bf16[64,16,256]{2,1,0:T(8,128)(2,1)S(1)}, u32[]{:S(2)}, u32[]{:S(2)}) async-start(bf16[64,16,256]{2,1,0:T(8,128)(2,1)} %bitcast.24), calls=%async_computation | async-start | bytes 1048576 | tf_op jit(solution)/shard_map/all_to_all | solution.py:491
  37.9 3.8 %collective-permute-start = (bf16[1024,256]{1,0:T(8,128)(2,1)S(1)}, bf16[1024,256]{1,0:T(8,128)(2,1)S(1)}, u32[]{:S(2)}, u32[]{:S(2)}) collective-permute-start(bf16[1024,256]{1,0:T(8,128)(2,1)S(1)} %bitcast.18), channel_id=1, source_target_pairs={{0,4},{1,5},{2,6},{3,7},{4,0},{5,1},{6,2},{7,3},{8,12},{9,13},{10,... | collective-permute-start | bytes 1572872 | tf_op jit(solution)/shard_map/ppermute | solution.py:488
  38.5 14.8 %collective-permute-start.1 = (bf16[1024,256]{1,0:T(8,128)(2,1)S(1)}, bf16[1024,256]{1,0:T(8,128)(2,1)S(1)}, u32[]{:S(2)}, u32[]{:S(2)}) collective-permute-start(bf16[1024,256]{1,0:T(8,128)(2,1)S(1)} %bitcast.19), channel_id=1, source_target_pairs={{0,1},{1,6},{2,7},{3,0},{4,5},{5,2},{6,3},{7,4},{8,9},{9,14},{10,1... | collective-permute-start | bytes 1572872 | tf_op jit(solution)/shard_map/ppermute | solution.py:488
  39.9 13.4 %collective-permute-start.2 = (bf16[1024,256]{1,0:T(8,128)(2,1)S(1)}, bf16[1024,256]{1,0:T(8,128)(2,1)S(1)}, u32[]{:S(2)}, u32[]{:S(2)}) collective-permute-start(bf16[1024,256]{1,0:T(8,128)(2,1)S(1)} %bitcast.20), channel_id=1, source_target_pairs={{0,3},{1,0},{2,1},{3,2},{4,7},{5,4},{6,5},{7,6},{8,11},{9,8},{10,9... | collective-permute-start | bytes 1572872 | tf_op jit(solution)/shard_map/ppermute | solution.py:488
  61.9 1.8 %collective-permute-start.3 = (f32[2,8,128]{2,1,0:T(8,128)S(1)}, f32[2,8,128]{2,1,0:T(8,128)S(1)}, u32[]{:S(2)}, u32[]{:S(2)}) collective-permute-start(f32[2,8,128]{2,1,0:T(8,128)S(1)} %get-tuple-element.26), channel_id=1, source_target_pairs={{0,4},{1,5},{2,6},{3,7},{4,0},{5,1},{6,2},{7,3},{8,12},{9,13},{10,... | collective-permute-start | bytes 24584 | tf_op jit(solution)/shard_map/ppermute | solution.py:488
  63.8 6.8 %collective-permute-start.4 = (f32[3,8,128]{2,1,0:T(8,128)S(1)}, f32[3,8,128]{2,1,0:T(8,128)S(1)}, u32[]{:S(2)}, u32[]{:S(2)}) collective-permute-start(f32[3,8,128]{2,1,0:T(8,128)S(1)} %maximum_add_fusion), channel_id=1, source_target_pairs={{0,32},{1,33},{2,34},{3,35},{4,220},{5,221},{6,222},{7,223},{8,40}... | collective-permute-start | bytes 36872 | tf_op jit(solution)/shard_map/ppermute | solution.py:488
  70.6 4.7 %collective-permute-start.5 = (f32[3,8,128]{2,1,0:T(8,128)S(1)}, f32[3,8,128]{2,1,0:T(8,128)S(1)}, u32[]{:S(2)}, u32[]{:S(2)}) collective-permute-start(f32[3,8,128]{2,1,0:T(8,128)S(1)} %collective-permute-done.4.refs_0_), channel_id=1, source_target_pairs={{0,1},{1,2},{2,3},{3,0},{4,5},{5,6},{6,7},{7,4},{8,9},{9,10},{10,1... | collective-permute-start | bytes 36872 | tf_op jit(solution)/shard_map/ppermute | solution.py:488
  71.9 4.0 %collective-permute-start.6 = (f32[3,8,128]{2,1,0:T(8,128)S(1)}, f32[3,8,128]{2,1,0:T(8,128)S(1)}, u32[]{:S(2)}, u32[]{:S(2)}) collective-permute-start(f32[3,8,128]{2,1,0:T(8,128)S(1)} %collective-permute-done.4.refs_0_), channel_id=1, source_target_pairs={{0,2},{1,3},{2,0},{3,1},{4,6},{5,7},{6,4},{7,5},{8,10},{9,11},{10,... | collective-permute-start | bytes 36872 | tf_op jit(solution)/shard_map/ppermute | solution.py:488
  74.7 2.5 %collective-permute-start.7 = (f32[3,8,128]{2,1,0:T(8,128)S(1)}, f32[3,8,128]{2,1,0:T(8,128)S(1)}, u32[]{:S(2)}, u32[]{:S(2)}) collective-permute-start(f32[3,8,128]{2,1,0:T(8,128)S(1)} %collective-permute-done.4.refs_0_), channel_id=1, source_target_pairs={{0,3},{1,0},{2,1},{3,2},{4,7},{5,4},{6,5},{7,6},{8,11},{9,8},{10,9... | collective-permute-start | bytes 36872 | tf_op jit(solution)/shard_map/ppermute | solution.py:488

commit v6 on v5

--- a/solution.py
+++ b/solution.py
@@ -375,7 +375,7 @@
         move_ref[1, row, :] = jnp.where(cross == 0, 0.0, left[u])
 
 
-FAR_TILE = (512, 512)
+FAR_TILE = (1024, 256)
 
 
 def pair_scratch(columns, tile):

time: 78.5 us -> 77.4 us (0.986)
  Pallas kernels: 26.1 us -> 25 us
    pallas_call x1, Pallas kernels: 8.63 us -> 7.54 us  [far_pairs(): pl.pallas_call(far_kernel, out_shape=(jax.ShapeDtypeStruct((3, 8, LANES),...]
where the time goes in v6:
time: 77.4 us; the launch traced here: 77.2 us
  waiting for transfers between devices  27 us (35%)
  Pallas kernels  25 us (32%)
  starting transfers between devices  24.6 us (32%)
    ppermute x8, waiting for transfers between devices, shift(): return lax.ppermute(value, ('band', 'rep'), joint(move))  13.6 us
    all_to_all x1, waiting for transfers between devices, on_device(): lax.all_to_all(payload.reshape(bands, 16, 256), 'band', split_axis=0, con...  13.5 us
    all_to_all x1, starting transfers between devices, on_device(): lax.all_to_all(payload.reshape(bands, 16, 256), 'band', split_axis=0, con...  13 us
    ppermute x8, starting transfers between devices, shift(): return lax.ppermute(value, ('band', 'rep'), joint(move))  11.6 us
    pallas_call x1, Pallas kernels, far_pairs(): pl.pallas_call(far_kernel, out_shape=(jax.ShapeDtypeStruct((3, 8, LANES),...  7.54 us
    pallas_call x1, Pallas kernels, send_rows(): pl.pallas_call(send_kernel, out_shape=jax.ShapeDtypeStruct((1024, 256), j...  7.15 us
    pallas_call x1, Pallas kernels, near_pairs(): pl.pallas_call(near_kernel, out_shape=(jax.ShapeDtypeStruct((2, 8, LANES)...  5.16 us
    pallas_call x1, Pallas kernels, place(): pl.pallas_call(place_kernel, out_shape=(jax.ShapeDtypeStruct((2, 64, LANE...  4.12 us
  transfers between devices with their start and end apart: 9, of which 6 were waited for; matrix products, arithmetic and copies ran while one was open for 1% of the time, Pallas kernels for 12%

profile of v6, /device:TPU:1, one launch (start us, length us, event | category | flops | bytes accessed | tf_op | source)
XLA Modules:
  0.0 77.2 jit_solution(18218819906162759167)
XLA Ops:
  0.0 0.0 copy-start
  0.0 7.2 %send_rows.1 = bf16[1024,256]{1,0:T(8,128)(2,1)} custom-call(s32[2048,128]{1,0:T(8,128)} %bitcast.16, bf16[4096,256]{1,0:T(8,128)(2,1)} %points_hbm.1), custom_call_target="tpu_custom_call" | custom-call | tf_op jit(solution)/shard_map/send_rows/pallas_call | solution.py:94
  7.2 13.0 %all-to-all-start = ((bf16[64,16,256]{2,1,0:T(8,128)(2,1)}), bf16[64,16,256]{2,1,0:T(8,128)(2,1)S(1)}, u32[]{:S(2)}, u32[]{:S(2)}) async-start(bf16[64,16,256]{2,1,0:T(8,128)(2,1)} %bitcast.24), calls=%async_computation | async-start | bytes 1048576 | tf_op jit(solution)/shard_map/all_to_all | solution.py:491
  20.2 0.1 stack.47.s_ref
  20.3 0.0 copy-done.1
  20.3 0.0 copy-done.2
  20.3 4.1 %place.1 = (f32[2,64,128]{2,1,0:T(8,128)S(1)}, f32[2,128,64]{2,1,0:T(8,128)S(1)}, s32[32,128]{1,0:T(8,128)S(1)}) custom-call(s32[11]{0:T(128)S(1)} %stack.47.s_ref, s32[2048,128]{1,0:T(8,128)S(1)} %bitcast.17, s32[2048,128]{1,0:T(8,128)S(1)} %bitcast.23), custom_call_target="tpu_custom_call" | custom-call | flops 2000000000 | bytes 10000000 | tf_op jit(solution)/shard_map/place/pallas_call | solution.py:168
  24.4 13.5 %all-to-all-done = bf16[64,16,256]{2,1,0:T(8,128)(2,1)S(1)} async-done(((bf16[64,16,256]{2,1,0:T(8,128)(2,1)}), bf16[64,16,256]{2,1,0:T(8,128)(2,1)S(1)}, u32[]{:S(2)}, u32[]{:S(2)}) %all-to-all-start) | async-done | bytes 524320 | tf_op jit(solution)/shard_map/all_to_all | solution.py:491
  37.9 0.4 collective-permute-start
  38.3 0.0 copy-done
  38.3 0.2 dynamic-slice_reduce_fusion
  38.5 1.4 %collective-permute-start.1 = (bf16[1024,256]{1,0:T(8,128)(2,1)S(1)}, bf16[1024,256]{1,0:T(8,128)(2,1)S(1)}, u32[]{:S(2)}, u32[]{:S(2)}) collective-permute-start(bf16[1024,256]{1,0:T(8,128)(2,1)S(1)} %bitcast.19), channel_id=1, source_target_pairs={{0,1},{1,6},{2,7},{3,0},{4,5},{5,2},{6,3},{7,4},{8,9},{9,14},{10,1... | collective-permute-start | bytes 1572872 | tf_op jit(solution)/shard_map/ppermute | solution.py:488
  39.9 1.7 %collective-permute-start.2 = (bf16[1024,256]{1,0:T(8,128)(2,1)S(1)}, bf16[1024,256]{1,0:T(8,128)(2,1)S(1)}, u32[]{:S(2)}, u32[]{:S(2)}) collective-permute-start(bf16[1024,256]{1,0:T(8,128)(2,1)S(1)} %bitcast.20), channel_id=1, source_target_pairs={{0,3},{1,0},{2,1},{3,2},{4,7},{5,4},{6,5},{7,6},{8,11},{9,8},{10,9... | collective-permute-start | bytes 1572872 | tf_op jit(solution)/shard_map/ppermute | solution.py:488
  41.6 0.1 compare_reduce_fusion
  41.7 0.0 collective-permute-done.other_ref.other_hbm
  41.7 5.2 %near_pairs.1 = (f32[2,8,128]{2,1,0:T(8,128)S(1)}, f32[8,2048]{1,0:T(8,128)S(1)}) custom-call(s32[11]{0:T(128)S(1)} %stack.47.s_ref, f32[16]{0:T(128)S(1)} %broadcast_select_fusion.keep_ref, bf16[1024,256]{1,0:T(8,128)(2,1)S(1)} %bitcast.21, bf16[1024,256]{1,0:T(8,128)(2,1)S(1)} %collective-permute-done.other_ref.other_hbm, ...), custom_call_target="tpu_custom_call" | custom-call | flops 2000000000 | bytes 10000000 | tf_op jit(solution)/shard_map/near_pairs/pallas_call | solution.py:394
  46.8 6.5 %collective-permute-done.1.left_hbm = bf16[1024,256]{1,0:T(8,128)(2,1)S(1)} collective-permute-done((bf16[1024,256]{1,0:T(8,128)(2,1)S(1)}, bf16[1024,256]{1,0:T(8,128)(2,1)S(1)}, u32[]{:S(2)}, u32[]{:S(2)}) %collective-permute-start.1) | collective-permute-done | bytes 524320 | tf_op jit(solution)/shard_map/ppermute | solution.py:488
  53.3 0.0 collective-permute-done.2.right_ref
  53.3 7.5 %far_pairs.1 = (f32[3,8,128]{2,1,0:T(8,128)S(1)}, f32[2,8,128]{2,1,0:T(8,128)S(1)}) custom-call(s32[11]{0:T(128)S(1)} %stack.47.s_ref, f32[16]{0:T(128)S(1)} %broadcast_select_fusion.keep_ref, bf16[1024,256]{1,0:T(8,128)(2,1)S(1)} %bitcast.22, bf16[1024,256]{1,0:T(8,128)(2,1)S(1)} %collective-permute-done.other_ref.other_hbm, ...), custom_call_target="tpu_custom_call" | custom-call | flops 4000000000 | bytes 10000000 | tf_op jit(solution)/shard_map/far_pairs/pallas_call | solution.py:410
  60.9 1.0 %collective-permute-start.3 = (f32[2,8,128]{2,1,0:T(8,128)S(1)}, f32[2,8,128]{2,1,0:T(8,128)S(1)}, u32[]{:S(2)}, u32[]{:S(2)}) collective-permute-start(f32[2,8,128]{2,1,0:T(8,128)S(1)} %get-tuple-element.26), channel_id=1, source_target_pairs={{0,4},{1,5},{2,6},{3,7},{4,0},{5,1},{6,2},{7,3},{8,12},{9,13},{10,... | collective-permute-start | bytes 24584 | tf_op jit(solution)/shard_map/ppermute | solution.py:488
  61.8 0.1 pad.1.clone
  61.9 0.8 collective-permute-done.3
  62.7 0.1 maximum_add_fusion
  62.7 2.4 %collective-permute-start.4 = (f32[3,8,128]{2,1,0:T(8,128)S(1)}, f32[3,8,128]{2,1,0:T(8,128)S(1)}, u32[]{:S(2)}, u32[]{:S(2)}) collective-permute-start(f32[3,8,128]{2,1,0:T(8,128)S(1)} %maximum_add_fusion), channel_id=1, source_target_pairs={{0,32},{1,33},{2,34},{3,35},{4,220},{5,221},{6,222},{7,223},{8,40}... | collective-permute-start | bytes 36872 | tf_op jit(solution)/shard_map/ppermute | solution.py:488
  65.1 4.4 %collective-permute-done.4.refs_0_ = f32[3,8,128]{2,1,0:T(8,128)S(1)} collective-permute-done((f32[3,8,128]{2,1,0:T(8,128)S(1)}, f32[3,8,128]{2,1,0:T(8,128)S(1)}, u32[]{:S(2)}, u32[]{:S(2)}) %collective-permute-start.4) | collective-permute-done | bytes 12320 | tf_op jit(solution)/shard_map/ppermute | solution.py:488
  69.5 1.3 %collective-permute-start.5 = (f32[3,8,128]{2,1,0:T(8,128)S(1)}, f32[3,8,128]{2,1,0:T(8,128)S(1)}, u32[]{:S(2)}, u32[]{:S(2)}) collective-permute-start(f32[3,8,128]{2,1,0:T(8,128)S(1)} %collective-permute-done.4.refs_0_), channel_id=1, source_target_pairs={{0,1},{1,2},{2,3},{3,0},{4,5},{5,6},{6,7},{7,4},{8,9},{9,10},{10,1... | collective-permute-start | bytes 36872 | tf_op jit(solution)/shard_map/ppermute | solution.py:488
  70.9 2.8 %collective-permute-start.6 = (f32[3,8,128]{2,1,0:T(8,128)S(1)}, f32[3,8,128]{2,1,0:T(8,128)S(1)}, u32[]{:S(2)}, u32[]{:S(2)}) collective-permute-start(f32[3,8,128]{2,1,0:T(8,128)S(1)} %collective-permute-done.4.refs_0_), channel_id=1, source_target_pairs={{0,2},{1,3},{2,0},{3,1},{4,6},{5,7},{6,4},{7,5},{8,10},{9,11},{10,... | collective-permute-start | bytes 36872 | tf_op jit(solution)/shard_map/ppermute | solution.py:488
  73.6 0.6 collective-permute-start.7
  74.3 0.0 collective-permute-done.5.refs_1_
  74.3 0.7 collective-permute-done.6.refs_2_
  74.9 1.3 %collective-permute-done.7.refs_3_ = f32[3,8,128]{2,1,0:T(8,128)S(1)} collective-permute-done((f32[3,8,128]{2,1,0:T(8,128)S(1)}, f32[3,8,128]{2,1,0:T(8,128)S(1)}, u32[]{:S(2)}, u32[]{:S(2)}) %collective-permute-start.7) | collective-permute-done | bytes 12320 | tf_op jit(solution)/shard_map/ppermute | solution.py:488
  76.2 1.0 %to_rank_order.1 = f32[32,128]{1,0:T(8,128)} custom-call(s32[32,128]{1,0:T(8,128)S(1)} %get-tuple-element.19.place_ref, f32[3,8,128]{2,1,0:T(8,128)S(1)} %collective-permute-done.4.refs_0_, f32[3,8,128]{2,1,0:T(8,128)S(1)} %collective-permute-done.5.refs_1_, f32[3,8,128]{2,1,0:T(8,128)S(1)} %collective-permute-done.6.refs_2_, ...), custom_call_target="tpu_custom_call" | custom-call | tf_op jit(solution)/shard_map/to_rank_order/pallas_call | solution.py:443
  (5 shorter events, 0.0 us)
Async XLA Ops:
  0.0 38.3 %copy-start = (s32[32,10]{0,1:T(8,128)S(1)}, s32[32,10]{0,1:T(8,128)}, u32[]{:S(2)}) copy-start(s32[32,10]{0,1:T(8,128)} %param.7) | copy-start | bytes 3844
  0.0 20.3 %copy-start.1 = (s32[262144]{0:T(1024)S(1)}, s32[262144]{0:T(1024)}, u32[]{:S(2)}) copy-start(s32[262144]{0:T(1024)} %param.5) | copy-start | bytes 3145732
  0.0 20.3 %copy-start.2 = (s32[262144]{0:T(1024)S(1)}, s32[262144]{0:T(1024)}, u32[]{:S(2)}) copy-start(s32[262144]{0:T(1024)} %param.6) | copy-start | bytes 3145732
  7.2 30.7 %all-to-all-start = ((bf16[64,16,256]{2,1,0:T(8,128)(2,1)}), bf16[64,16,256]{2,1,0:T(8,128)(2,1)S(1)}, u32[]{:S(2)}, u32[]{:S(2)}) async-start(bf16[64,16,256]{2,1,0:T(8,128)(2,1)} %bitcast.24), calls=%async_computation | async-start | bytes 1048576 | tf_op jit(solution)/shard_map/all_to_all | solution.py:491
  37.9 3.8 %collective-permute-start = (bf16[1024,256]{1,0:T(8,128)(2,1)S(1)}, bf16[1024,256]{1,0:T(8,128)(2,1)S(1)}, u32[]{:S(2)}, u32[]{:S(2)}) collective-permute-start(bf16[1024,256]{1,0:T(8,128)(2,1)S(1)} %bitcast.18), channel_id=1, source_target_pairs={{0,4},{1,5},{2,6},{3,7},{4,0},{5,1},{6,2},{7,3},{8,12},{9,13},{10,... | collective-permute-start | bytes 1572872 | tf_op jit(solution)/shard_map/ppermute | solution.py:488
  38.5 14.8 %collective-permute-start.1 = (bf16[1024,256]{1,0:T(8,128)(2,1)S(1)}, bf16[1024,256]{1,0:T(8,128)(2,1)S(1)}, u32[]{:S(2)}, u32[]{:S(2)}) collective-permute-start(bf16[1024,256]{1,0:T(8,128)(2,1)S(1)} %bitcast.19), channel_id=1, source_target_pairs={{0,1},{1,6},{2,7},{3,0},{4,5},{5,2},{6,3},{7,4},{8,9},{9,14},{10,1... | collective-permute-start | bytes 1572872 | tf_op jit(solution)/shard_map/ppermute | solution.py:488
  39.9 13.4 %collective-permute-start.2 = (bf16[1024,256]{1,0:T(8,128)(2,1)S(1)}, bf16[1024,256]{1,0:T(8,128)(2,1)S(1)}, u32[]{:S(2)}, u32[]{:S(2)}) collective-permute-start(bf16[1024,256]{1,0:T(8,128)(2,1)S(1)} %bitcast.20), channel_id=1, source_target_pairs={{0,3},{1,0},{2,1},{3,2},{4,7},{5,4},{6,5},{7,6},{8,11},{9,8},{10,9... | collective-permute-start | bytes 1572872 | tf_op jit(solution)/shard_map/ppermute | solution.py:488
  60.9 1.8 %collective-permute-start.3 = (f32[2,8,128]{2,1,0:T(8,128)S(1)}, f32[2,8,128]{2,1,0:T(8,128)S(1)}, u32[]{:S(2)}, u32[]{:S(2)}) collective-permute-start(f32[2,8,128]{2,1,0:T(8,128)S(1)} %get-tuple-element.26), channel_id=1, source_target_pairs={{0,4},{1,5},{2,6},{3,7},{4,0},{5,1},{6,2},{7,3},{8,12},{9,13},{10,... | collective-permute-start | bytes 24584 | tf_op jit(solution)/shard_map/ppermute | solution.py:488
  62.7 6.8 %collective-permute-start.4 = (f32[3,8,128]{2,1,0:T(8,128)S(1)}, f32[3,8,128]{2,1,0:T(8,128)S(1)}, u32[]{:S(2)}, u32[]{:S(2)}) collective-permute-start(f32[3,8,128]{2,1,0:T(8,128)S(1)} %maximum_add_fusion), channel_id=1, source_target_pairs={{0,32},{1,33},{2,34},{3,35},{4,220},{5,221},{6,222},{7,223},{8,40}... | collective-permute-start | bytes 36872 | tf_op jit(solution)/shard_map/ppermute | solution.py:488
  69.5 4.7 %collective-permute-start.5 = (f32[3,8,128]{2,1,0:T(8,128)S(1)}, f32[3,8,128]{2,1,0:T(8,128)S(1)}, u32[]{:S(2)}, u32[]{:S(2)}) collective-permute-start(f32[3,8,128]{2,1,0:T(8,128)S(1)} %collective-permute-done.4.refs_0_), channel_id=1, source_target_pairs={{0,1},{1,2},{2,3},{3,0},{4,5},{5,6},{6,7},{7,4},{8,9},{9,10},{10,1... | collective-permute-start | bytes 36872 | tf_op jit(solution)/shard_map/ppermute | solution.py:488
  70.9 4.0 %collective-permute-start.6 = (f32[3,8,128]{2,1,0:T(8,128)S(1)}, f32[3,8,128]{2,1,0:T(8,128)S(1)}, u32[]{:S(2)}, u32[]{:S(2)}) collective-permute-start(f32[3,8,128]{2,1,0:T(8,128)S(1)} %collective-permute-done.4.refs_0_), channel_id=1, source_target_pairs={{0,2},{1,3},{2,0},{3,1},{4,6},{5,7},{6,4},{7,5},{8,10},{9,11},{10,... | collective-permute-start | bytes 36872 | tf_op jit(solution)/shard_map/ppermute | solution.py:488
  73.6 2.5 %collective-permute-start.7 = (f32[3,8,128]{2,1,0:T(8,128)S(1)}, f32[3,8,128]{2,1,0:T(8,128)S(1)}, u32[]{:S(2)}, u32[]{:S(2)}) collective-permute-start(f32[3,8,128]{2,1,0:T(8,128)S(1)} %collective-permute-done.4.refs_0_), channel_id=1, source_target_pairs={{0,3},{1,0},{2,1},{3,2},{4,7},{5,4},{6,5},{7,6},{8,11},{9,8},{10,9... | collective-permute-start | bytes 36872 | tf_op jit(solution)/shard_map/ppermute | solution.py:488

commit v7 on v6

--- a/solution.py
+++ b/solution.py
@@ -320,59 +320,77 @@
         out_ref[1, u : u + 1, :] = other[u]
 
 
-def far_kernel(s_ref, keep_ref, own_hbm, other_hbm, left_hbm, right_ref, row_ref, col_ref, near_ref,
-               inverse_ref, stay_ref, move_ref, block_ref, left_meta, right_meta, keep, prod_a,
-               prod_b, row_sum, col_sum, sems):
+def right_pairs(s_ref, keep_ref, sources, columns, right_ref, row_ref, col_ref, inverse_ref, block_ref,
+                left_meta, right_meta, keep, prod_a, prod_b, row_sum, col_sum, sems):
     own_offset = s_ref[7]
-    other_offset = s_ref[8]
-    cross = s_ref[9]
-    left_offset = s_ref[10]
     copies = [
         pltpu.make_async_copy(source, block_ref.at[pl.ds(i * 1024, 1024), :], sems.at[i])
-        for i, source in enumerate((own_hbm, other_hbm, left_hbm))
+        for i, source in enumerate(sources)
     ]
     for copy in copies:
         copy.start()
     left_meta[0] = inverse_column(square_sums(right_ref[...]))
     load_column_meta(col_ref, 0, 1, left_meta)
-    load_row_meta(0, row_ref, 0, 0, keep_ref, own_offset, own_offset, right_meta, keep)
-    load_row_meta(1024, row_ref, 1, 0, keep_ref, own_offset, other_offset, right_meta, keep)
-    load_row_meta(2048, row_ref, cross, 3, keep_ref, own_offset, left_offset, right_meta, keep)
-    right_meta[0, :, 0:2048] = inverse_ref[...]
+    for i, (band, quarter, offset, known) in enumerate(columns):
+        load_row_meta(i * 1024, row_ref, band, quarter, keep_ref, own_offset, offset, right_meta, keep)
+        if known is not None:
+            right_meta[0, :, i * 1024 : (i + 1) * 1024] = inverse_ref[:, known * 1024 : (known + 1) * 1024]
     row_sum[...] = jnp.zeros_like(row_sum)
     col_sum[...] = jnp.zeros_like(col_sum)
     for copy in copies:
         copy.wait()
-    right_meta[0, :, 2048:3072] = inverse_row(square_sums(block_ref[2048:3072, :]))
-    rows, cols = prod_a.shape
-    steps = 1024 // rows
-    total = steps * (3072 // cols)
+    for i, column in enumerate(columns):
+        if column[3] is None:
+            at = slice(i * 1024, (i + 1) * 1024)
+            right_meta[0, :, at] = inverse_row(square_sums(block_ref[at, :]))
+    cols = prod_a.shape[1]
+    total = len(columns) * 1024 // cols
     product(right_ref, 0, block_ref, 0, prod_a)
-
-    def place_of(t):
-        return pl.multiple_of((t % steps) * rows, rows), pl.multiple_of((t // steps) * cols, cols)
 
     @pl.loop(0, total // 2)
     def _(i):
-        left_a, right_a = place_of(i * 2)
-        left_b, right_b = place_of(i * 2 + 1)
-        left_c, right_c = place_of(jnp.minimum(i * 2 + 2, total - 1))
-        product(right_ref, left_b, block_ref, right_b, prod_b)
-        weigh(prod_a, left_a, left_meta, right_a, right_meta, keep, row_sum, col_sum, False)
-        product(right_ref, left_c, block_ref, right_c, prod_a)
-        weigh(prod_b, left_b, left_meta, right_b, right_meta, keep, row_sum, col_sum, False)
-
+        at_a = pl.multiple_of(i * 2 * cols, cols)
+        at_b = pl.multiple_of((i * 2 + 1) * cols, cols)
+        at_c = pl.multiple_of(jnp.minimum(i * 2 + 2, total - 1) * cols, cols)
+        product(right_ref, 0, block_ref, at_b, prod_b)
+        weigh(prod_a, 0, left_meta, at_a, right_meta, keep, row_sum, col_sum, False)
+        product(right_ref, 0, block_ref, at_c, prod_a)
+        weigh(prod_b, 0, left_meta, at_b, right_meta, keep, row_sum, col_sum, False)
+
+
+def guest_kernel(s_ref, keep_ref, other_hbm, left_hbm, right_ref, row_ref, col_ref, near_ref,
+                 inverse_ref, stay_ref, move_ref, *scratch):
+    cross = s_ref[9]
+    right_pairs(
+        s_ref, keep_ref, (other_hbm, left_hbm), ((1, 0, s_ref[8], 1), (cross, 3, s_ref[10], None)),
+        right_ref, row_ref, col_ref, inverse_ref, *scratch,
+    )
+    row_sum, col_sum = scratch[6:8]
+    right = rows_to_lanes(row_sum)
+    other = cols_to_lanes(col_sum, 0)
+    left = cols_to_lanes(col_sum, 1024)
+    for u in range(8):
+        row = slice(u, u + 1)
+        stay_ref[0, row, :] = right[u]
+        stay_ref[1, row, :] = jnp.where(cross == 0, left[u], 0.0)
+        move_ref[0, row, :] = other[u] + near_ref[1, row, :]
+        move_ref[1, row, :] = jnp.where(cross == 0, 0.0, left[u])
+
+
+def own_kernel(s_ref, keep_ref, own_hbm, right_ref, row_ref, col_ref, near_ref, inverse_ref,
+               guest_ref, stay_ref, *scratch):
+    right_pairs(
+        s_ref, keep_ref, (own_hbm,), ((0, 0, s_ref[7], 0),),
+        right_ref, row_ref, col_ref, inverse_ref, *scratch,
+    )
+    row_sum, col_sum = scratch[6:8]
     right = rows_to_lanes(row_sum)
     own = cols_to_lanes(col_sum, 0)
-    other = cols_to_lanes(col_sum, 1024)
-    left = cols_to_lanes(col_sum, 2048)
     for u in range(8):
         row = slice(u, u + 1)
         stay_ref[0, row, :] = own[u] + near_ref[0, row, :]
-        stay_ref[1, row, :] = right[u]
-        stay_ref[2, row, :] = jnp.where(cross == 0, left[u], 0.0)
-        move_ref[0, row, :] = other[u] + near_ref[1, row, :]
-        move_ref[1, row, :] = jnp.where(cross == 0, 0.0, left[u])
+        stay_ref[1, row, :] = right[u] + guest_ref[0, row, :]
+        stay_ref[2, row, :] = guest_ref[1, row, :]
 
 
 FAR_TILE = (1024, 256)
@@ -406,22 +424,41 @@
     )(scalars, keep, own, other, rows, cols)
 
 
-def far_pairs(scalars, keep, own, other, left, right, rows, cols, near):
+def far_scratch(blocks):
+    return (
+        [pltpu.VMEM((blocks * 1024, 256), jnp.bfloat16)]
+        + pair_scratch(blocks * 1024, FAR_TILE)
+        + [pltpu.SemaphoreType.DMA((blocks,))]
+    )
+
+
+def guest_pairs(scalars, keep, other, left, right, rows, cols, near):
     return pl.pallas_call(
-        far_kernel,
+        guest_kernel,
         out_shape=(
-            jax.ShapeDtypeStruct((3, 8, LANES), jnp.float32),
+            jax.ShapeDtypeStruct((2, 8, LANES), jnp.float32),
             jax.ShapeDtypeStruct((2, 8, LANES), jnp.float32),
         ),
-        in_specs=[smem(), smem(), hbm(), hbm(), hbm()] + [vmem()] * 5,
+        in_specs=[smem(), smem(), hbm(), hbm()] + [vmem()] * 5,
         out_specs=(vmem(), vmem()),
-        scratch_shapes=[pltpu.VMEM((3072, 256), jnp.bfloat16)]
-        + pair_scratch(3072, FAR_TILE)
-        + [pltpu.SemaphoreType.DMA((3,))],
+        scratch_shapes=far_scratch(2),
         compiler_params=pltpu.CompilerParams(vmem_limit_bytes=VMEM),
-        cost_estimate=pl.CostEstimate(flops=4 * 10**9, bytes_accessed=10**7, transcendentals=0),
-        name="far_pairs",
-    )(scalars, keep, own, other, left, right, rows, cols, *near)
+        cost_estimate=pl.CostEstimate(flops=3 * 10**9, bytes_accessed=10**7, transcendentals=0),
+        name="guest_pairs",
+    )(scalars, keep, other, left, right, rows, cols, *near)
+
+
+def own_pairs(scalars, keep, own, right, rows, cols, near, guests):
+    return pl.pallas_call(
+        own_kernel,
+        out_shape=jax.ShapeDtypeStruct((3, 8, LANES), jnp.float32),
+        in_specs=[smem(), smem(), hbm()] + [vmem()] * 6,
+        out_specs=vmem(),
+        scratch_shapes=far_scratch(1),
+        compiler_params=pltpu.CompilerParams(vmem_limit_bytes=VMEM),
+        cost_estimate=pl.CostEstimate(flops=2 * 10**9, bytes_accessed=10**7, transcendentals=0),
+        name="own_pairs",
+    )(scalars, keep, own, right, rows, cols, *near, guests)
 
 
 def rank_kernel(place_ref, *refs):
@@ -502,8 +539,9 @@
     left = shift(own, to_right)
 
     near = near_pairs(scalars, keep, own, other, rows, cols)
-    stay, move = far_pairs(scalars, keep, own, other, left, right, rows, cols, near)
+    guests, move = guest_pairs(scalars, keep, other, left, right, rows, cols, near)
     moved = shift(move, lambda d, r: (d ^ 1, r))
+    stay = own_pairs(scalars, keep, own, right, rows, cols, near, guests)
     sums = stay + jnp.stack([moved[0], jnp.zeros_like(moved[0]), moved[1]])
     home = shift(sums, lambda d, r: (block_band(d), r))
     pieces = [home] + [

time: 77.4 us -> 78.9 us (1.019)
  starting transfers between devices: 24.6 us -> 22.6 us
  Pallas kernels: 25 us -> 26.8 us
  waiting for transfers between devices: 27 us -> 28.7 us
    ppermute x8, starting transfers between devices: 11.6 us -> 9.63 us  [shift(): return lax.ppermute(value, ('band', 'rep'), joint(move))]
    pallas_call x1 -> x2, Pallas kernels: 7.54 us -> 9.35 us  [the longest x1 5.68 us: guest_pairs(): pl.pallas_call(guest_kernel, out_shape=(jax.ShapeDtypeStruct((2, 8, LANES...]
    ppermute x8, waiting for transfers between devices: 13.6 us -> 15.2 us  [shift(): return lax.ppermute(value, ('band', 'rep'), joint(move))]
  transfers between devices with their start and end apart: 9 -> 9, of which waited for: 6 -> 7; matrix products, arithmetic and copies ran while one was open for 1% -> 1% of each run, Pallas kernels for 12% -> 16%
where the time goes in v7:
time: 78.9 us; the launch traced here: 78.8 us
  waiting for transfers between devices  28.7 us (36%)
  Pallas kernels  26.8 us (34%)
  starting transfers between devices  22.6 us (29%)
    ppermute x8, waiting for transfers between devices, shift(): return lax.ppermute(value, ('band', 'rep'), joint(move))  15.2 us
    all_to_all x1, waiting for transfers between devices, on_device(): lax.all_to_all(payload.reshape(bands, 16, 256), 'band', split_axis=0, con...  13.5 us
    all_to_all x1, starting transfers between devices, on_device(): lax.all_to_all(payload.reshape(bands, 16, 256), 'band', split_axis=0, con...  13 us
    ppermute x8, starting transfers between devices, shift(): return lax.ppermute(value, ('band', 'rep'), joint(move))  9.63 us
    pallas_call x1, Pallas kernels, send_rows(): pl.pallas_call(send_kernel, out_shape=jax.ShapeDtypeStruct((1024, 256), j...  7.15 us
    pallas_call x1, Pallas kernels, guest_pairs(): pl.pallas_call(guest_kernel, out_shape=(jax.ShapeDtypeStruct((2, 8, LANES...  5.68 us
    pallas_call x1, Pallas kernels, near_pairs(): pl.pallas_call(near_kernel, out_shape=(jax.ShapeDtypeStruct((2, 8, LANES)...  5.15 us
    pallas_call x1, Pallas kernels, place(): pl.pallas_call(place_kernel, out_shape=(jax.ShapeDtypeStruct((2, 64, LANE...  4.12 us
  transfers between devices with their start and end apart: 9, of which 7 were waited for; matrix products, arithmetic and copies ran while one was open for 1% of the time, Pallas kernels for 16%

profile of v7, /device:TPU:1, one launch (start us, length us, event | category | flops | bytes accessed | tf_op | source)
XLA Modules:
  0.0 78.8 jit_solution(6878602831815180499)
XLA Ops:
  0.0 0.0 copy-start
  0.0 7.2 %send_rows.1 = bf16[1024,256]{1,0:T(8,128)(2,1)} custom-call(s32[2048,128]{1,0:T(8,128)} %bitcast.16, bf16[4096,256]{1,0:T(8,128)(2,1)} %points_hbm.1), custom_call_target="tpu_custom_call" | custom-call | tf_op jit(solution)/shard_map/send_rows/pallas_call | solution.py:94
  7.2 13.0 %all-to-all-start = ((bf16[64,16,256]{2,1,0:T(8,128)(2,1)}), bf16[64,16,256]{2,1,0:T(8,128)(2,1)S(1)}, u32[]{:S(2)}, u32[]{:S(2)}) async-start(bf16[64,16,256]{2,1,0:T(8,128)(2,1)} %bitcast.24), calls=%async_computation | async-start | bytes 1048576 | tf_op jit(solution)/shard_map/all_to_all | solution.py:528
  20.2 0.1 stack.47.s_ref
  20.3 0.0 copy-done.2
  20.3 4.1 %place.1 = (f32[2,64,128]{2,1,0:T(8,128)S(1)}, f32[2,128,64]{2,1,0:T(8,128)S(1)}, s32[32,128]{1,0:T(8,128)S(1)}) custom-call(s32[11]{0:T(128)S(1)} %stack.47.s_ref, s32[2048,128]{1,0:T(8,128)S(1)} %bitcast.17, s32[2048,128]{1,0:T(8,128)S(1)} %bitcast.23), custom_call_target="tpu_custom_call" | custom-call | flops 2000000000 | bytes 10000000 | tf_op jit(solution)/shard_map/place/pallas_call | solution.py:168
  24.4 13.5 %all-to-all-done = bf16[64,16,256]{2,1,0:T(8,128)(2,1)S(1)} async-done(((bf16[64,16,256]{2,1,0:T(8,128)(2,1)}), bf16[64,16,256]{2,1,0:T(8,128)(2,1)S(1)}, u32[]{:S(2)}, u32[]{:S(2)}) %all-to-all-start) | async-done | bytes 524320 | tf_op jit(solution)/shard_map/all_to_all | solution.py:528
  37.9 0.4 collective-permute-start.1
  38.3 0.1 pad.1.clone
  38.4 0.0 copy-done
  38.4 0.2 dynamic-slice_reduce_fusion
  38.6 2.8 %collective-permute-start = (bf16[1024,256]{1,0:T(8,128)(2,1)S(1)}, bf16[1024,256]{1,0:T(8,128)(2,1)S(1)}, u32[]{:S(2)}, u32[]{:S(2)}) collective-permute-start(bf16[1024,256]{1,0:T(8,128)(2,1)S(1)} %bitcast.19), channel_id=1, source_target_pairs={{0,3},{1,0},{2,1},{3,2},{4,7},{5,4},{6,5},{7,6},{8,11},{9,8},{10,9... | collective-permute-start | bytes 1572872 | tf_op jit(solution)/shard_map/ppermute | solution.py:525
  41.4 0.0 collective-permute-start.2
  41.4 0.1 compare_reduce_fusion
  41.5 0.0 collective-permute-done.1.other_ref.other_hbm
  41.5 5.2 %near_pairs.1 = (f32[2,8,128]{2,1,0:T(8,128)S(1)}, f32[8,2048]{1,0:T(8,128)S(1)}) custom-call(s32[11]{0:T(128)S(1)} %stack.47.s_ref, f32[16]{0:T(128)S(1)} %broadcast_select_fusion.keep_ref, bf16[1024,256]{1,0:T(8,128)(2,1)S(1)} %bitcast.21, bf16[1024,256]{1,0:T(8,128)(2,1)S(1)} %collective-permute-done.1.other_ref.other_hbm, ...), custom_call_target="tpu_custom_call" | custom-call | flops 2000000000 | bytes 10000000 | tf_op jit(solution)/shard_map/near_pairs/pallas_call | solution.py:412
  46.6 5.9 %collective-permute-done.right_ref = bf16[1024,256]{1,0:T(8,128)(2,1)S(1)} collective-permute-done((bf16[1024,256]{1,0:T(8,128)(2,1)S(1)}, bf16[1024,256]{1,0:T(8,128)(2,1)S(1)}, u32[]{:S(2)}, u32[]{:S(2)}) %collective-permute-start) | collective-permute-done | bytes 524320 | tf_op jit(solution)/shard_map/ppermute | solution.py:525
  52.6 3.1 %collective-permute-done.2.left_hbm = bf16[1024,256]{1,0:T(8,128)(2,1)S(1)} collective-permute-done((bf16[1024,256]{1,0:T(8,128)(2,1)S(1)}, bf16[1024,256]{1,0:T(8,128)(2,1)S(1)}, u32[]{:S(2)}, u32[]{:S(2)}) %collective-permute-start.2) | collective-permute-done | bytes 524320 | tf_op jit(solution)/shard_map/ppermute | solution.py:525
  55.6 5.7 %guest_pairs.1 = (f32[2,8,128]{2,1,0:T(8,128)S(1)}, f32[2,8,128]{2,1,0:T(8,128)S(1)}) custom-call(s32[11]{0:T(128)S(1)} %stack.47.s_ref, f32[16]{0:T(128)S(1)} %broadcast_select_fusion.keep_ref, bf16[1024,256]{1,0:T(8,128)(2,1)S(1)} %collective-permute-done.1.other_ref.other_hbm, bf16[1024,256]{1,0:T(8,128)(2,1)S(1)} %collective-permute-done.2.left_hbm, ...), custom_call_target="tpu_custom_call" | custom-call | flops 3000000000 | bytes 10000000 | tf_op jit(solution)/shard_map/guest_pairs/pallas_call | solution.py:436
  61.3 1.4 %collective-permute-start.3 = (f32[2,8,128]{2,1,0:T(8,128)S(1)}, f32[2,8,128]{2,1,0:T(8,128)S(1)}, u32[]{:S(2)}, u32[]{:S(2)}) collective-permute-start(f32[2,8,128]{2,1,0:T(8,128)S(1)} %get-tuple-element.26), channel_id=1, source_target_pairs={{0,4},{1,5},{2,6},{3,7},{4,0},{5,1},{6,2},{7,3},{8,12},{9,13},{10,... | collective-permute-start | bytes 24584 | tf_op jit(solution)/shard_map/ppermute | solution.py:525
  62.7 3.7 %own_pairs.1 = f32[3,8,128]{2,1,0:T(8,128)S(1)} custom-call(s32[11]{0:T(128)S(1)} %stack.47.s_ref, f32[16]{0:T(128)S(1)} %broadcast_select_fusion.keep_ref, bf16[1024,256]{1,0:T(8,128)(2,1)S(1)} %bitcast.22, bf16[1024,256]{1,0:T(8,128)(2,1)S(1)} %collective-permute-done.right_ref, f32[2,64,128]{2,1,0:T(8,128)S(1)} %get-tuple-element.21.row_ref, ...), custom_call_target="tpu_custom_call" | custom-call | flops 2000000000 | bytes 10000000 | tf_op jit(solution)/shard_map/own_pairs/pallas_call | solution.py:452
  66.4 0.0 collective-permute-done.3
  66.4 0.1 maximum_add_fusion
  66.5 2.4 %collective-permute-start.4 = (f32[3,8,128]{2,1,0:T(8,128)S(1)}, f32[3,8,128]{2,1,0:T(8,128)S(1)}, u32[]{:S(2)}, u32[]{:S(2)}) collective-permute-start(f32[3,8,128]{2,1,0:T(8,128)S(1)} %maximum_add_fusion), channel_id=1, source_target_pairs={{0,32},{1,33},{2,34},{3,35},{4,220},{5,221},{6,222},{7,223},{8,40}... | collective-permute-start | bytes 36872 | tf_op jit(solution)/shard_map/ppermute | solution.py:525
  68.9 4.4 %collective-permute-done.4.refs_0_ = f32[3,8,128]{2,1,0:T(8,128)S(1)} collective-permute-done((f32[3,8,128]{2,1,0:T(8,128)S(1)}, f32[3,8,128]{2,1,0:T(8,128)S(1)}, u32[]{:S(2)}, u32[]{:S(2)}) %collective-permute-start.4) | collective-permute-done | bytes 12320 | tf_op jit(solution)/shard_map/ppermute | solution.py:525
  73.3 0.0 collective-permute-start.5
  73.3 1.2 %collective-permute-start.6 = (f32[3,8,128]{2,1,0:T(8,128)S(1)}, f32[3,8,128]{2,1,0:T(8,128)S(1)}, u32[]{:S(2)}, u32[]{:S(2)}) collective-permute-start(f32[3,8,128]{2,1,0:T(8,128)S(1)} %collective-permute-done.4.refs_0_), channel_id=1, source_target_pairs={{0,2},{1,3},{2,0},{3,1},{4,6},{5,7},{6,4},{7,5},{8,10},{9,11},{10,... | collective-permute-start | bytes 36872 | tf_op jit(solution)/shard_map/ppermute | solution.py:525
  74.4 1.5 %collective-permute-start.7 = (f32[3,8,128]{2,1,0:T(8,128)S(1)}, f32[3,8,128]{2,1,0:T(8,128)S(1)}, u32[]{:S(2)}, u32[]{:S(2)}) collective-permute-start(f32[3,8,128]{2,1,0:T(8,128)S(1)} %collective-permute-done.4.refs_0_), channel_id=1, source_target_pairs={{0,3},{1,0},{2,1},{3,2},{4,7},{5,4},{6,5},{7,6},{8,11},{9,8},{10,9... | collective-permute-start | bytes 36872 | tf_op jit(solution)/shard_map/ppermute | solution.py:525
  75.9 1.1 %collective-permute-done.5.refs_1_ = f32[3,8,128]{2,1,0:T(8,128)S(1)} collective-permute-done((f32[3,8,128]{2,1,0:T(8,128)S(1)}, f32[3,8,128]{2,1,0:T(8,128)S(1)}, u32[]{:S(2)}, u32[]{:S(2)}) %collective-permute-start.5) | collective-permute-done | bytes 12320 | tf_op jit(solution)/shard_map/ppermute | solution.py:525
  77.0 0.3 collective-permute-done.6.refs_2_
  77.3 0.4 collective-permute-done.7.refs_3_
  77.7 1.0 %to_rank_order.1 = f32[32,128]{1,0:T(8,128)} custom-call(s32[32,128]{1,0:T(8,128)S(1)} %get-tuple-element.19.place_ref, f32[3,8,128]{2,1,0:T(8,128)S(1)} %collective-permute-done.4.refs_0_, f32[3,8,128]{2,1,0:T(8,128)S(1)} %collective-permute-done.5.refs_1_, f32[3,8,128]{2,1,0:T(8,128)S(1)} %collective-permute-done.6.refs_2_, ...), custom_call_target="tpu_custom_call" | custom-call | tf_op jit(solution)/shard_map/to_rank_order/pallas_call | solution.py:480
  (6 shorter events, 0.0 us)
Async XLA Ops:
  0.0 38.4 %copy-start = (s32[32,10]{0,1:T(8,128)S(1)}, s32[32,10]{0,1:T(8,128)}, u32[]{:S(2)}) copy-start(s32[32,10]{0,1:T(8,128)} %param.7) | copy-start | bytes 3844
  0.0 20.3 %copy-start.1 = (s32[262144]{0:T(1024)S(1)}, s32[262144]{0:T(1024)}, u32[]{:S(2)}) copy-start(s32[262144]{0:T(1024)} %param.5) | copy-start | bytes 3145732
  0.0 20.3 %copy-start.2 = (s32[262144]{0:T(1024)S(1)}, s32[262144]{0:T(1024)}, u32[]{:S(2)}) copy-start(s32[262144]{0:T(1024)} %param.6) | copy-start | bytes 3145732
  7.2 30.7 %all-to-all-start = ((bf16[64,16,256]{2,1,0:T(8,128)(2,1)}), bf16[64,16,256]{2,1,0:T(8,128)(2,1)S(1)}, u32[]{:S(2)}, u32[]{:S(2)}) async-start(bf16[64,16,256]{2,1,0:T(8,128)(2,1)} %bitcast.24), calls=%async_computation | async-start | bytes 1048576 | tf_op jit(solution)/shard_map/all_to_all | solution.py:528
  37.9 3.6 %collective-permute-start.1 = (bf16[1024,256]{1,0:T(8,128)(2,1)S(1)}, bf16[1024,256]{1,0:T(8,128)(2,1)S(1)}, u32[]{:S(2)}, u32[]{:S(2)}) collective-permute-start(bf16[1024,256]{1,0:T(8,128)(2,1)S(1)} %bitcast.18), channel_id=1, source_target_pairs={{0,4},{1,5},{2,6},{3,7},{4,0},{5,1},{6,2},{7,3},{8,12},{9,13},{10,... | collective-permute-start | bytes 1572872 | tf_op jit(solution)/shard_map/ppermute | solution.py:525
  38.6 14.0 %collective-permute-start = (bf16[1024,256]{1,0:T(8,128)(2,1)S(1)}, bf16[1024,256]{1,0:T(8,128)(2,1)S(1)}, u32[]{:S(2)}, u32[]{:S(2)}) collective-permute-start(bf16[1024,256]{1,0:T(8,128)(2,1)S(1)} %bitcast.19), channel_id=1, source_target_pairs={{0,3},{1,0},{2,1},{3,2},{4,7},{5,4},{6,5},{7,6},{8,11},{9,8},{10,9... | collective-permute-start | bytes 1572872 | tf_op jit(solution)/shard_map/ppermute | solution.py:525
  41.4 14.3 %collective-permute-start.2 = (bf16[1024,256]{1,0:T(8,128)(2,1)S(1)}, bf16[1024,256]{1,0:T(8,128)(2,1)S(1)}, u32[]{:S(2)}, u32[]{:S(2)}) collective-permute-start(bf16[1024,256]{1,0:T(8,128)(2,1)S(1)} %bitcast.20), channel_id=1, source_target_pairs={{0,1},{1,6},{2,7},{3,0},{4,5},{5,2},{6,3},{7,4},{8,9},{9,14},{10,1... | collective-permute-start | bytes 1572872 | tf_op jit(solution)/shard_map/ppermute | solution.py:525
  61.3 5.0 %collective-permute-start.3 = (f32[2,8,128]{2,1,0:T(8,128)S(1)}, f32[2,8,128]{2,1,0:T(8,128)S(1)}, u32[]{:S(2)}, u32[]{:S(2)}) collective-permute-start(f32[2,8,128]{2,1,0:T(8,128)S(1)} %get-tuple-element.26), channel_id=1, source_target_pairs={{0,4},{1,5},{2,6},{3,7},{4,0},{5,1},{6,2},{7,3},{8,12},{9,13},{10,... | collective-permute-start | bytes 24584 | tf_op jit(solution)/shard_map/ppermute | solution.py:525
  66.5 6.8 %collective-permute-start.4 = (f32[3,8,128]{2,1,0:T(8,128)S(1)}, f32[3,8,128]{2,1,0:T(8,128)S(1)}, u32[]{:S(2)}, u32[]{:S(2)}) collective-permute-start(f32[3,8,128]{2,1,0:T(8,128)S(1)} %maximum_add_fusion), channel_id=1, source_target_pairs={{0,32},{1,33},{2,34},{3,35},{4,220},{5,221},{6,222},{7,223},{8,40}... | collective-permute-start | bytes 36872 | tf_op jit(solution)/shard_map/ppermute | solution.py:525
  73.3 3.8 %collective-permute-start.5 = (f32[3,8,128]{2,1,0:T(8,128)S(1)}, f32[3,8,128]{2,1,0:T(8,128)S(1)}, u32[]{:S(2)}, u32[]{:S(2)}) collective-permute-start(f32[3,8,128]{2,1,0:T(8,128)S(1)} %collective-permute-done.4.refs_0_), channel_id=1, source_target_pairs={{0,1},{1,2},{2,3},{3,0},{4,5},{5,6},{6,7},{7,4},{8,9},{9,10},{10,1... | collective-permute-start | bytes 36872 | tf_op jit(solution)/shard_map/ppermute | solution.py:525
  73.3 4.1 %collective-permute-start.6 = (f32[3,8,128]{2,1,0:T(8,128)S(1)}, f32[3,8,128]{2,1,0:T(8,128)S(1)}, u32[]{:S(2)}, u32[]{:S(2)}) collective-permute-start(f32[3,8,128]{2,1,0:T(8,128)S(1)} %collective-permute-done.4.refs_0_), channel_id=1, source_target_pairs={{0,2},{1,3},{2,0},{3,1},{4,6},{5,7},{6,4},{7,5},{8,10},{9,11},{10,... | collective-permute-start | bytes 36872 | tf_op jit(solution)/shard_map/ppermute | solution.py:525
  74.4 3.3 %collective-permute-start.7 = (f32[3,8,128]{2,1,0:T(8,128)S(1)}, f32[3,8,128]{2,1,0:T(8,128)S(1)}, u32[]{:S(2)}, u32[]{:S(2)}) collective-permute-start(f32[3,8,128]{2,1,0:T(8,128)S(1)} %collective-permute-done.4.refs_0_), channel_id=1, source_target_pairs={{0,3},{1,0},{2,1},{3,2},{4,7},{5,4},{6,5},{7,6},{8,11},{9,8},{10,9... | collective-permute-start | bytes 36872 | tf_op jit(solution)/shard_map/ppermute | solution.py:525

commit v8 on v6

--- a/solution.py
+++ b/solution.py
@@ -121,9 +121,12 @@
         for copy in copies[x]:
             copy.start()
     rep = s_ref[2]
+    core = s_ref[6]
+    row_sums = []
+    col_sums = []
     prefix = prefix_matrix()
     shard_iota = lax.broadcasted_iota(jnp.int32, (64, LANES), 0)
-    u_iota = lax.broadcasted_iota(jnp.int32, (32, LANES), 0)
+    u_iota = lax.broadcasted_iota(jnp.int32, (64, LANES), 0)
     v_iota = lax.broadcasted_iota(jnp.int32, (LANES, LANES), 0)
     for x in range(3):
         for copy in copies[x]:
@@ -141,27 +144,39 @@
             slot = slot.astype(jnp.int32) - 1
             carry = carry + counts[:, LANES:]
             quarter = slot >> 4
-            v = (shard & 7) * 16 + (slot & 15)
+            chip = shard >> 1
+            parity = (shard & 1) ^ core
+            side = core if x == 2 else x
+            v = (chip & 3) * 32 + side * 16 + (slot & 15)
             if x == 2:
-                place_ref[j : j + 1, :] = (((rep - quarter) & 3) * 8 + (shard >> 3)) * 128 + v
+                u = (parity * 4 + ((rep - quarter) & 3)) * 8 + (chip >> 2)
+                place_ref[j : j + 1, :] = u * 128 + v
             else:
-                u = ((quarter - rep) & 3) * 8 + (shard >> 3)
+                u = parity * 32 + ((quarter - rep) & 3) * 8 + (chip >> 2)
                 u_hot = u == u_iota
                 t = thr[j : j + 1, :]
                 lanes = slice(j * LANES, (j + 1) * LANES)
-                u_ref[0:32, lanes] = jnp.where(u_hot, (t >> 4).astype(jnp.float32), 0.0).astype(jnp.bfloat16)
-                u_ref[32:64, lanes] = jnp.where(u_hot, (t & 15).astype(jnp.float32), 0.0).astype(jnp.bfloat16)
-                u_ref[64:96, lanes] = jnp.where(u_hot, float(j >= 16), 0.0).astype(jnp.bfloat16)
+                u_ref[0:64, lanes] = jnp.where(u_hot, (t >> 4).astype(jnp.float32), 0.0).astype(jnp.bfloat16)
+                u_ref[64:128, lanes] = jnp.where(u_hot, (t & 15).astype(jnp.float32), 0.0).astype(jnp.bfloat16)
+                u_ref[128:192, lanes] = jnp.where(u_hot, float(j >= 16), 0.0).astype(jnp.bfloat16)
                 v_ref[:, lanes] = jnp.where(v == v_iota, 1.0, 0.0).astype(jnp.bfloat16)
         if x < 2:
             us = u_ref[...]
             vs = v_ref[...]
-            rows = lax.dot_general(us, vs, NT, preferred_element_type=jnp.float32)
-            cols = lax.dot_general(vs, us, NT, preferred_element_type=jnp.float32)
-            row_ref[x, 0:32, :] = 1024.0 / (rows[0:32] * 16.0 + rows[32:64])
-            row_ref[x, 32:64, :] = rows[64:96]
-            col_ref[x, :, 0:32] = 1024.0 / (cols[:, 0:32] * 16.0 + cols[:, 32:64])
-            col_ref[x, :, 32:64] = cols[:, 64:96]
+            row_sums.append(lax.dot_general(us, vs, NT, preferred_element_type=jnp.float32))
+            col_sums.append(lax.dot_general(vs, us, NT, preferred_element_type=jnp.float32))
+        if x == 1:
+            rows = row_sums[0] + row_sums[1]
+            cols = col_sums[0] + col_sums[1]
+            row_rho = 1024.0 / (rows[0:64] * 16.0 + rows[64:128])
+            col_rho = 1024.0 / (cols[:, 0:64] * 16.0 + cols[:, 64:128])
+            for p in range(2):
+                at = slice(p * 32, p * 32 + 32)
+                up = slice(128 + p * 32, 160 + p * 32)
+                row_ref[p, 0:32, :] = row_rho[at]
+                row_ref[p, 32:64, :] = rows[up]
+                col_ref[p, :, 0:32] = col_rho[:, at]
+                col_ref[p, :, 32:64] = cols[:, up]
 
 
 def place(scalars, rank2d, thr2d):
@@ -175,7 +190,7 @@
         in_specs=[smem(), hbm(), hbm()],
         out_specs=(vmem(),) * 3,
         scratch_shapes=[
-            pltpu.VMEM((96, 4096), jnp.bfloat16),
+            pltpu.VMEM((192, 4096), jnp.bfloat16),
             pltpu.VMEM((LANES, 4096), jnp.bfloat16),
             pltpu.VMEM((3, 32, LANES), jnp.int32),
             pltpu.VMEM((3, 32, LANES), jnp.int32),
@@ -220,15 +235,20 @@
         meta[2, rows, :] = jnp.broadcast_to(col_ref[band, :, 32 + i : 33 + i], (LANES, LANES))
 
 
-def load_row_meta(at, row_ref, band, quarter, keep_ref, row_offset, col_offset, meta, keep):
+def load_row_meta(at, row_ref, parity, quarter, keep_ref, offsets, meta, keep):
+    second = ((lax.broadcasted_iota(jnp.int32, (8, LANES), 1) >> 4) & 1) == 1
     for u in range(8):
         lanes = slice(at + u * LANES, at + (u + 1) * LANES)
         i = quarter * 8 + u
-        meta[1, :, lanes] = jnp.broadcast_to(row_ref[band, i : i + 1, :], (8, LANES))
-        upper = jnp.broadcast_to(row_ref[band, 32 + i : 33 + i, :], (8, LANES)) > 0.5
-        for t in range(2):
-            code = (row_offset + t) * 4 + col_offset
-            keep[t, :, lanes] = jnp.where(upper, keep_ref[code + 1], keep_ref[code])
+        meta[1, :, lanes] = jnp.broadcast_to(row_ref[parity, i : i + 1, :], (8, LANES))
+        upper = jnp.broadcast_to(row_ref[parity, 32 + i : 33 + i, :], (8, LANES)) > 0.5
+        for t in range(4):
+            code = (offsets[t // 2] + t % 2) * 4
+            one, two = (
+                jnp.where(upper, keep_ref[code + offset + 1], keep_ref[code + offset])
+                for offset in offsets
+            )
+            keep[t, :, lanes] = jnp.where(second, two, one)
 
 
 def product(left_ref, left_at, right_ref, right_at, prod_ref):
@@ -252,7 +272,10 @@
         for ch in range(chunks):
             inv_j = right_meta[0, :, lanes[ch]][None]
             rho_j = right_meta[1, :, lanes[ch]][None]
-            kept = jnp.where(upper, keep[1, :, lanes[ch]][None], keep[0, :, lanes[ch]][None])
+            k = [keep[t, :, lanes[ch]][None] for t in range(4)]
+            kept = jnp.concatenate(
+                [jnp.where(upper[:2], k[1], k[0]), jnp.where(upper[2:], k[3], k[2])], axis=0
+            )
             p = prod_ref[i * 32 : i * 32 + 32, ch * LANES : (ch + 1) * LANES].reshape(4, 8, LANES)
             near = (p * inv_i) * inv_j - 1.0
             w = jnp.maximum(near * jnp.maximum(rho_i, rho_j) + kept, 0.0)
@@ -289,16 +312,15 @@
 def near_kernel(s_ref, keep_ref, own_ref, other_ref, row_ref, col_ref, out_ref, inverse_ref,
                 left_meta, right_meta, keep, prod_a, prod_b, row_sum, col_sum):
     core = s_ref[6]
-    own_offset = s_ref[7]
-    other_offset = s_ref[8]
+    offsets = (s_ref[7], s_ref[8])
     terms = square_sums(own_ref[...])
     left_meta[0] = inverse_column(terms)
     right_meta[0, :, 0:1024] = inverse_row(terms)
     right_meta[0, :, 1024:2048] = inverse_row(square_sums(other_ref[...]))
     inverse_ref[...] = right_meta[0]
     load_column_meta(col_ref, 0, 0, left_meta)
-    load_row_meta(0, row_ref, 0, 0, keep_ref, own_offset, own_offset, right_meta, keep)
-    load_row_meta(1024, row_ref, 1, 0, keep_ref, own_offset, other_offset, right_meta, keep)
+    load_row_meta(0, row_ref, 0, 0, keep_ref, offsets, right_meta, keep)
+    load_row_meta(1024, row_ref, 1, 0, keep_ref, offsets, right_meta, keep)
     row_sum[...] = jnp.zeros_like(row_sum)
     col_sum[...] = jnp.zeros_like(col_sum)
 
@@ -320,13 +342,11 @@
         out_ref[1, u : u + 1, :] = other[u]
 
 
-def far_kernel(s_ref, keep_ref, own_hbm, other_hbm, left_hbm, right_ref, row_ref, col_ref, near_ref,
-               inverse_ref, stay_ref, move_ref, block_ref, left_meta, right_meta, keep, prod_a,
+def far_kernel(s_ref, keep_ref, own_hbm, other_hbm, right_ref, left_hbm, row_ref, col_ref, near_ref,
+               inverse_ref, out_ref, block_ref, left_meta, right_meta, keep, prod_a,
                prod_b, row_sum, col_sum, sems):
-    own_offset = s_ref[7]
-    other_offset = s_ref[8]
+    offsets = (s_ref[7], s_ref[8])
     cross = s_ref[9]
-    left_offset = s_ref[10]
     copies = [
         pltpu.make_async_copy(source, block_ref.at[pl.ds(i * 1024, 1024), :], sems.at[i])
         for i, source in enumerate((own_hbm, other_hbm, left_hbm))
@@ -335,9 +355,9 @@
         copy.start()
     left_meta[0] = inverse_column(square_sums(right_ref[...]))
     load_column_meta(col_ref, 0, 1, left_meta)
-    load_row_meta(0, row_ref, 0, 0, keep_ref, own_offset, own_offset, right_meta, keep)
-    load_row_meta(1024, row_ref, 1, 0, keep_ref, own_offset, other_offset, right_meta, keep)
-    load_row_meta(2048, row_ref, cross, 3, keep_ref, own_offset, left_offset, right_meta, keep)
+    load_row_meta(0, row_ref, 0, 0, keep_ref, offsets, right_meta, keep)
+    load_row_meta(1024, row_ref, 1, 0, keep_ref, offsets, right_meta, keep)
+    load_row_meta(2048, row_ref, cross, 3, keep_ref, offsets, right_meta, keep)
     right_meta[0, :, 0:2048] = inverse_ref[...]
     row_sum[...] = jnp.zeros_like(row_sum)
     col_sum[...] = jnp.zeros_like(col_sum)
@@ -368,11 +388,10 @@
     left = cols_to_lanes(col_sum, 2048)
     for u in range(8):
         row = slice(u, u + 1)
-        stay_ref[0, row, :] = own[u] + near_ref[0, row, :]
-        stay_ref[1, row, :] = right[u]
-        stay_ref[2, row, :] = jnp.where(cross == 0, left[u], 0.0)
-        move_ref[0, row, :] = other[u] + near_ref[1, row, :]
-        move_ref[1, row, :] = jnp.where(cross == 0, 0.0, left[u])
+        out_ref[0, row, :] = own[u] + near_ref[0, row, :]
+        out_ref[1, row, :] = other[u] + near_ref[1, row, :]
+        out_ref[2, row, :] = right[u]
+        out_ref[3, row, :] = left[u]
 
 
 FAR_TILE = (1024, 256)
@@ -382,7 +401,7 @@
     return [
         pltpu.VMEM((3, 1024, LANES), jnp.float32),
         pltpu.VMEM((2, 8, columns), jnp.float32),
-        pltpu.VMEM((2, 8, columns), jnp.float32),
+        pltpu.VMEM((4, 8, columns), jnp.float32),
         pltpu.VMEM(tile, jnp.float32),
         pltpu.VMEM(tile, jnp.float32),
         pltpu.VMEM((1024, LANES), jnp.float32),
@@ -406,22 +425,19 @@
     )(scalars, keep, own, other, rows, cols)
 
 
-def far_pairs(scalars, keep, own, other, left, right, rows, cols, near):
+def far_pairs(scalars, keep, own, other, right, left, rows, cols, near):
     return pl.pallas_call(
         far_kernel,
-        out_shape=(
-            jax.ShapeDtypeStruct((3, 8, LANES), jnp.float32),
-            jax.ShapeDtypeStruct((2, 8, LANES), jnp.float32),
-        ),
-        in_specs=[smem(), smem(), hbm(), hbm(), hbm()] + [vmem()] * 5,
-        out_specs=(vmem(), vmem()),
+        out_shape=jax.ShapeDtypeStruct((4, 8, LANES), jnp.float32),
+        in_specs=[smem(), smem(), hbm(), hbm(), vmem(), hbm()] + [vmem()] * 4,
+        out_specs=vmem(),
         scratch_shapes=[pltpu.VMEM((3072, 256), jnp.bfloat16)]
         + pair_scratch(3072, FAR_TILE)
         + [pltpu.SemaphoreType.DMA((3,))],
         compiler_params=pltpu.CompilerParams(vmem_limit_bytes=VMEM),
         cost_estimate=pl.CostEstimate(flops=4 * 10**9, bytes_accessed=10**7, transcendentals=0),
         name="far_pairs",
-    )(scalars, keep, own, other, left, right, rows, cols, *near)
+    )(scalars, keep, own, other, right, left, rows, cols, *near)
 
 
 def rank_kernel(place_ref, *refs):
@@ -430,12 +446,13 @@
     lane = place_at & 127
     which = place_at >> 7
     total = jnp.zeros((32, LANES), jnp.float32)
-    for s in range(4):
-        block = pieces[s][0] + pieces[(s + 1) % 4][1] + pieces[(s + 3) % 4][2]
+    for i in range(8):
+        p, s = i // 4, i % 4
+        block = pieces[s][p] + pieces[(s + 1) % 4][2 + p] + pieces[(s + 3) % 4][4 + p]
         for u in range(8):
             row = jnp.broadcast_to(block[u : u + 1, :], (32, LANES))
             value = jnp.take_along_axis(row, lane, axis=1)
-            total = jnp.where(which == s * 8 + u, value, total)
+            total = jnp.where(which == i * 8 + u, value, total)
     out_ref[...] = total * (1.0 / TILE)
 
 
@@ -459,13 +476,13 @@
     host = device ^ 8
     own_band = jnp.where(core == 0, host, bands - host)
     other_band = bands - 1 - own_band
-    own_offset = jnp.where(own_band < bands // 2, 0, 2)
-    other_offset = 2 - own_offset
+    first_band = jnp.where(core == 0, own_band, other_band)
+    second_band = bands - 1 - first_band
+    first_offset = jnp.where(first_band < bands // 2, 0, 2)
     cross = (rep >= 2).astype(jnp.int32)
-    left_offset = jnp.where(cross == 1, other_offset, own_offset)
     scalars = jnp.stack([
-        device, rep * 16, rep, own_band, other_band, device, core,
-        own_offset, other_offset, cross, left_offset,
+        device, rep * 16, rep, first_band, second_band, device, core,
+        first_offset, 2 - first_offset, cross,
     ]).astype(jnp.int32)
     codes = lax.dynamic_index_in_dim(kept_tiles, jnp.minimum(own_band, other_band), 0, keepdims=False)
     ids = jnp.arange(16, dtype=jnp.int32)
@@ -489,7 +506,8 @@
 
     payload = send_rows(rank2d, points)
     own = lax.all_to_all(
-        payload.reshape(bands, 16, 256), "band", split_axis=0, concat_axis=0, tiled=True
+        payload.reshape(bands // 2, 32, 256), "band", split_axis=0, concat_axis=0, tiled=True,
+        axis_index_groups=[list(range(k, bands, 2)) for k in range(2)],
     ).reshape(1024, 256)
     own, rows, cols, place_at = lax.optimization_barrier((own, *place(scalars, rank2d, thr2d)))
 
@@ -498,13 +516,17 @@
         return (d if q < 2 else d ^ 1), q
 
     other = shift(own, lambda d, r: (d ^ 1, r))
+    left = shift(own, to_right)
     right = shift(own, lambda d, r: (d, (r - 1) % reps))
-    left = shift(own, to_right)
 
     near = near_pairs(scalars, keep, own, other, rows, cols)
-    stay, move = far_pairs(scalars, keep, own, other, left, right, rows, cols, near)
-    moved = shift(move, lambda d, r: (d ^ 1, r))
-    sums = stay + jnp.stack([moved[0], jnp.zeros_like(moved[0]), moved[1]])
+    sums = far_pairs(scalars, keep, own, other, right, left, rows, cols, near)
+    theirs = shift(sums, lambda d, r: (d ^ 1, r))
+    swap = cross == 1
+    sums = jnp.stack([
+        sums[0] + theirs[1], sums[1] + theirs[0], sums[2], theirs[2],
+        jnp.where(swap, theirs[3], sums[3]), jnp.where(swap, sums[3], theirs[3]),
+    ])
     home = shift(sums, lambda d, r: (block_band(d), r))
     pieces = [home] + [
         shift(home, lambda d, r, s=s: (d, (r + s) % reps)) for s in range(1, reps)

time: 77.4 us -> 78.4 us (1.013)
  Pallas kernels: 25 us -> 27.4 us
  starting transfers between devices: 24.6 us -> 23.7 us
    all_to_all x1, waiting for transfers between devices: 13.5 us -> 10.6 us  [on_device(): lax.all_to_all(payload.reshape(bands // 2, 32, 256), 'band', split_axis=0...]
    ppermute x8, waiting for transfers between devices: 13.6 us -> 16.1 us  [shift(): return lax.ppermute(value, ('band', 'rep'), joint(move))]
    pallas_call x1, Pallas kernels: 4.12 us -> 5.58 us  [place(): pl.pallas_call(place_kernel, out_shape=(jax.ShapeDtypeStruct((2, 64, LANE...]
    all_to_all x1, starting transfers between devices: 13 us -> 11.9 us  [on_device(): lax.all_to_all(payload.reshape(bands // 2, 32, 256), 'band', split_axis=0...]
  transfers between devices with their start and end apart: 9 -> 9, of which waited for: 6 -> 6; matrix products, arithmetic and copies ran while one was open for 1% -> 0% of each run, Pallas kernels for 12% -> 14%
where the time goes in v8:
time: 78.4 us; the launch traced here: 78.2 us
  Pallas kernels  27.4 us (35%)
  waiting for transfers between devices  26.6 us (34%)
  starting transfers between devices  23.7 us (30%)
    ppermute x8, waiting for transfers between devices, shift(): return lax.ppermute(value, ('band', 'rep'), joint(move))  16.1 us
    all_to_all x1, starting transfers between devices, on_device(): lax.all_to_all(payload.reshape(bands // 2, 32, 256), 'band', split_axis=0...  11.9 us
    ppermute x8, starting transfers between devices, shift(): return lax.ppermute(value, ('band', 'rep'), joint(move))  11.8 us
    all_to_all x1, waiting for transfers between devices, on_device(): lax.all_to_all(payload.reshape(bands // 2, 32, 256), 'band', split_axis=0...  10.6 us
    pallas_call x1, Pallas kernels, far_pairs(): pl.pallas_call(far_kernel, out_shape=jax.ShapeDtypeStruct((4, 8, LANES),...  7.99 us
    pallas_call x1, Pallas kernels, send_rows(): pl.pallas_call(send_kernel, out_shape=jax.ShapeDtypeStruct((1024, 256), j...  7.16 us
    pallas_call x1, Pallas kernels, place(): pl.pallas_call(place_kernel, out_shape=(jax.ShapeDtypeStruct((2, 64, LANE...  5.58 us
    pallas_call x1, Pallas kernels, near_pairs(): pl.pallas_call(near_kernel, out_shape=(jax.ShapeDtypeStruct((2, 8, LANES)...  5.27 us
  transfers between devices with their start and end apart: 9, of which 6 were waited for; matrix products, arithmetic and copies ran while one was open for 0% of the time, Pallas kernels for 14%

profile of v8, /device:TPU:1, one launch (start us, length us, event | category | flops | bytes accessed | tf_op | source)
XLA Modules:
  0.0 78.2 jit_solution(4334278607643575232)
XLA Ops:
  0.0 0.0 copy-start
  0.0 0.0 copy-start.1
  0.0 0.0 copy-start.2
  0.0 7.2 %send_rows.1 = bf16[1024,256]{1,0:T(8,128)(2,1)} custom-call(s32[2048,128]{1,0:T(8,128)} %bitcast.14, bf16[4096,256]{1,0:T(8,128)(2,1)} %points_hbm.1), custom_call_target="tpu_custom_call" | custom-call | tf_op jit(solution)/shard_map/send_rows/pallas_call | solution.py:94
  7.2 11.9 %all-to-all-start = ((bf16[32,32,256]{2,1,0:T(8,128)(2,1)}), bf16[32,32,256]{2,1,0:T(8,128)(2,1)S(1)}, u32[]{:S(2)}, u32[]{:S(2)}) async-start(bf16[32,32,256]{2,1,0:T(8,128)(2,1)} %bitcast.22), calls=%async_computation | async-start | bytes 1048576 | tf_op jit(solution)/shard_map/all_to_all | solution.py:508
  19.1 0.1 stack.47.s_ref
  19.2 0.0 copy-done.1
  19.2 0.0 copy-done.2
  19.2 5.6 %place.1 = (f32[2,64,128]{2,1,0:T(8,128)S(1)}, f32[2,128,64]{2,1,0:T(8,128)S(1)}, s32[32,128]{1,0:T(8,128)S(1)}) custom-call(s32[10]{0:T(128)S(1)} %stack.47.s_ref, s32[2048,128]{1,0:T(8,128)S(1)} %bitcast.15, s32[2048,128]{1,0:T(8,128)S(1)} %bitcast.21), custom_call_target="tpu_custom_call" | custom-call | flops 2000000000 | bytes 10000000 | tf_op jit(solution)/shard_map/place/pallas_call | solution.py:183
  24.8 10.6 %all-to-all-done = bf16[32,32,256]{2,1,0:T(8,128)(2,1)S(1)} async-done(((bf16[32,32,256]{2,1,0:T(8,128)(2,1)}), bf16[32,32,256]{2,1,0:T(8,128)(2,1)S(1)}, u32[]{:S(2)}, u32[]{:S(2)}) %all-to-all-start) | async-done | bytes 524320 | tf_op jit(solution)/shard_map/all_to_all | solution.py:508
  35.3 2.4 %collective-permute-start = (bf16[1024,256]{1,0:T(8,128)(2,1)S(1)}, bf16[1024,256]{1,0:T(8,128)(2,1)S(1)}, u32[]{:S(2)}, u32[]{:S(2)}) collective-permute-start(bf16[1024,256]{1,0:T(8,128)(2,1)S(1)} %bitcast.16), channel_id=1, source_target_pairs={{0,4},{1,5},{2,6},{3,7},{4,0},{5,1},{6,2},{7,3},{8,12},{9,13},{10,... | collective-permute-start | bytes 1572872 | tf_op jit(solution)/shard_map/ppermute | solution.py:505
  37.7 0.0 copy-done
  37.7 0.2 dynamic-slice_reduce_fusion
  37.9 1.4 %collective-permute-start.2 = (bf16[1024,256]{1,0:T(8,128)(2,1)S(1)}, bf16[1024,256]{1,0:T(8,128)(2,1)S(1)}, u32[]{:S(2)}, u32[]{:S(2)}) collective-permute-start(bf16[1024,256]{1,0:T(8,128)(2,1)S(1)} %bitcast.17), channel_id=1, source_target_pairs={{0,1},{1,6},{2,7},{3,0},{4,5},{5,2},{6,3},{7,4},{8,9},{9,14},{10,1... | collective-permute-start | bytes 1572872 | tf_op jit(solution)/shard_map/ppermute | solution.py:505
  39.3 1.7 %collective-permute-start.1 = (bf16[1024,256]{1,0:T(8,128)(2,1)S(1)}, bf16[1024,256]{1,0:T(8,128)(2,1)S(1)}, u32[]{:S(2)}, u32[]{:S(2)}) collective-permute-start(bf16[1024,256]{1,0:T(8,128)(2,1)S(1)} %bitcast.18), channel_id=1, source_target_pairs={{0,3},{1,0},{2,1},{3,2},{4,7},{5,4},{6,5},{7,6},{8,11},{9,8},{10,9... | collective-permute-start | bytes 1572872 | tf_op jit(solution)/shard_map/ppermute | solution.py:505
  41.0 0.1 compare_reduce_fusion
  41.1 0.0 collective-permute-done.other_ref.other_hbm
  41.1 5.3 %near_pairs.1 = (f32[2,8,128]{2,1,0:T(8,128)S(1)}, f32[8,2048]{1,0:T(8,128)S(1)}) custom-call(s32[10]{0:T(128)S(1)} %stack.47.s_ref, f32[16]{0:T(128)S(1)} %broadcast_select_fusion.keep_ref, bf16[1024,256]{1,0:T(8,128)(2,1)S(1)} %bitcast.19, bf16[1024,256]{1,0:T(8,128)(2,1)S(1)} %collective-permute-done.other_ref.other_hbm, ...), custom_call_target="tpu_custom_call" | custom-call | flops 2000000000 | bytes 10000000 | tf_op jit(solution)/shard_map/near_pairs/pallas_call | solution.py:413
  46.4 6.5 %collective-permute-done.2.left_hbm = bf16[1024,256]{1,0:T(8,128)(2,1)S(1)} collective-permute-done((bf16[1024,256]{1,0:T(8,128)(2,1)S(1)}, bf16[1024,256]{1,0:T(8,128)(2,1)S(1)}, u32[]{:S(2)}, u32[]{:S(2)}) %collective-permute-start.2) | collective-permute-done | bytes 524320 | tf_op jit(solution)/shard_map/ppermute | solution.py:505
  52.9 0.0 collective-permute-done.1.right_ref
  52.9 8.0 %far_pairs.1 = f32[4,8,128]{2,1,0:T(8,128)S(1)} custom-call(s32[10]{0:T(128)S(1)} %stack.47.s_ref, f32[16]{0:T(128)S(1)} %broadcast_select_fusion.keep_ref, bf16[1024,256]{1,0:T(8,128)(2,1)S(1)} %bitcast.20, bf16[1024,256]{1,0:T(8,128)(2,1)S(1)} %collective-permute-done.other_ref.other_hbm, bf16[1024,256]{1,0:T(8,128)(2,1)S(1)} %collective-permute-done.1.right_ref, ...), custom_call_target="tpu_custom_call" | custom-call | flops 4000000000 | bytes 10000000 | tf_op jit(solution)/shard_map/far_pairs/pallas_call | solution.py:429
  60.9 0.8 %collective-permute-start.3 = (f32[4,8,128]{2,1,0:T(8,128)S(1)}, f32[4,8,128]{2,1,0:T(8,128)S(1)}, u32[]{:S(2)}, u32[]{:S(2)}) collective-permute-start(f32[4,8,128]{2,1,0:T(8,128)S(1)} %far_pairs.1), channel_id=1, source_target_pairs={{0,4},{1,5},{2,6},{3,7},{4,0},{5,1},{6,2},{7,3},{8,12},{9,13},{10,... | collective-permute-start | bytes 49160 | tf_op jit(solution)/shard_map/ppermute | solution.py:505
  61.7 0.8 %collective-permute-done.3 = f32[4,8,128]{2,1,0:T(8,128)S(1)} collective-permute-done((f32[4,8,128]{2,1,0:T(8,128)S(1)}, f32[4,8,128]{2,1,0:T(8,128)S(1)}, u32[]{:S(2)}, u32[]{:S(2)}) %collective-permute-start.3) | collective-permute-done | bytes 16416 | tf_op jit(solution)/shard_map/ppermute | solution.py:505
  62.6 2.0 %collective-permute-start.4 = (f32[6,8,128]{2,1,0:T(8,128)S(1)}, f32[6,8,128]{2,1,0:T(8,128)S(1)}, u32[]{:S(2)}, u32[]{:S(2)}) collective-permute-start(f32[6,8,128]{2,1,0:T(8,128)S(1)} %constant_dynamic-update-slice_fusion), channel_id=1, source_target_pairs={{0,32},{1,33},{2,34},{3,35},{4,220},{5,221},{6,222},{7,223},{8,40}... | collective-permute-start | bytes 73736 | tf_op jit(solution)/shard_map/ppermute | solution.py:505
  64.6 5.1 %collective-permute-done.4.refs_0_ = f32[6,8,128]{2,1,0:T(8,128)S(1)} collective-permute-done((f32[6,8,128]{2,1,0:T(8,128)S(1)}, f32[6,8,128]{2,1,0:T(8,128)S(1)}, u32[]{:S(2)}, u32[]{:S(2)}) %collective-permute-start.4) | collective-permute-done | bytes 24608 | tf_op jit(solution)/shard_map/ppermute | solution.py:505
  69.7 2.9 %collective-permute-start.7 = (f32[6,8,128]{2,1,0:T(8,128)S(1)}, f32[6,8,128]{2,1,0:T(8,128)S(1)}, u32[]{:S(2)}, u32[]{:S(2)}) collective-permute-start(f32[6,8,128]{2,1,0:T(8,128)S(1)} %collective-permute-done.4.refs_0_), channel_id=1, source_target_pairs={{0,3},{1,0},{2,1},{3,2},{4,7},{5,4},{6,5},{7,6},{8,11},{9,8},{10,9... | collective-permute-start | bytes 73736 | tf_op jit(solution)/shard_map/ppermute | solution.py:505
  72.6 0.1 collective-permute-start.6
  72.7 0.5 collective-permute-start.5
  73.2 0.4 collective-permute-done.7.refs_3_
  73.5 3.3 %collective-permute-done.6.refs_2_ = f32[6,8,128]{2,1,0:T(8,128)S(1)} collective-permute-done((f32[6,8,128]{2,1,0:T(8,128)S(1)}, f32[6,8,128]{2,1,0:T(8,128)S(1)}, u32[]{:S(2)}, u32[]{:S(2)}) %collective-permute-start.6) | collective-permute-done | bytes 24608 | tf_op jit(solution)/shard_map/ppermute | solution.py:505
  76.8 0.0 collective-permute-done.5.refs_1_
  76.8 1.4 %to_rank_order.1 = f32[32,128]{1,0:T(8,128)} custom-call(s32[32,128]{1,0:T(8,128)S(1)} %get-tuple-element.17.place_ref, f32[6,8,128]{2,1,0:T(8,128)S(1)} %collective-permute-done.4.refs_0_, f32[6,8,128]{2,1,0:T(8,128)S(1)} %collective-permute-done.5.refs_1_, f32[6,8,128]{2,1,0:T(8,128)S(1)} %collective-permute-done.6.refs_2_, ...), custom_call_target="tpu_custom_call" | custom-call | tf_op jit(solution)/shard_map/to_rank_order/pallas_call | solution.py:460
  (8 shorter events, 0.0 us)
Async XLA Ops:
  0.0 37.7 %copy-start = (s32[32,10]{0,1:T(8,128)S(1)}, s32[32,10]{0,1:T(8,128)}, u32[]{:S(2)}) copy-start(s32[32,10]{0,1:T(8,128)} %param.7) | copy-start | bytes 3844
  0.0 19.2 %copy-start.1 = (s32[262144]{0:T(1024)S(1)}, s32[262144]{0:T(1024)}, u32[]{:S(2)}) copy-start(s32[262144]{0:T(1024)} %param.5) | copy-start | bytes 3145732
  0.0 19.2 %copy-start.2 = (s32[262144]{0:T(1024)S(1)}, s32[262144]{0:T(1024)}, u32[]{:S(2)}) copy-start(s32[262144]{0:T(1024)} %param.6) | copy-start | bytes 3145732
  7.2 28.2 %all-to-all-start = ((bf16[32,32,256]{2,1,0:T(8,128)(2,1)}), bf16[32,32,256]{2,1,0:T(8,128)(2,1)S(1)}, u32[]{:S(2)}, u32[]{:S(2)}) async-start(bf16[32,32,256]{2,1,0:T(8,128)(2,1)} %bitcast.22), calls=%async_computation | async-start | bytes 1048576 | tf_op jit(solution)/shard_map/all_to_all | solution.py:508
  35.3 5.8 %collective-permute-start = (bf16[1024,256]{1,0:T(8,128)(2,1)S(1)}, bf16[1024,256]{1,0:T(8,128)(2,1)S(1)}, u32[]{:S(2)}, u32[]{:S(2)}) collective-permute-start(bf16[1024,256]{1,0:T(8,128)(2,1)S(1)} %bitcast.16), channel_id=1, source_target_pairs={{0,4},{1,5},{2,6},{3,7},{4,0},{5,1},{6,2},{7,3},{8,12},{9,13},{10,... | collective-permute-start | bytes 1572872 | tf_op jit(solution)/shard_map/ppermute | solution.py:505
  37.9 15.0 %collective-permute-start.2 = (bf16[1024,256]{1,0:T(8,128)(2,1)S(1)}, bf16[1024,256]{1,0:T(8,128)(2,1)S(1)}, u32[]{:S(2)}, u32[]{:S(2)}) collective-permute-start(bf16[1024,256]{1,0:T(8,128)(2,1)S(1)} %bitcast.17), channel_id=1, source_target_pairs={{0,1},{1,6},{2,7},{3,0},{4,5},{5,2},{6,3},{7,4},{8,9},{9,14},{10,1... | collective-permute-start | bytes 1572872 | tf_op jit(solution)/shard_map/ppermute | solution.py:505
  39.3 13.6 %collective-permute-start.1 = (bf16[1024,256]{1,0:T(8,128)(2,1)S(1)}, bf16[1024,256]{1,0:T(8,128)(2,1)S(1)}, u32[]{:S(2)}, u32[]{:S(2)}) collective-permute-start(bf16[1024,256]{1,0:T(8,128)(2,1)S(1)} %bitcast.18), channel_id=1, source_target_pairs={{0,3},{1,0},{2,1},{3,2},{4,7},{5,4},{6,5},{7,6},{8,11},{9,8},{10,9... | collective-permute-start | bytes 1572872 | tf_op jit(solution)/shard_map/ppermute | solution.py:505
  60.9 1.7 %collective-permute-start.3 = (f32[4,8,128]{2,1,0:T(8,128)S(1)}, f32[4,8,128]{2,1,0:T(8,128)S(1)}, u32[]{:S(2)}, u32[]{:S(2)}) collective-permute-start(f32[4,8,128]{2,1,0:T(8,128)S(1)} %far_pairs.1), channel_id=1, source_target_pairs={{0,4},{1,5},{2,6},{3,7},{4,0},{5,1},{6,2},{7,3},{8,12},{9,13},{10,... | collective-permute-start | bytes 49160 | tf_op jit(solution)/shard_map/ppermute | solution.py:505
  62.6 7.1 %collective-permute-start.4 = (f32[6,8,128]{2,1,0:T(8,128)S(1)}, f32[6,8,128]{2,1,0:T(8,128)S(1)}, u32[]{:S(2)}, u32[]{:S(2)}) collective-permute-start(f32[6,8,128]{2,1,0:T(8,128)S(1)} %constant_dynamic-update-slice_fusion), channel_id=1, source_target_pairs={{0,32},{1,33},{2,34},{3,35},{4,220},{5,221},{6,222},{7,223},{8,40}... | collective-permute-start | bytes 73736 | tf_op jit(solution)/shard_map/ppermute | solution.py:505
  69.7 3.9 %collective-permute-start.7 = (f32[6,8,128]{2,1,0:T(8,128)S(1)}, f32[6,8,128]{2,1,0:T(8,128)S(1)}, u32[]{:S(2)}, u32[]{:S(2)}) collective-permute-start(f32[6,8,128]{2,1,0:T(8,128)S(1)} %collective-permute-done.4.refs_0_), channel_id=1, source_target_pairs={{0,3},{1,0},{2,1},{3,2},{4,7},{5,4},{6,5},{7,6},{8,11},{9,8},{10,9... | collective-permute-start | bytes 73736 | tf_op jit(solution)/shard_map/ppermute | solution.py:505
  72.6 4.2 %collective-permute-start.6 = (f32[6,8,128]{2,1,0:T(8,128)S(1)}, f32[6,8,128]{2,1,0:T(8,128)S(1)}, u32[]{:S(2)}, u32[]{:S(2)}) collective-permute-start(f32[6,8,128]{2,1,0:T(8,128)S(1)} %collective-permute-done.4.refs_0_), channel_id=1, source_target_pairs={{0,2},{1,3},{2,0},{3,1},{4,6},{5,7},{6,4},{7,5},{8,10},{9,11},{10,... | collective-permute-start | bytes 73736 | tf_op jit(solution)/shard_map/ppermute | solution.py:505
  72.7 4.2 %collective-permute-start.5 = (f32[6,8,128]{2,1,0:T(8,128)S(1)}, f32[6,8,128]{2,1,0:T(8,128)S(1)}, u32[]{:S(2)}, u32[]{:S(2)}) collective-permute-start(f32[6,8,128]{2,1,0:T(8,128)S(1)} %collective-permute-done.4.refs_0_), channel_id=1, source_target_pairs={{0,1},{1,2},{2,3},{3,0},{4,5},{5,6},{6,7},{7,4},{8,9},{9,10},{10,1... | collective-permute-start | bytes 73736 | tf_op jit(solution)/shard_map/ppermute | solution.py:505

commit v9 on v6

--- a/solution.py
+++ b/solution.py
@@ -506,10 +506,8 @@
     moved = shift(move, lambda d, r: (d ^ 1, r))
     sums = stay + jnp.stack([moved[0], jnp.zeros_like(moved[0]), moved[1]])
     home = shift(sums, lambda d, r: (block_band(d), r))
-    pieces = [home] + [
-        shift(home, lambda d, r, s=s: (d, (r + s) % reps)) for s in range(1, reps)
-    ]
-    return to_rank_order(place_at, pieces).reshape(points.shape[0])
+    moved = {s: shift(home, lambda d, r, s=s: (d, (r + s) % reps)) for s in (2, 1, 3)}
+    return to_rank_order(place_at, [home, moved[1], moved[2], moved[3]]).reshape(points.shape[0])
 
 
 def solution(mesh):

time: 77.4 us -> 77.4 us (level)
  no operation moved by 1% of the time
where the time goes in v9:
time: 77.4 us; the launch traced here: 77.2 us
  waiting for transfers between devices  27 us (35%)
  Pallas kernels  25 us (32%)
  starting transfers between devices  24.6 us (32%)
    ppermute x8, waiting for transfers between devices, shift(): return lax.ppermute(value, ('band', 'rep'), joint(move))  13.6 us
    all_to_all x1, waiting for transfers between devices, on_device(): lax.all_to_all(payload.reshape(bands, 16, 256), 'band', split_axis=0, con...  13.5 us
    all_to_all x1, starting transfers between devices, on_device(): lax.all_to_all(payload.reshape(bands, 16, 256), 'band', split_axis=0, con...  13 us
    ppermute x8, starting transfers between devices, shift(): return lax.ppermute(value, ('band', 'rep'), joint(move))  11.6 us
    pallas_call x1, Pallas kernels, far_pairs(): pl.pallas_call(far_kernel, out_shape=(jax.ShapeDtypeStruct((3, 8, LANES),...  7.54 us
    pallas_call x1, Pallas kernels, send_rows(): pl.pallas_call(send_kernel, out_shape=jax.ShapeDtypeStruct((1024, 256), j...  7.15 us
    pallas_call x1, Pallas kernels, near_pairs(): pl.pallas_call(near_kernel, out_shape=(jax.ShapeDtypeStruct((2, 8, LANES)...  5.16 us
    pallas_call x1, Pallas kernels, place(): pl.pallas_call(place_kernel, out_shape=(jax.ShapeDtypeStruct((2, 64, LANE...  4.12 us
  transfers between devices with their start and end apart: 9, of which 6 were waited for; matrix products, arithmetic and copies ran while one was open for 1% of the time, Pallas kernels for 12%

profile of v9, /device:TPU:1, one launch (start us, length us, event | category | flops | bytes accessed | tf_op | source)
XLA Modules:
  0.0 77.2 jit_solution(18218819906162759167)
XLA Ops:
  0.0 0.0 copy-start
  0.0 7.2 %send_rows.1 = bf16[1024,256]{1,0:T(8,128)(2,1)} custom-call(s32[2048,128]{1,0:T(8,128)} %bitcast.16, bf16[4096,256]{1,0:T(8,128)(2,1)} %points_hbm.1), custom_call_target="tpu_custom_call" | custom-call | tf_op jit(solution)/shard_map/send_rows/pallas_call | solution.py:94
  7.2 13.0 %all-to-all-start = ((bf16[64,16,256]{2,1,0:T(8,128)(2,1)}), bf16[64,16,256]{2,1,0:T(8,128)(2,1)S(1)}, u32[]{:S(2)}, u32[]{:S(2)}) async-start(bf16[64,16,256]{2,1,0:T(8,128)(2,1)} %bitcast.24), calls=%async_computation | async-start | bytes 1048576 | tf_op jit(solution)/shard_map/all_to_all | solution.py:491
  20.2 0.1 stack.47.s_ref
  20.3 0.0 copy-done.1
  20.3 0.0 copy-done.2
  20.3 4.1 %place.1 = (f32[2,64,128]{2,1,0:T(8,128)S(1)}, f32[2,128,64]{2,1,0:T(8,128)S(1)}, s32[32,128]{1,0:T(8,128)S(1)}) custom-call(s32[11]{0:T(128)S(1)} %stack.47.s_ref, s32[2048,128]{1,0:T(8,128)S(1)} %bitcast.17, s32[2048,128]{1,0:T(8,128)S(1)} %bitcast.23), custom_call_target="tpu_custom_call" | custom-call | flops 2000000000 | bytes 10000000 | tf_op jit(solution)/shard_map/place/pallas_call | solution.py:168
  24.4 13.5 %all-to-all-done = bf16[64,16,256]{2,1,0:T(8,128)(2,1)S(1)} async-done(((bf16[64,16,256]{2,1,0:T(8,128)(2,1)}), bf16[64,16,256]{2,1,0:T(8,128)(2,1)S(1)}, u32[]{:S(2)}, u32[]{:S(2)}) %all-to-all-start) | async-done | bytes 524320 | tf_op jit(solution)/shard_map/all_to_all | solution.py:491
  37.9 0.4 collective-permute-start
  38.3 0.0 copy-done
  38.3 0.2 dynamic-slice_reduce_fusion
  38.5 1.4 %collective-permute-start.1 = (bf16[1024,256]{1,0:T(8,128)(2,1)S(1)}, bf16[1024,256]{1,0:T(8,128)(2,1)S(1)}, u32[]{:S(2)}, u32[]{:S(2)}) collective-permute-start(bf16[1024,256]{1,0:T(8,128)(2,1)S(1)} %bitcast.19), channel_id=1, source_target_pairs={{0,1},{1,6},{2,7},{3,0},{4,5},{5,2},{6,3},{7,4},{8,9},{9,14},{10,1... | collective-permute-start | bytes 1572872 | tf_op jit(solution)/shard_map/ppermute | solution.py:488
  39.9 1.7 %collective-permute-start.2 = (bf16[1024,256]{1,0:T(8,128)(2,1)S(1)}, bf16[1024,256]{1,0:T(8,128)(2,1)S(1)}, u32[]{:S(2)}, u32[]{:S(2)}) collective-permute-start(bf16[1024,256]{1,0:T(8,128)(2,1)S(1)} %bitcast.20), channel_id=1, source_target_pairs={{0,3},{1,0},{2,1},{3,2},{4,7},{5,4},{6,5},{7,6},{8,11},{9,8},{10,9... | collective-permute-start | bytes 1572872 | tf_op jit(solution)/shard_map/ppermute | solution.py:488
  41.6 0.1 compare_reduce_fusion
  41.7 0.0 collective-permute-done.other_ref.other_hbm
  41.7 5.2 %near_pairs.1 = (f32[2,8,128]{2,1,0:T(8,128)S(1)}, f32[8,2048]{1,0:T(8,128)S(1)}) custom-call(s32[11]{0:T(128)S(1)} %stack.47.s_ref, f32[16]{0:T(128)S(1)} %broadcast_select_fusion.keep_ref, bf16[1024,256]{1,0:T(8,128)(2,1)S(1)} %bitcast.21, bf16[1024,256]{1,0:T(8,128)(2,1)S(1)} %collective-permute-done.other_ref.other_hbm, ...), custom_call_target="tpu_custom_call" | custom-call | flops 2000000000 | bytes 10000000 | tf_op jit(solution)/shard_map/near_pairs/pallas_call | solution.py:394
  46.8 6.5 %collective-permute-done.1.left_hbm = bf16[1024,256]{1,0:T(8,128)(2,1)S(1)} collective-permute-done((bf16[1024,256]{1,0:T(8,128)(2,1)S(1)}, bf16[1024,256]{1,0:T(8,128)(2,1)S(1)}, u32[]{:S(2)}, u32[]{:S(2)}) %collective-permute-start.1) | collective-permute-done | bytes 524320 | tf_op jit(solution)/shard_map/ppermute | solution.py:488
  53.3 0.0 collective-permute-done.2.right_ref
  53.3 7.5 %far_pairs.1 = (f32[3,8,128]{2,1,0:T(8,128)S(1)}, f32[2,8,128]{2,1,0:T(8,128)S(1)}) custom-call(s32[11]{0:T(128)S(1)} %stack.47.s_ref, f32[16]{0:T(128)S(1)} %broadcast_select_fusion.keep_ref, bf16[1024,256]{1,0:T(8,128)(2,1)S(1)} %bitcast.22, bf16[1024,256]{1,0:T(8,128)(2,1)S(1)} %collective-permute-done.other_ref.other_hbm, ...), custom_call_target="tpu_custom_call" | custom-call | flops 4000000000 | bytes 10000000 | tf_op jit(solution)/shard_map/far_pairs/pallas_call | solution.py:410
  60.9 1.0 %collective-permute-start.3 = (f32[2,8,128]{2,1,0:T(8,128)S(1)}, f32[2,8,128]{2,1,0:T(8,128)S(1)}, u32[]{:S(2)}, u32[]{:S(2)}) collective-permute-start(f32[2,8,128]{2,1,0:T(8,128)S(1)} %get-tuple-element.26), channel_id=1, source_target_pairs={{0,4},{1,5},{2,6},{3,7},{4,0},{5,1},{6,2},{7,3},{8,12},{9,13},{10,... | collective-permute-start | bytes 24584 | tf_op jit(solution)/shard_map/ppermute | solution.py:488
  61.8 0.1 pad.1.clone
  61.9 0.8 collective-permute-done.3
  62.7 0.1 maximum_add_fusion
  62.7 2.4 %collective-permute-start.4 = (f32[3,8,128]{2,1,0:T(8,128)S(1)}, f32[3,8,128]{2,1,0:T(8,128)S(1)}, u32[]{:S(2)}, u32[]{:S(2)}) collective-permute-start(f32[3,8,128]{2,1,0:T(8,128)S(1)} %maximum_add_fusion), channel_id=1, source_target_pairs={{0,32},{1,33},{2,34},{3,35},{4,220},{5,221},{6,222},{7,223},{8,40}... | collective-permute-start | bytes 36872 | tf_op jit(solution)/shard_map/ppermute | solution.py:488
  65.1 4.4 %collective-permute-done.4.refs_0_ = f32[3,8,128]{2,1,0:T(8,128)S(1)} collective-permute-done((f32[3,8,128]{2,1,0:T(8,128)S(1)}, f32[3,8,128]{2,1,0:T(8,128)S(1)}, u32[]{:S(2)}, u32[]{:S(2)}) %collective-permute-start.4) | collective-permute-done | bytes 12320 | tf_op jit(solution)/shard_map/ppermute | solution.py:488
  69.5 1.3 %collective-permute-start.5 = (f32[3,8,128]{2,1,0:T(8,128)S(1)}, f32[3,8,128]{2,1,0:T(8,128)S(1)}, u32[]{:S(2)}, u32[]{:S(2)}) collective-permute-start(f32[3,8,128]{2,1,0:T(8,128)S(1)} %collective-permute-done.4.refs_0_), channel_id=1, source_target_pairs={{0,1},{1,2},{2,3},{3,0},{4,5},{5,6},{6,7},{7,4},{8,9},{9,10},{10,1... | collective-permute-start | bytes 36872 | tf_op jit(solution)/shard_map/ppermute | solution.py:488
  70.9 2.8 %collective-permute-start.6 = (f32[3,8,128]{2,1,0:T(8,128)S(1)}, f32[3,8,128]{2,1,0:T(8,128)S(1)}, u32[]{:S(2)}, u32[]{:S(2)}) collective-permute-start(f32[3,8,128]{2,1,0:T(8,128)S(1)} %collective-permute-done.4.refs_0_), channel_id=1, source_target_pairs={{0,2},{1,3},{2,0},{3,1},{4,6},{5,7},{6,4},{7,5},{8,10},{9,11},{10,... | collective-permute-start | bytes 36872 | tf_op jit(solution)/shard_map/ppermute | solution.py:488
  73.6 0.6 collective-permute-start.7
  74.3 0.0 collective-permute-done.5.refs_1_
  74.3 0.7 collective-permute-done.6.refs_2_
  74.9 1.3 %collective-permute-done.7.refs_3_ = f32[3,8,128]{2,1,0:T(8,128)S(1)} collective-permute-done((f32[3,8,128]{2,1,0:T(8,128)S(1)}, f32[3,8,128]{2,1,0:T(8,128)S(1)}, u32[]{:S(2)}, u32[]{:S(2)}) %collective-permute-start.7) | collective-permute-done | bytes 12320 | tf_op jit(solution)/shard_map/ppermute | solution.py:488
  76.2 1.0 %to_rank_order.1 = f32[32,128]{1,0:T(8,128)} custom-call(s32[32,128]{1,0:T(8,128)S(1)} %get-tuple-element.19.place_ref, f32[3,8,128]{2,1,0:T(8,128)S(1)} %collective-permute-done.4.refs_0_, f32[3,8,128]{2,1,0:T(8,128)S(1)} %collective-permute-done.5.refs_1_, f32[3,8,128]{2,1,0:T(8,128)S(1)} %collective-permute-done.6.refs_2_, ...), custom_call_target="tpu_custom_call" | custom-call | tf_op jit(solution)/shard_map/to_rank_order/pallas_call | solution.py:443
  (5 shorter events, 0.0 us)
Async XLA Ops:
  0.0 38.3 %copy-start = (s32[32,10]{0,1:T(8,128)S(1)}, s32[32,10]{0,1:T(8,128)}, u32[]{:S(2)}) copy-start(s32[32,10]{0,1:T(8,128)} %param.7) | copy-start | bytes 3844
  0.0 20.3 %copy-start.1 = (s32[262144]{0:T(1024)S(1)}, s32[262144]{0:T(1024)}, u32[]{:S(2)}) copy-start(s32[262144]{0:T(1024)} %param.5) | copy-start | bytes 3145732
  0.0 20.3 %copy-start.2 = (s32[262144]{0:T(1024)S(1)}, s32[262144]{0:T(1024)}, u32[]{:S(2)}) copy-start(s32[262144]{0:T(1024)} %param.6) | copy-start | bytes 3145732
  7.2 30.7 %all-to-all-start = ((bf16[64,16,256]{2,1,0:T(8,128)(2,1)}), bf16[64,16,256]{2,1,0:T(8,128)(2,1)S(1)}, u32[]{:S(2)}, u32[]{:S(2)}) async-start(bf16[64,16,256]{2,1,0:T(8,128)(2,1)} %bitcast.24), calls=%async_computation | async-start | bytes 1048576 | tf_op jit(solution)/shard_map/all_to_all | solution.py:491
  37.9 3.8 %collective-permute-start = (bf16[1024,256]{1,0:T(8,128)(2,1)S(1)}, bf16[1024,256]{1,0:T(8,128)(2,1)S(1)}, u32[]{:S(2)}, u32[]{:S(2)}) collective-permute-start(bf16[1024,256]{1,0:T(8,128)(2,1)S(1)} %bitcast.18), channel_id=1, source_target_pairs={{0,4},{1,5},{2,6},{3,7},{4,0},{5,1},{6,2},{7,3},{8,12},{9,13},{10,... | collective-permute-start | bytes 1572872 | tf_op jit(solution)/shard_map/ppermute | solution.py:488
  38.5 14.8 %collective-permute-start.1 = (bf16[1024,256]{1,0:T(8,128)(2,1)S(1)}, bf16[1024,256]{1,0:T(8,128)(2,1)S(1)}, u32[]{:S(2)}, u32[]{:S(2)}) collective-permute-start(bf16[1024,256]{1,0:T(8,128)(2,1)S(1)} %bitcast.19), channel_id=1, source_target_pairs={{0,1},{1,6},{2,7},{3,0},{4,5},{5,2},{6,3},{7,4},{8,9},{9,14},{10,1... | collective-permute-start | bytes 1572872 | tf_op jit(solution)/shard_map/ppermute | solution.py:488
  39.9 13.4 %collective-permute-start.2 = (bf16[1024,256]{1,0:T(8,128)(2,1)S(1)}, bf16[1024,256]{1,0:T(8,128)(2,1)S(1)}, u32[]{:S(2)}, u32[]{:S(2)}) collective-permute-start(bf16[1024,256]{1,0:T(8,128)(2,1)S(1)} %bitcast.20), channel_id=1, source_target_pairs={{0,3},{1,0},{2,1},{3,2},{4,7},{5,4},{6,5},{7,6},{8,11},{9,8},{10,9... | collective-permute-start | bytes 1572872 | tf_op jit(solution)/shard_map/ppermute | solution.py:488
  60.9 1.8 %collective-permute-start.3 = (f32[2,8,128]{2,1,0:T(8,128)S(1)}, f32[2,8,128]{2,1,0:T(8,128)S(1)}, u32[]{:S(2)}, u32[]{:S(2)}) collective-permute-start(f32[2,8,128]{2,1,0:T(8,128)S(1)} %get-tuple-element.26), channel_id=1, source_target_pairs={{0,4},{1,5},{2,6},{3,7},{4,0},{5,1},{6,2},{7,3},{8,12},{9,13},{10,... | collective-permute-start | bytes 24584 | tf_op jit(solution)/shard_map/ppermute | solution.py:488
  62.7 6.8 %collective-permute-start.4 = (f32[3,8,128]{2,1,0:T(8,128)S(1)}, f32[3,8,128]{2,1,0:T(8,128)S(1)}, u32[]{:S(2)}, u32[]{:S(2)}) collective-permute-start(f32[3,8,128]{2,1,0:T(8,128)S(1)} %maximum_add_fusion), channel_id=1, source_target_pairs={{0,32},{1,33},{2,34},{3,35},{4,220},{5,221},{6,222},{7,223},{8,40}... | collective-permute-start | bytes 36872 | tf_op jit(solution)/shard_map/ppermute | solution.py:488
  69.5 4.7 %collective-permute-start.5 = (f32[3,8,128]{2,1,0:T(8,128)S(1)}, f32[3,8,128]{2,1,0:T(8,128)S(1)}, u32[]{:S(2)}, u32[]{:S(2)}) collective-permute-start(f32[3,8,128]{2,1,0:T(8,128)S(1)} %collective-permute-done.4.refs_0_), channel_id=1, source_target_pairs={{0,1},{1,2},{2,3},{3,0},{4,5},{5,6},{6,7},{7,4},{8,9},{9,10},{10,1... | collective-permute-start | bytes 36872 | tf_op jit(solution)/shard_map/ppermute | solution.py:488
  70.9 4.0 %collective-permute-start.6 = (f32[3,8,128]{2,1,0:T(8,128)S(1)}, f32[3,8,128]{2,1,0:T(8,128)S(1)}, u32[]{:S(2)}, u32[]{:S(2)}) collective-permute-start(f32[3,8,128]{2,1,0:T(8,128)S(1)} %collective-permute-done.4.refs_0_), channel_id=1, source_target_pairs={{0,2},{1,3},{2,0},{3,1},{4,6},{5,7},{6,4},{7,5},{8,10},{9,11},{10,... | collective-permute-start | bytes 36872 | tf_op jit(solution)/shard_map/ppermute | solution.py:488
  73.6 2.5 %collective-permute-start.7 = (f32[3,8,128]{2,1,0:T(8,128)S(1)}, f32[3,8,128]{2,1,0:T(8,128)S(1)}, u32[]{:S(2)}, u32[]{:S(2)}) collective-permute-start(f32[3,8,128]{2,1,0:T(8,128)S(1)} %collective-permute-done.4.refs_0_), channel_id=1, source_target_pairs={{0,3},{1,0},{2,1},{3,2},{4,7},{5,4},{6,5},{7,6},{8,11},{9,8},{10,9... | collective-permute-start | bytes 36872 | tf_op jit(solution)/shard_map/ppermute | solution.py:488
